TPU v7x, 128 devices: a whole 4x4x4 slice. The times are simulated.
128 devices in a mesh: row: 8 (over y_lo, z), col: 16 (over y_hi, x, core).
Axes of the slice: x: 4, y: 4 (y_hi: 2, y_lo: 2; y = y_hi * 2 + y_lo), z: 4, core: 2. Of those that a mesh axis runs over, the one named last changes fastest.
Arguments:
- eigvecs: float32 [65536, 4096], P(('row', 'col')), may hold values from -6 to 6
- panels: float32 [3, 256, 65536], P(None, None, ('row', 'col')), may hold values from -0.09375 to 0.09375
- tri_factors: float32 [3, 256, 256], replicated, may hold values from -0.2 to 0.6, as said below
Outputs:
- back: float32 [65536, 4096], P('row', 'col')
Inputs may be any that keep to these rules, and one draw needn't show every extreme that they name: `tri_factors`: each factor is upper triangular; diagonal entries lie in 0.2 to 0.6.
All inputs are finite; a program needn't handle non-finite values.
Results may differ from a plain program's by a relative error of at most 0.00013.
Values sent between devices are 32-bit elements; how exact they have to be, the bound alone decides.
No kernel may reach another device: no remote copies, remote signals or barrier semaphores. Data moves between devices by JAX's collectives and lax.ppermute only.
A program may use at most 128 MiB of HBM per device.

v0:
```python
import jax
import jax.numpy as jnp
from jax import lax
from jax.sharding import PartitionSpec as P


def product(left, right):
    return jnp.dot(left, right, precision=lax.Precision.HIGHEST, preferred_element_type=jnp.float32)


def spread(panel_t, right):
    return lax.dot_general(
        panel_t,
        right,
        (((0,), (0,)), ((), ())),
        precision=lax.Precision.HIGHEST,
        preferred_element_type=jnp.float32,
    )


def shaped(raw, start, offset):
    count = raw.shape[0]
    width = raw.shape[1]
    place = start + lax.broadcasted_iota(jnp.int32, (count, width), 1)
    limit = offset + lax.broadcasted_iota(jnp.int32, (count, width), 0)
    return jnp.where(
        place < limit, jnp.float32(0.0), jnp.where(place == limit, jnp.float32(1.0), raw)
    )


def apply_chain(block, vectors, tri_factors, total_single):
    for index in reversed(range(len(vectors))):
        w_block = total_single(product(vectors[index], block))
        block = block - spread(vectors[index], product(tri_factors[index], w_block))
    return block


def tile_single(values):
    return lax.psum(values, "row")


def on_device(eigvecs, panels, tri_factors):
    block_size = tri_factors.shape[1]
    count = tri_factors.shape[0]
    tiles = lax.all_to_all(eigvecs, "col", split_axis=1, concat_axis=0, tiled=True)
    gathered = lax.all_gather(panels, "col", axis=2, tiled=True)
    start = lax.axis_index("row") * tiles.shape[0]
    vectors = [shaped(gathered[index], start, (index + 1) * block_size) for index in range(count)]
    return apply_chain(tiles, vectors, tri_factors, tile_single)


def solution(mesh):
    in_specs = (P(("row", "col"), None), P(None, None, ("row", "col")), P())
    out_specs = P("row", "col")
    return jax.shard_map(
        on_device, mesh=mesh, in_specs=in_specs, out_specs=out_specs, check_vma=False
    )
```

profile of v0, /device:TPU:2, one launch (start us, length us, event | category | flops | bytes accessed | tf_op | source)
XLA Modules:
  0.0 585.2 jit_solution(4360634410430133219)
XLA Ops:
  6.5 0.0 all-gather.2.cloned.1.call-start
  6.5 0.7 all-gather.2.cloned.1.call-update
  7.3 7.7 %copy.7 = f32[64,16,8,256]{3,2,0,1:T(8,128)} copy(f32[64,16,8,256]{3,2,1,0:T(8,128)} %bitcast.50) | data formatting | bytes 16777216 | tf_op jit(solution)/shard_map/all_to_all | solution.py:45
  14.9 7.5 %all-to-all-start = ((f32[512,16,256]{2,0,1:T(8,128)}), f32[512,16,256]{2,0,1:T(8,128)}, u32[]{:S(2)}, u32[]{:S(2)}) async-start(f32[512,16,256]{2,0,1:T(8,128)} %bitcast.49), calls=%async_computation | async-start | bytes 16777216 | tf_op jit(solution)/shard_map/all_to_all | solution.py:45
  22.4 0.0 all-reduce.4.cloned.1.call-start
  22.5 127.6 %all-to-all-done = f32[512,16,256]{2,0,1:T(8,128)} async-done(((f32[512,16,256]{2,0,1:T(8,128)}), f32[512,16,256]{2,0,1:T(8,128)}, u32[]{:S(2)}, u32[]{:S(2)}) %all-to-all-start) | async-done | bytes 8388640 | tf_op jit(solution)/shard_map/all_to_all | solution.py:45
  150.1 102.2 %all-gather.2.cloned.1.call-done = f32[3,256,8192]{2,1,0:T(8,128)} async-done(((f32[3,256,512]{2,1,0:T(8,128)}), f32[3,256,8192]{2,1,0:T(8,128)}) %all-gather.2.cloned.1.call-update) | async-done | bytes 25165840 | tf_op jit(solution)/shard_map/all_gather | solution.py:46
  252.3 0.0 copy-start.2
  252.3 14.9 %fusion.4 = f32[256,256]{1,0:T(8,128)} fusion(f32[8192,256]{1,0:T(8,128)} %bitcast.1, f32[3,256,8192]{2,1,0:T(8,128)} %all-gather.2.cloned.1.call-done, s32[8192]{0:T(1024)S(1)} %iota_add_fusion, s32[256]{0:T(256)S(1)} %iota_add_fusion.3), kind=kOutput, calls=%fused_computation.10 | convolution fusion | flops 6450839552 | bytes 17073152 | tf_op jit(solution)/shard_map/dot_general | solution.py:8
  267.2 0.0 all-reduce.4.cloned.1.call-update
  267.3 0.0 all-reduce.6.cloned.1.call-start
  267.3 73.4 %all-reduce.4.cloned.1.call-done = f32[256,256]{1,0:T(8,128)} async-done(((f32[256,256]{1,0:T(8,128)}), f32[256,256]{1,0:T(8,128)}) %all-reduce.4.cloned.1.call-update) | async-done | bytes 262160 | tf_op jit(solution)/shard_map/psum | solution.py:39
  340.7 0.0 copy-done.2
  340.7 1.5 fusion.50
  342.3 17.4 %convolution_subtract_fusion.2 = f32[8192,256]{1,0:T(8,128)S(1)} fusion(f32[8192,256]{1,0:T(8,128)} %bitcast.1, f32[256,256]{1,0:T(8,128)S(1)} %fusion.50, f32[3,256,8192]{2,1,0:T(8,128)} %all-gather.2.cloned.1.call-done, s32[8192]{0:T(1024)S(1)} %iota_add_fusion, s32[256]{0:T(256)S(1)} %iota_add_fusion.3), kind=kOutput, calls=%fused_computation.2 | convolution fusion | flops 6452936704 | bytes 25461760 | tf_op jit(solution)/shard_map/dot_general | solution.py:12
  359.6 0.0 copy-start
  359.7 3.4 copy-done
  363.0 12.3 %fusion.17 = f32[256,256]{1,0:T(8,128)} fusion(f32[8192,256]{1,0:T(8,128)S(1)} %convolution_subtract_fusion.2, f32[3,256,8192]{2,1,0:T(8,128)} %all-gather.2.cloned.1.call-done, s32[8192]{0:T(1024)S(1)} %iota_add_fusion, s32[256]{0:T(256)S(1)} %iota_add_fusion.2), kind=kOutput, calls=%fused_computation.22 | convolution fusion | flops 6450839552 | bytes 17073152 | tf_op jit(solution)/shard_map/dot_general | solution.py:8
  375.4 0.0 all-reduce.6.cloned.1.call-update
  375.4 0.3 all-reduce.8.cloned.1.call-start
  375.7 73.4 %all-reduce.6.cloned.1.call-done = f32[256,256]{1,0:T(8,128)} async-done(((f32[256,256]{1,0:T(8,128)}), f32[256,256]{1,0:T(8,128)}) %all-reduce.6.cloned.1.call-update) | async-done | bytes 262160 | tf_op jit(solution)/shard_map/psum | solution.py:39
  449.1 1.5 fusion.48
  450.6 17.2 %convolution_subtract_fusion.1 = f32[8192,256]{1,0:T(8,128)S(1)} fusion(f32[8192,256]{1,0:T(8,128)} %copy-done, f32[256,256]{1,0:T(8,128)S(1)} %fusion.48, f32[3,256,8192]{2,1,0:T(8,128)} %all-gather.2.cloned.1.call-done, s32[8192]{0:T(1024)S(1)} %iota_add_fusion, s32[256]{0:T(256)S(1)} %iota_add_fusion.2), kind=kOutput, calls=%fused_computation.1 | convolution fusion | flops 6452936704 | bytes 25461760 | tf_op jit(solution)/shard_map/dot_general | solution.py:12
  467.8 0.0 copy-start.1
  467.8 3.4 copy-done.1
  471.2 12.5 %fusion.20 = f32[256,256]{1,0:T(8,128)} fusion(f32[8192,256]{1,0:T(8,128)S(1)} %convolution_subtract_fusion.1, f32[3,256,8192]{2,1,0:T(8,128)} %all-gather.2.cloned.1.call-done, s32[8192]{0:T(1024)S(1)} %iota_add_fusion, s32[256]{0:T(256)S(1)} %iota_add_fusion.1), kind=kOutput, calls=%fused_computation.23 | convolution fusion | flops 6450839552 | bytes 17073152 | tf_op jit(solution)/shard_map/dot_general | solution.py:8
  483.8 0.0 all-reduce.8.cloned.1.call-update
  483.8 73.7 %all-reduce.8.cloned.1.call-done = f32[256,256]{1,0:T(8,128)} async-done(((f32[256,256]{1,0:T(8,128)}), f32[256,256]{1,0:T(8,128)}) %all-reduce.8.cloned.1.call-update) | async-done | bytes 262160 | tf_op jit(solution)/shard_map/psum | solution.py:39
  557.5 1.5 fusion.46
  559.0 19.2 %convolution_subtract_fusion = f32[8192,256]{1,0:T(8,128)} fusion(f32[8192,256]{1,0:T(8,128)} %copy-done.1, f32[256,256]{1,0:T(8,128)S(1)} %fusion.46, f32[3,256,8192]{2,1,0:T(8,128)} %all-gather.2.cloned.1.call-done, s32[8192]{0:T(1024)S(1)} %iota_add_fusion, s32[256]{0:T(256)S(1)} %iota_add_fusion.1), kind=kOutput, calls=%fused_computation | convolution fusion | flops 6452936704 | bytes 25461760 | tf_op jit(solution)/shard_map/dot_general | solution.py:12
  (4 shorter events, 0.0 us)
Async XLA Ops:
  6.5 245.8 %all-gather.2.cloned.1.call-start = ((), (), s32[]{:S(2)}) async-start(), calls=%async_computation.1 | async-start | bytes 26738688 | tf_op jit(solution)/shard_map/all_gather | solution.py:46
  14.9 135.2 %all-to-all-start = ((f32[512,16,256]{2,0,1:T(8,128)}), f32[512,16,256]{2,0,1:T(8,128)}, u32[]{:S(2)}, u32[]{:S(2)}) async-start(f32[512,16,256]{2,0,1:T(8,128)} %bitcast.49), calls=%async_computation | async-start | bytes 16777216 | tf_op jit(solution)/shard_map/all_to_all | solution.py:45
  22.4 318.3 %all-reduce.4.cloned.1.call-start = ((), (), s32[]{:S(2)}) async-start(), calls=%async_computation.2 | async-start | bytes 524288 | tf_op jit(solution)/shard_map/psum | solution.py:39
  252.3 88.4 %copy-start.2 = (f32[3,256,256]{2,1,0:T(8,128)S(1)}, f32[3,256,256]{2,1,0:T(8,128)}, u32[]{:S(2)}) copy-start(f32[3,256,256]{2,1,0:T(8,128)} %param.5) | copy-start | bytes 2359300
  267.3 181.8 %all-reduce.6.cloned.1.call-start = ((), (), s32[]{:S(2)}) async-start(), calls=%async_computation.3 | async-start | bytes 524288 | tf_op jit(solution)/shard_map/psum | solution.py:39
  359.6 3.4 copy-start
  375.4 182.1 %all-reduce.8.cloned.1.call-start = ((), (), s32[]{:S(2)}) async-start(), calls=%async_computation.4 | async-start | bytes 524288 | tf_op jit(solution)/shard_map/psum | solution.py:39
  467.8 3.4 copy-start.1
Sparse Core Ops, SparseCore 0:
  9.8 242.4 all-gather.1
  267.4 73.3 all-reduce.3
  375.5 73.5 all-reduce.5
  483.9 73.5 all-reduce.7
where the time goes:
time: 591 us; the launch traced here: 585 us
  waiting for transfers between devices  451 us (76%)
  matrix products  98.1 us (17%)
  local copies, waits for them, and re-layouts  14.5 us (2%)
  between operations  13.7 us (2%)
  starting transfers between devices  7.81 us (1%)
    psum x3, waiting for transfers between devices, tile_single(): return lax.psum(values, 'row')  221 us
    all_to_all x1, waiting for transfers between devices, on_device(): lax.all_to_all(eigvecs, 'col', split_axis=1, concat_axis=0, tiled=True)  128 us
    all_gather x1, waiting for transfers between devices, on_device(): gathered = lax.all_gather(panels, 'col', axis=2, tiled=True)  102 us
    dot_general x3, matrix products, spread(): lax.dot_general(panel_t, right, (((0,), (0,)), ((), ())), precision=lax.P...  53.7 us
    dot_general x6, matrix products, product(): jnp.dot(left, right, precision=lax.Precision.HIGHEST, preferred_element_t...  44.4 us
  transfers between devices with their start and end apart: 5, of which 5 were waited for; matrix products, arithmetic and copies ran while one was open for 1% of the time, Pallas kernels for 0%

commit v1 on v0

v1 whole, which is shorter than its diff:
```python
import jax
import jax.numpy as jnp
from jax import lax
from jax.experimental import pallas as pl
from jax.experimental.pallas import tpu as pltpu
from jax.sharding import Mesh
from jax.sharding import PartitionSpec as P

AXES = ("ylo", "z", "yhi", "x", "core")
ROW = ("ylo", "z")
COL = ("yhi", "x", "core")


def exact(left, right):
    return jnp.dot(left, right, precision=lax.Precision.HIGHEST, preferred_element_type=jnp.float32)


def halves(values):
    high = values.astype(jnp.bfloat16)
    low = (values - high.astype(jnp.float32)).astype(jnp.bfloat16)
    return high, low


def triple(left, right, dims):
    left_high, left_low = halves(left)
    right_high, right_low = halves(right)

    def dot(a, b):
        return lax.dot_general(a, b, (dims, ((), ())), preferred_element_type=jnp.float32)

    return dot(left_high, right_high) + (dot(left_high, right_low) + dot(left_low, right_high))


def project_kernel(v_ref, e_ref, w_ref):
    @pl.when(pl.program_id(0) == 0)
    def _():
        w_ref[...] = jnp.zeros_like(w_ref)

    w_ref[...] += triple(v_ref[0], e_ref[...], ((1,), (0,)))


def project(vectors, block):
    pieces, count, depth = vectors.shape
    width = block.shape[1]
    return pl.pallas_call(
        project_kernel,
        grid=(pieces,),
        in_specs=[
            pl.BlockSpec((1, count, depth), lambda k: (k, 0, 0)),
            pl.BlockSpec((depth, width), lambda k: (k, 0)),
        ],
        out_specs=pl.BlockSpec((count, width), lambda k: (0, 0)),
        out_shape=jax.ShapeDtypeStruct((count, width), jnp.float32),
        compiler_params=pltpu.CompilerParams(vmem_limit_bytes=40 * 2**20),
        cost_estimate=pl.CostEstimate(
            flops=6 * pieces * count * depth * width,
            bytes_accessed=4 * pieces * depth * (count + width),
            transcendentals=0,
        ),
    )(vectors, block)


def update_kernel(v_ref, e_ref, y_ref, o_ref):
    o_ref[...] = e_ref[...] - triple(v_ref[0], y_ref[...], ((0,), (0,)))


def update(vectors, block, y):
    pieces, count, depth = vectors.shape
    width = block.shape[1]
    return pl.pallas_call(
        update_kernel,
        grid=(pieces,),
        in_specs=[
            pl.BlockSpec((1, count, depth), lambda k: (k, 0, 0)),
            pl.BlockSpec((depth, width), lambda k: (k, 0)),
            pl.BlockSpec((count, width), lambda k: (0, 0)),
        ],
        out_specs=pl.BlockSpec((depth, width), lambda k: (k, 0)),
        out_shape=jax.ShapeDtypeStruct(block.shape, jnp.float32),
        compiler_params=pltpu.CompilerParams(vmem_limit_bytes=40 * 2**20),
        cost_estimate=pl.CostEstimate(
            flops=6 * pieces * count * depth * width,
            bytes_accessed=4 * pieces * depth * (count + 2 * width),
            transcendentals=0,
        ),
    )(vectors, block, y)


def row_sum(values):
    groups = lax.axis_size(ROW)
    parts = lax.all_to_all(values, ROW, split_axis=0, concat_axis=0, tiled=True)
    total = jnp.sum(parts.reshape(groups, -1, parts.shape[1]), axis=0)
    spread = jnp.broadcast_to(total[None], (groups,) + total.shape).reshape(parts.shape)
    return lax.all_to_all(spread, ROW, split_axis=0, concat_axis=0, tiled=True)


def ring(size, step):
    return [(i, (i + step) % size) for i in range(size)]


def x_ring(held):
    size = lax.axis_size("x")
    result = list(held)
    lefts, rights = [], []
    for piece, start, where in held:
        y, x, core = where
        lefts.append((lax.ppermute(piece, "x", ring(size, 1)), start, (y, (x + size - 1) % size, core)))
        rights.append((lax.ppermute(piece, "x", ring(size, -1)), start, (y, (x + 1) % size, core)))
    for (left, start, where), (right, _, _) in zip(lefts, rights):
        y, x, core = where
        half = left.shape[0] // 2
        far = (y, (x + size - 1) % size, core)
        result.append((lax.ppermute(left[:half], "x", ring(size, 1)), start, far))
        result.append((lax.ppermute(right[half:], "x", ring(size, -1)), start + half, far))
    return result + lefts + rights


def pair(held, axis, place):
    result = list(held)
    for piece, start, where in held:
        there = list(where)
        there[place] = 1 - there[place]
        result.append((lax.ppermute(piece, axis, ring(2, 1)), start, tuple(there)))
    return result


def gather(panels):
    count, depth = panels.shape
    cut = 2 * count // 3
    here = (lax.axis_index("yhi"), lax.axis_index("x"), lax.axis_index("core"))
    first = [(panels[cut:], cut, here)]
    second = [(panels[:cut], 0, here)]
    second = x_ring(pair(second, "yhi", 0))
    first = pair(x_ring(first), "yhi", 0)
    held = pair(first + second, "core", 2)
    sizes = (2, lax.axis_size("x"), 2)
    full = jnp.zeros((sizes[0] * sizes[1] * sizes[2], count, depth), jnp.float32)
    for piece, start, (y, x, core) in held:
        place = (y * sizes[1] + x) * sizes[2] + core
        full = lax.dynamic_update_slice(full, piece[None], (place, start, 0))
    return full


def on_device(eigvecs, panels, tri_factors):
    count, block_size, depth = panels.shape
    total = count * block_size
    row = lax.axis_index(ROW)
    col = lax.axis_index(COL)
    place = (row * lax.axis_size(COL) + col) * depth + lax.broadcasted_iota(jnp.int32, (total, depth), 1)
    limit = block_size + lax.broadcasted_iota(jnp.int32, (total, depth), 0)
    shaped = panels.reshape(total, depth)
    shaped = jnp.where(place < limit, 0.0, jnp.where(place == limit, 1.0, shaped))
    block = lax.all_to_all(eigvecs, COL, split_axis=1, concat_axis=0, tiled=True)
    vectors = gather(shaped)
    gram = lax.psum(jnp.concatenate([
        lax.dot_general(
            shaped[:block_size],
            shaped[block_size:],
            (((1,), (1,)), ((), ())),
            precision=lax.Precision.HIGHEST,
            preferred_element_type=jnp.float32,
        ),
        lax.dot_general(
            shaped[block_size : 2 * block_size],
            shaped[2 * block_size :],
            (((1,), (1,)), ((), ())),
            precision=lax.Precision.HIGHEST,
            preferred_element_type=jnp.float32,
        ),
    ], axis=1), AXES)
    g01, g02, g12 = (gram[:, i * block_size : (i + 1) * block_size] for i in range(3))
    t0, t1, t2 = (tri_factors[i] for i in range(3))
    m12 = -exact(t1, exact(g12, t2))
    m01 = -exact(t0, exact(g01, t1))
    m02 = -exact(t0, exact(g02, t2) + exact(g01, m12))
    zero = jnp.zeros_like(t0)
    mixer = jnp.concatenate([
        jnp.concatenate([t0, m01, m02], axis=1),
        jnp.concatenate([zero, t1, m12], axis=1),
        jnp.concatenate([zero, zero, t2], axis=1),
    ], axis=0)
    w = row_sum(project(vectors, block))
    return update(vectors, block, exact(mixer, w))


def solution(mesh):
    fine = Mesh(mesh.devices.reshape(2, 4, 2, 4, 2), AXES)
    in_specs = (P(AXES, None), P(None, None, AXES), P())
    out_specs = P(ROW, COL)
    return jax.shard_map(on_device, mesh=fine, in_specs=in_specs, out_specs=out_specs, check_vma=False)
```

time: 591 us -> 468 us (0.79)
  waiting for transfers between devices: 451 us -> 275 us
  matrix products: 98.1 us -> 10.8 us
  local copies, waits for them, and re-layouts: 14.5 us -> 73.5 us
  Pallas kernels: 0 us -> 44.1 us
  starting transfers between devices: 7.81 us -> 44.7 us
    all_to_all x1 -> x3, waiting for transfers between devices: 128 us -> 21.1 us  [the longest x1 10.7 us: row_sum(): parts = lax.all_to_all(values, ROW, split_axis=0, concat_axis=0, tiled=True)]
    all_gather x1 -> x0, waiting for transfers between devices: 102 us -> none  [on_device(): gathered = lax.all_gather(panels, 'col', axis=2, tiled=True)]
    dot_general x9 -> x10, matrix products: 98.1 us -> 10.8 us  [the longest x8 9.14 us: exact(): jnp.dot(left, right, precision=lax.Precision.HIGHEST, preferred_element_t...]
    ppermute x0 -> x38, waiting for transfers between devices: none -> 45.2 us  [the longest x3 17.6 us: x_ring(): lax.ppermute(piece, 'x', ring(size, -1))]
    pallas_call x0 -> x2, Pallas kernels: none -> 44.1 us  [the longest x1 23 us: update(): pl.pallas_call(update_kernel, grid=(pieces,), in_specs=[pl.BlockSpec((1,...]
    dynamic_update_slice x0 -> x40, local copies, waits for them, and re-layouts: none -> 41.6 us  [gather(): full = lax.dynamic_update_slice(full, piece[None], (place, start, 0))]
    ppermute x0 -> x38, starting transfers between devices: none -> 28.2 us  [the longest x26 15.1 us: pair(): result.append((lax.ppermute(piece, axis, ring(2, 1)), start, tuple(there)))]
    broadcast_in_dim x0 -> x3, local copies, waits for them, and re-layouts: none -> 12.6 us  [the longest x1 11.6 us: gather(): jnp.zeros((sizes[0] * sizes[1] * sizes[2], count, depth), jnp.float32)]
  transfers between devices with their start and end apart: 5 -> 42, of which waited for: 5 -> 10; matrix products, arithmetic and copies ran while one was open for 1% -> 17% of each run, Pallas kernels for 0% -> 0%
where the time goes in v1:
time: 468 us; the launch traced here: 464 us
  waiting for transfers between devices  275 us (59%)
  local copies, waits for them, and re-layouts  73.5 us (16%)
  starting transfers between devices  44.7 us (10%)
  Pallas kernels  44.1 us (9%)
  between operations  13.6 us (3%)
  matrix products  10.8 us (2%)
    psum x1, waiting for transfers between devices, on_device(): lax.psum(jnp.concatenate([lax.dot_general(shaped[:block_size], shaped[blo...  209 us
    dynamic_update_slice x40, local copies, waits for them, and re-layouts, gather(): full = lax.dynamic_update_slice(full, piece[None], (place, start, 0))  41.6 us
    pallas_call x1, Pallas kernels, update(): pl.pallas_call(update_kernel, grid=(pieces,), in_specs=[pl.BlockSpec((1,...  23 us
    pallas_call x1, Pallas kernels, project(): pl.pallas_call(project_kernel, grid=(pieces,), in_specs=[pl.BlockSpec((1,...  21.2 us
    ppermute x3, waiting for transfers between devices, x_ring(): lax.ppermute(piece, 'x', ring(size, -1))  17.6 us
    ppermute x26, starting transfers between devices, pair(): result.append((lax.ppermute(piece, axis, ring(2, 1)), start, tuple(there)))  15.1 us
    ppermute x26, waiting for transfers between devices, pair(): result.append((lax.ppermute(piece, axis, ring(2, 1)), start, tuple(there)))  14.2 us
    ppermute x3, waiting for transfers between devices, x_ring(): lax.ppermute(right[half:], 'x', ring(size, -1))  13.4 us
  transfers between devices with their start and end apart: 42, of which 10 were waited for; matrix products, arithmetic and copies ran while one was open for 17% of the time, Pallas kernels for 0%

profile of v1, /device:TPU:2, one launch (start us, length us, event | category | flops | bytes accessed | tf_op | source)
XLA Modules:
  0.0 464.5 jit_solution(5711307119382208229)
XLA Ops:
  6.5 1.7 fusion.13
  11.1 3.2 collective-permute-start.4
  17.2 7.7 %copy.15 = f32[64,16,8,256]{3,2,0,1:T(8,128)} copy(f32[64,16,8,256]{3,2,1,0:T(8,128)} %bitcast.125) | data formatting | bytes 16777216 | tf_op jit(solution)/shard_map/all_to_all | solution.py:153
  24.9 7.4 %all-to-all-start = ((f32[512,16,256]{2,0,1:T(8,128)}), f32[512,16,256]{2,0,1:T(8,128)}, u32[]{:S(2)}, u32[]{:S(2)}) async-start(f32[512,16,256]{2,0,1:T(8,128)} %bitcast.124), calls=%async_computation | async-start | bytes 16777216 | tf_op jit(solution)/shard_map/all_to_all | solution.py:153
  36.0 1.7 slice.70
  39.1 11.6 %broadcast_in_dim.139 = f32[16,768,512]{2,1,0:T(8,128)} broadcast(f32[]{:T(128)} %constant.63.clone.1), dimensions={} | broadcast | bytes 25165828 | tf_op jit(solution)/shard_map/broadcast_in_dim | solution.py:137
  51.6 1.8 copy.10
  53.4 1.8 copy.11
  55.2 1.8 copy.12
  59.2 208.6 %all-reduce.3.cloned.1.call-done = f32[256,768]{1,0:T(8,128)} async-done(((f32[256,768]{1,0:T(8,128)}), f32[256,768]{1,0:T(8,128)}) %all-reduce.3.cloned.1.call-update) | async-done | bytes 786448 | tf_op jit(solution)/shard_map/psum | solution.py:155
  267.8 2.1 fusion.23
  271.0 1.7 bitcast_dynamic-update-slice_fusion.39
  272.7 2.7 collective-permute-start.5
  277.0 1.9 bitcast_dynamic-update-slice_fusion.30
  278.9 1.9 bitcast_dynamic-update-slice_fusion.29
  281.8 2.5 collective-permute-start.6
  284.3 1.9 bitcast_dynamic-update-slice_fusion.28
  288.7 5.4 %collective-permute-done.12 = f32[512,512]{1,0:T(8,128)S(1)} collective-permute-done((f32[512,512]{1,0:T(8,128)}, f32[512,512]{1,0:T(8,128)S(1)}, u32[]{:S(2)}, u32[]{:S(2)}) %collective-permute-start.12) | collective-permute-done | bytes 1048608 | tf_op jit(solution)/shard_map/ppermute | solution.py:108
  294.2 8.8 %collective-permute-done.6 = f32[128,512]{1,0:T(8,128)S(1)} collective-permute-done((f32[128,512]{1,0:T(8,128)}, f32[128,512]{1,0:T(8,128)S(1)}, u32[]{:S(2)}, u32[]{:S(2)}) %collective-permute-start.6) | collective-permute-done | bytes 262176 | tf_op jit(solution)/shard_map/ppermute | solution.py:123
  303.7 2.0 collective-permute-start.16
  306.5 5.0 %collective-permute-done.8 = f32[256,512]{1,0:T(8,128)S(1)} collective-permute-done((f32[256,512]{1,0:T(8,128)}, f32[256,512]{1,0:T(8,128)S(1)}, u32[]{:S(2)}, u32[]{:S(2)}) %collective-permute-start.8) | collective-permute-done | bytes 524320 | tf_op jit(solution)/shard_map/ppermute | solution.py:123
  315.6 2.3 bitcast_dynamic-update-slice_fusion.10
  317.8 12.2 %collective-permute-done.16 = f32[512,512]{1,0:T(8,128)S(1)} collective-permute-done((f32[512,512]{1,0:T(8,128)}, f32[512,512]{1,0:T(8,128)S(1)}, u32[]{:S(2)}, u32[]{:S(2)}) %collective-permute-start.16) | collective-permute-done | bytes 1048608 | tf_op jit(solution)/shard_map/ppermute | solution.py:108
  332.5 7.6 %collective-permute-done.13 = f32[256,512]{1,0:T(8,128)S(1)} collective-permute-done((f32[256,512]{1,0:T(8,128)S(1)}, f32[256,512]{1,0:T(8,128)S(1)}, u32[]{:S(2)}, u32[]{:S(2)}) %collective-permute-start.13) | collective-permute-done | bytes 524320 | tf_op jit(solution)/shard_map/ppermute | solution.py:114
  342.3 5.8 %collective-permute-done.17 = f32[256,512]{1,0:T(8,128)S(1)} collective-permute-done((f32[256,512]{1,0:T(8,128)S(1)}, f32[256,512]{1,0:T(8,128)S(1)}, u32[]{:S(2)}, u32[]{:S(2)}) %collective-permute-start.17) | collective-permute-done | bytes 524320 | tf_op jit(solution)/shard_map/ppermute | solution.py:114
  375.1 21.2 %shard_map.37 = f32[768,256]{1,0:T(8,128)} custom-call(f32[16,768,512]{2,1,0:T(8,128)} %bitcast_dynamic-update-slice_fusion.v_ref, f32[8192,256]{1,0:T(8,128)} %bitcast.42.e_ref), custom_call_target="tpu_custom_call" | custom-call | flops 9663676416 | bytes 33554432 | tf_op jit(solution)/shard_map/pallas_call | solution.py:45
  396.3 5.3 %all-to-all-start.1 = ((f32[8,96,256]{2,1,0:T(8,128)}), f32[8,96,256]{2,1,0:T(8,128)S(1)}, u32[]{:S(2)}, u32[]{:S(2)}) async-start(f32[8,96,256]{2,1,0:T(8,128)} %bitcast.50), calls=%async_computation.1 | async-start | bytes 1572864 | tf_op jit(solution)/shard_map/all_to_all | solution.py:91
  403.0 10.7 %all-to-all-done.1 = f32[8,96,256]{2,1,0:T(8,128)S(1)} async-done(((f32[8,96,256]{2,1,0:T(8,128)}), f32[8,96,256]{2,1,0:T(8,128)S(1)}, u32[]{:S(2)}, u32[]{:S(2)}) %all-to-all-start.1) | async-done | bytes 786464 | tf_op jit(solution)/shard_map/all_to_all | solution.py:91
  414.7 3.8 all-to-all-start.2
  420.0 10.4 %all-to-all-done.2 = f32[8,96,256]{2,1,0:T(8,128)S(1)} async-done(((f32[8,96,256]{2,1,0:T(8,128)}), f32[8,96,256]{2,1,0:T(8,128)S(1)}, u32[]{:S(2)}, u32[]{:S(2)}) %all-to-all-start.2) | async-done | bytes 786464 | tf_op jit(solution)/shard_map/all_to_all | solution.py:94
  430.5 4.1 fusion.y_ref
  434.6 23.0 %shard_map.38 = f32[8192,256]{1,0:T(8,128)} custom-call(f32[16,768,512]{2,1,0:T(8,128)} %bitcast_dynamic-update-slice_fusion.v_ref, f32[8192,256]{1,0:T(8,128)} %bitcast.42.e_ref, f32[768,256]{1,0:T(8,128)S(1)} %fusion.y_ref), custom_call_target="tpu_custom_call" | custom-call | flops 9663676416 | bytes 41943040 | tf_op jit(solution)/shard_map/pallas_call | solution.py:70
  (132 shorter events, 61.4 us)
Async XLA Ops:
  9.1 26.9 %collective-permute-start = (f32[256,512]{1,0:T(8,128)}, f32[256,512]{1,0:T(8,128)}, u32[]{:S(2)}, u32[]{:S(2)}) collective-permute-start(f32[256,512]{1,0:T(8,128)} %slice.69), channel_id=1, source_target_pairs={{0,2},{2,4},{4,6},{6,0},{1,3},{3,5},{5,7},{7,1},{8,10},{10,12},{12... | collective-permute-start | bytes 1572872 | tf_op jit(solution)/shard_map/ppermute | solution.py:107
  10.6 46.4 %collective-permute-start.2 = (f32[256,512]{1,0:T(8,128)}, f32[256,512]{1,0:T(8,128)}, u32[]{:S(2)}, u32[]{:S(2)}) collective-permute-start(f32[256,512]{1,0:T(8,128)} %slice.69), channel_id=1, source_target_pairs={{0,6},{2,0},{4,2},{6,4},{1,7},{3,1},{5,3},{7,5},{8,14},{10,8},{12,... | collective-permute-start | bytes 1572872 | tf_op jit(solution)/shard_map/ppermute | solution.py:108
  11.1 269.7 %collective-permute-start.4 = (f32[256,512]{1,0:T(8,128)}, f32[256,512]{1,0:T(8,128)}, u32[]{:S(2)}, u32[]{:S(2)}) collective-permute-start(f32[256,512]{1,0:T(8,128)} %slice.69), channel_id=1, source_target_pairs={{0,8},{8,0},{1,9},{9,1},{2,10},{10,2},{3,11},{11,3},{4,12},{12,4},... | collective-permute-start | bytes 1572872 | tf_op jit(solution)/shard_map/ppermute | solution.py:123
  15.4 270.8 %collective-permute-start.9 = (f32[512,512]{1,0:T(8,128)}, f32[512,512]{1,0:T(8,128)}, u32[]{:S(2)}, u32[]{:S(2)}) collective-permute-start(f32[512,512]{1,0:T(8,128)} %slice.72), channel_id=1, source_target_pairs={{0,8},{8,0},{1,9},{9,1},{2,10},{10,2},{3,11},{11,3},{4,12},{12,4},... | collective-permute-start | bytes 3145736 | tf_op jit(solution)/shard_map/ppermute | solution.py:123
  15.7 271.5 %collective-permute-start.10 = (f32[512,512]{1,0:T(8,128)}, f32[512,512]{1,0:T(8,128)S(1)}, u32[]{:S(2)}, u32[]{:S(2)}) collective-permute-start(f32[512,512]{1,0:T(8,128)} %slice.72), channel_id=1, source_target_pairs={{0,2},{2,4},{4,6},{6,0},{1,3},{3,5},{5,7},{7,1},{8,10},{10,12},{12... | collective-permute-start | bytes 3145736 | tf_op jit(solution)/shard_map/ppermute | solution.py:107
  24.9 350.2 %all-to-all-start = ((f32[512,16,256]{2,0,1:T(8,128)}), f32[512,16,256]{2,0,1:T(8,128)}, u32[]{:S(2)}, u32[]{:S(2)}) async-start(f32[512,16,256]{2,0,1:T(8,128)} %bitcast.124), calls=%async_computation | async-start | bytes 16777216 | tf_op jit(solution)/shard_map/all_to_all | solution.py:153
  32.3 235.5 %all-reduce.3.cloned.1.call-start = ((), (), s32[]{:S(2)}) async-start(), calls=%async_computation.3 | async-start | bytes 1572864 | tf_op jit(solution)/shard_map/psum | solution.py:155
  37.7 232.2 %collective-permute-start.1 = (f32[128,512]{1,0:T(8,128)}, f32[128,512]{1,0:T(8,128)}, u32[]{:S(2)}, u32[]{:S(2)}) collective-permute-start(f32[128,512]{1,0:T(8,128)} %slice.70), channel_id=1, source_target_pairs={{0,2},{2,4},{4,6},{6,0},{1,3},{3,5},{5,7},{7,1},{8,10},{10,12},{12... | collective-permute-start | bytes 786440 | tf_op jit(solution)/shard_map/ppermute | solution.py:113
  58.6 214.0 %collective-permute-start.3 = (f32[128,512]{1,0:T(8,128)}, f32[128,512]{1,0:T(8,128)}, u32[]{:S(2)}, u32[]{:S(2)}) collective-permute-start(f32[128,512]{1,0:T(8,128)} %slice.71), channel_id=1, source_target_pairs={{0,6},{2,0},{4,2},{6,4},{1,7},{3,1},{5,3},{7,5},{8,14},{10,8},{12,... | collective-permute-start | bytes 786440 | tf_op jit(solution)/shard_map/ppermute | solution.py:114
  269.9 24.2 %collective-permute-start.12 = (f32[512,512]{1,0:T(8,128)}, f32[512,512]{1,0:T(8,128)S(1)}, u32[]{:S(2)}, u32[]{:S(2)}) collective-permute-start(f32[512,512]{1,0:T(8,128)} %slice.72), channel_id=1, source_target_pairs={{0,6},{2,0},{4,2},{6,4},{1,7},{3,1},{5,3},{7,5},{8,14},{10,8},{12,... | collective-permute-start | bytes 3145736 | tf_op jit(solution)/shard_map/ppermute | solution.py:108
  272.7 9.2 %collective-permute-start.5 = (f32[128,512]{1,0:T(8,128)}, f32[128,512]{1,0:T(8,128)S(1)}, u32[]{:S(2)}, u32[]{:S(2)}) collective-permute-start(f32[128,512]{1,0:T(8,128)} %collective-permute-done.1), channel_id=1, source_target_pairs={{0,8},{8,0},{1,9},{9,1},{2,10},{10,2},{3,11},{11,3},{4,12},{12,4},... | collective-permute-start | bytes 786440 | tf_op jit(solution)/shard_map/ppermute | solution.py:123
  280.8 22.9 %collective-permute-start.7 = (f32[256,512]{1,0:T(8,128)}, f32[256,512]{1,0:T(8,128)S(1)}, u32[]{:S(2)}, u32[]{:S(2)}) collective-permute-start(f32[256,512]{1,0:T(8,128)} %collective-permute-done), channel_id=1, source_target_pairs={{0,8},{8,0},{1,9},{9,1},{2,10},{10,2},{3,11},{11,3},{4,12},{12,4},... | collective-permute-start | bytes 1572872 | tf_op jit(solution)/shard_map/ppermute | solution.py:123
  281.8 21.2 %collective-permute-start.6 = (f32[128,512]{1,0:T(8,128)}, f32[128,512]{1,0:T(8,128)S(1)}, u32[]{:S(2)}, u32[]{:S(2)}) collective-permute-start(f32[128,512]{1,0:T(8,128)} %collective-permute-done.3), channel_id=1, source_target_pairs={{0,8},{8,0},{1,9},{9,1},{2,10},{10,2},{3,11},{11,3},{4,12},{12,4},... | collective-permute-start | bytes 786440 | tf_op jit(solution)/shard_map/ppermute | solution.py:123
  286.2 25.3 %collective-permute-start.8 = (f32[256,512]{1,0:T(8,128)}, f32[256,512]{1,0:T(8,128)S(1)}, u32[]{:S(2)}, u32[]{:S(2)}) collective-permute-start(f32[256,512]{1,0:T(8,128)} %collective-permute-done.2), channel_id=1, source_target_pairs={{0,8},{8,0},{1,9},{9,1},{2,10},{10,2},{3,11},{11,3},{4,12},{12,4},... | collective-permute-start | bytes 1572872 | tf_op jit(solution)/shard_map/ppermute | solution.py:123
  287.2 27.6 %collective-permute-start.14 = (f32[512,512]{1,0:T(8,128)}, f32[512,512]{1,0:T(8,128)S(1)}, u32[]{:S(2)}, u32[]{:S(2)}) collective-permute-start(f32[512,512]{1,0:T(8,128)} %collective-permute-done.9), channel_id=1, source_target_pairs={{0,2},{2,4},{4,6},{6,0},{1,3},{3,5},{5,7},{7,1},{8,10},{10,12},{12... | collective-permute-start | bytes 3145736 | tf_op jit(solution)/shard_map/ppermute | solution.py:107
  294.1 59.1 %collective-permute-start.18 = (f32[256,512]{1,0:T(8,128)}, f32[256,512]{1,0:T(8,128)S(1)}, u32[]{:S(2)}, u32[]{:S(2)}) collective-permute-start(f32[256,512]{1,0:T(8,128)} %slice.69), channel_id=1, source_target_pairs={{0,1},{1,0},{2,3},{3,2},{4,5},{5,4},{6,7},{7,6},{8,9},{9,8},{10,11... | collective-permute-start | bytes 1572872 | tf_op jit(solution)/shard_map/ppermute | solution.py:123
  303.0 27.1 %collective-permute-start.11 = (f32[256,512]{1,0:T(8,128)S(1)}, f32[256,512]{1,0:T(8,128)S(1)}, u32[]{:S(2)}, u32[]{:S(2)}) collective-permute-start(f32[256,512]{1,0:T(8,128)S(1)} %slice.73), channel_id=1, source_target_pairs={{0,2},{2,4},{4,6},{6,0},{1,3},{3,5},{5,7},{7,1},{8,10},{10,12},{12... | collective-permute-start | bytes 1572872 | tf_op jit(solution)/shard_map/ppermute | solution.py:113
  303.7 26.3 %collective-permute-start.16 = (f32[512,512]{1,0:T(8,128)}, f32[512,512]{1,0:T(8,128)S(1)}, u32[]{:S(2)}, u32[]{:S(2)}) collective-permute-start(f32[512,512]{1,0:T(8,128)} %collective-permute-done.9), channel_id=1, source_target_pairs={{0,6},{2,0},{4,2},{6,4},{1,7},{3,1},{5,3},{7,5},{8,14},{10,8},{12,... | collective-permute-start | bytes 3145736 | tf_op jit(solution)/shard_map/ppermute | solution.py:108
  311.5 28.6 %collective-permute-start.13 = (f32[256,512]{1,0:T(8,128)S(1)}, f32[256,512]{1,0:T(8,128)S(1)}, u32[]{:S(2)}, u32[]{:S(2)}) collective-permute-start(f32[256,512]{1,0:T(8,128)S(1)} %slice.74), channel_id=1, source_target_pairs={{0,6},{2,0},{4,2},{6,4},{1,7},{3,1},{5,3},{7,5},{8,14},{10,8},{12,... | collective-permute-start | bytes 1572872 | tf_op jit(solution)/shard_map/ppermute | solution.py:114
  314.9 26.1 %collective-permute-start.15 = (f32[256,512]{1,0:T(8,128)S(1)}, f32[256,512]{1,0:T(8,128)S(1)}, u32[]{:S(2)}, u32[]{:S(2)}) collective-permute-start(f32[256,512]{1,0:T(8,128)S(1)} %slice.75), channel_id=1, source_target_pairs={{0,2},{2,4},{4,6},{6,0},{1,3},{3,5},{5,7},{7,1},{8,10},{10,12},{12... | collective-permute-start | bytes 1572872 | tf_op jit(solution)/shard_map/ppermute | solution.py:113
  330.0 33.8 %collective-permute-start.28 = (f32[512,512]{1,0:T(8,128)}, f32[512,512]{1,0:T(8,128)S(1)}, u32[]{:S(2)}, u32[]{:S(2)}) collective-permute-start(f32[512,512]{1,0:T(8,128)} %slice.72), channel_id=1, source_target_pairs={{0,1},{1,0},{2,3},{3,2},{4,5},{5,4},{6,7},{7,6},{8,9},{9,8},{10,11... | collective-permute-start | bytes 3145736 | tf_op jit(solution)/shard_map/ppermute | solution.py:123
  330.1 18.0 %collective-permute-start.17 = (f32[256,512]{1,0:T(8,128)S(1)}, f32[256,512]{1,0:T(8,128)S(1)}, u32[]{:S(2)}, u32[]{:S(2)}) collective-permute-start(f32[256,512]{1,0:T(8,128)S(1)} %slice.76), channel_id=1, source_target_pairs={{0,6},{2,0},{4,2},{6,4},{1,7},{3,1},{5,3},{7,5},{8,14},{10,8},{12,... | collective-permute-start | bytes 1572872 | tf_op jit(solution)/shard_map/ppermute | solution.py:114
  340.2 16.4 %collective-permute-start.21 = (f32[256,512]{1,0:T(8,128)}, f32[256,512]{1,0:T(8,128)S(1)}, u32[]{:S(2)}, u32[]{:S(2)}) collective-permute-start(f32[256,512]{1,0:T(8,128)} %collective-permute-done), channel_id=1, source_target_pairs={{0,1},{1,0},{2,3},{3,2},{4,5},{5,4},{6,7},{7,6},{8,9},{9,8},{10,11... | collective-permute-start | bytes 1572872 | tf_op jit(solution)/shard_map/ppermute | solution.py:123
  341.0 16.4 %collective-permute-start.22 = (f32[256,512]{1,0:T(8,128)}, f32[256,512]{1,0:T(8,128)S(1)}, u32[]{:S(2)}, u32[]{:S(2)}) collective-permute-start(f32[256,512]{1,0:T(8,128)} %collective-permute-done.2), channel_id=1, source_target_pairs={{0,1},{1,0},{2,3},{3,2},{4,5},{5,4},{6,7},{7,6},{8,9},{9,8},{10,11... | collective-permute-start | bytes 1572872 | tf_op jit(solution)/shard_map/ppermute | solution.py:123
  348.1 6.5 %collective-permute-start.19 = (f32[128,512]{1,0:T(8,128)}, f32[128,512]{1,0:T(8,128)S(1)}, u32[]{:S(2)}, u32[]{:S(2)}) collective-permute-start(f32[128,512]{1,0:T(8,128)} %collective-permute-done.1), channel_id=1, source_target_pairs={{0,1},{1,0},{2,3},{3,2},{4,5},{5,4},{6,7},{7,6},{8,9},{9,8},{10,11... | collective-permute-start | bytes 786440 | tf_op jit(solution)/shard_map/ppermute | solution.py:123
  359.7 5.7 %collective-permute-start.29 = (f32[512,512]{1,0:T(8,128)}, f32[512,512]{1,0:T(8,128)S(1)}, u32[]{:S(2)}, u32[]{:S(2)}) collective-permute-start(f32[512,512]{1,0:T(8,128)} %collective-permute-done.9), channel_id=1, source_target_pairs={{0,1},{1,0},{2,3},{3,2},{4,5},{5,4},{6,7},{7,6},{8,9},{9,8},{10,11... | collective-permute-start | bytes 3145736 | tf_op jit(solution)/shard_map/ppermute | solution.py:123
  360.9 10.0 %collective-permute-start.34 = (f32[512,512]{1,0:T(8,128)S(1)}, f32[512,512]{1,0:T(8,128)S(1)}, u32[]{:S(2)}, u32[]{:S(2)}) collective-permute-start(f32[512,512]{1,0:T(8,128)S(1)} %collective-permute-done.10), channel_id=1, source_target_pairs={{0,1},{1,0},{2,3},{3,2},{4,5},{5,4},{6,7},{7,6},{8,9},{9,8},{10,11... | collective-permute-start | bytes 3145736 | tf_op jit(solution)/shard_map/ppermute | solution.py:123
  363.9 8.0 %collective-permute-start.35 = (f32[512,512]{1,0:T(8,128)S(1)}, f32[512,512]{1,0:T(8,128)S(1)}, u32[]{:S(2)}, u32[]{:S(2)}) collective-permute-start(f32[512,512]{1,0:T(8,128)S(1)} %collective-permute-done.14), channel_id=1, source_target_pairs={{0,1},{1,0},{2,3},{3,2},{4,5},{5,4},{6,7},{7,6},{8,9},{9,8},{10,11... | collective-permute-start | bytes 3145736 | tf_op jit(solution)/shard_map/ppermute | solution.py:123
  367.8 5.2 %collective-permute-start.36 = (f32[512,512]{1,0:T(8,128)S(1)}, f32[512,512]{1,0:T(8,128)S(1)}, u32[]{:S(2)}, u32[]{:S(2)}) collective-permute-start(f32[512,512]{1,0:T(8,128)S(1)} %collective-permute-done.12), channel_id=1, source_target_pairs={{0,1},{1,0},{2,3},{3,2},{4,5},{5,4},{6,7},{7,6},{8,9},{9,8},{10,11... | collective-permute-start | bytes 3145736 | tf_op jit(solution)/shard_map/ppermute | solution.py:123
  368.7 5.4 %collective-permute-start.37 = (f32[512,512]{1,0:T(8,128)S(1)}, f32[512,512]{1,0:T(8,128)S(1)}, u32[]{:S(2)}, u32[]{:S(2)}) collective-permute-start(f32[512,512]{1,0:T(8,128)S(1)} %collective-permute-done.16), channel_id=1, source_target_pairs={{0,1},{1,0},{2,3},{3,2},{4,5},{5,4},{6,7},{7,6},{8,9},{9,8},{10,11... | collective-permute-start | bytes 3145736 | tf_op jit(solution)/shard_map/ppermute | solution.py:123
  396.3 17.4 %all-to-all-start.1 = ((f32[8,96,256]{2,1,0:T(8,128)}), f32[8,96,256]{2,1,0:T(8,128)S(1)}, u32[]{:S(2)}, u32[]{:S(2)}) async-start(f32[8,96,256]{2,1,0:T(8,128)} %bitcast.50), calls=%async_computation.1 | async-start | bytes 1572864 | tf_op jit(solution)/shard_map/all_to_all | solution.py:91
  414.7 15.8 %all-to-all-start.2 = ((f32[8,96,256]{2,1,0:T(8,128)}), f32[8,96,256]{2,1,0:T(8,128)S(1)}, u32[]{:S(2)}, u32[]{:S(2)}) async-start(f32[8,96,256]{2,1,0:T(8,128)} %broadcast_in_dim.183), calls=%async_computation.2 | async-start | bytes 1572864 | tf_op jit(solution)/shard_map/all_to_all | solution.py:94
  (13 other events, 139.0 us)
Sparse Core Ops, SparseCore 0:
  37.8 229.9 all-reduce.2

commit v2 on v0

v2 whole, which is shorter than its diff:
```python
import functools

import jax
import jax.numpy as jnp
from jax import lax
from jax.experimental import pallas as pl
from jax.experimental.pallas import tpu as pltpu
from jax.sharding import Mesh
from jax.sharding import PartitionSpec as P

AXES = ("ylo", "z", "yhi", "x", "core")
ROW = ("ylo", "z")
COL = ("yhi", "x", "core")


def halves(values):
    high = values.astype(jnp.bfloat16)
    low = (values - high.astype(jnp.float32)).astype(jnp.bfloat16)
    return high, low


def triple(left, right, dims):
    left_high, left_low = halves(left)
    right_high, right_low = halves(right)

    def dot(a, b):
        return lax.dot_general(a, b, (dims, ((), ())), preferred_element_type=jnp.float32)

    return dot(left_high, right_high) + (dot(left_high, right_low) + dot(left_low, right_high))


def fetch(sources, places, k, buffers, sems):
    slot = lax.rem(k, 2)
    for n, (source, buffer) in enumerate(zip(sources, buffers)):
        sem = sems.at[n, slot]
        if isinstance(source, list):
            for i, piece in enumerate(source):

                @pl.when(k == i)
                def _(piece=piece):
                    pltpu.make_async_copy(piece, buffer.at[slot], sem).start()

        else:
            depth = buffer.shape[1]
            rows = pl.ds(pl.multiple_of(places[k] * depth, depth), depth)
            pltpu.make_async_copy(source.at[rows], buffer.at[slot], sem).start()


def arrive(k, buffers, sems):
    slot = lax.rem(k, 2)
    for n, buffer in enumerate(buffers):
        pltpu.make_async_copy(buffer.at[slot], buffer.at[slot], sems.at[n, slot]).wait()
    return slot


def pass_kernel(blocks, has_old, has_new, places, e_ref, *rest):
    rest = list(rest)
    old = [rest.pop(0) for _ in range(blocks)] if has_old else None
    new = [rest.pop(0) for _ in range(blocks)] if has_new else None
    if has_old:
        t_ref, sum_ref = rest.pop(0), rest.pop(0)
        o_ref = rest.pop(0)
    if has_new:
        w_ref = rest.pop(0)
    sources, buffers = [e_ref], [rest.pop(0)]
    if has_old:
        sources.append(old)
        buffers.append(rest.pop(0))
    if has_new:
        sources.append(new)
        buffers.append(rest.pop(0))
    if has_old:
        o_buf, y_ref, o_sems = rest.pop(0), rest.pop(0), rest.pop(0)
    sems = rest.pop(0)
    depth = buffers[0].shape[1]

    def leave(k):
        slot = lax.rem(k, 2)
        rows = pl.ds(pl.multiple_of(places[k] * depth, depth), depth)
        return pltpu.make_async_copy(o_buf.at[slot], o_ref.at[rows], o_sems.at[slot])

    fetch(sources, places, 0, buffers, sems)
    if has_old:
        y_ref[...] = triple(t_ref[...], sum_ref[...], ((1,), (0,)))
    if has_new:
        w_ref[...] = jnp.zeros_like(w_ref)

    @pl.loop(0, blocks)
    def _(k):
        @pl.when(k + 1 < blocks)
        def _():
            fetch(sources, places, k + 1, buffers, sems)

        slot = arrive(k, buffers, sems)
        block = buffers[0][slot]
        if has_old:

            @pl.when(k >= 2)
            def _():
                leave(k - 2).wait()

            block = block - triple(buffers[1][slot], y_ref[...], ((0,), (0,)))
            o_buf[slot] = block
            leave(k).start()
        if has_new:
            w_ref[...] += triple(buffers[-1][slot], block, ((1,), (0,)))

    if has_old:
        leave(blocks - 2).wait()
        leave(blocks - 1).wait()


def one_pass(places, block, old=None, factor=None, total=None, new=None):
    pieces = old if old is not None else new
    blocks = len(pieces)
    count, depth = pieces[0].shape
    width = block.shape[1]
    far = pl.BlockSpec(memory_space=pltpu.HBM)
    near = pl.BlockSpec(memory_space=pltpu.VMEM)
    operands, in_specs = [places, block], [pl.BlockSpec(memory_space=pltpu.SMEM), far]
    out_specs, out_shape = [], []
    scratch = [pltpu.VMEM((2, depth, width), jnp.float32)]
    products = 0
    for pieces in (old, new):
        if pieces is not None:
            operands += pieces
            in_specs += [far] * blocks
            scratch.append(pltpu.VMEM((2, count, depth), jnp.float32))
            products += 1
    if old is not None:
        operands += [factor, total]
        in_specs += [near, near]
        out_specs.append(far)
        out_shape.append(jax.ShapeDtypeStruct(block.shape, jnp.float32))
        scratch += [
            pltpu.VMEM((2, depth, width), jnp.float32),
            pltpu.VMEM((count, width), jnp.float32),
            pltpu.SemaphoreType.DMA((2,)),
        ]
    if new is not None:
        out_specs.append(near)
        out_shape.append(jax.ShapeDtypeStruct((count, width), jnp.float32))
    scratch.append(pltpu.SemaphoreType.DMA((1 + products, 2)))
    return pl.pallas_call(
        functools.partial(pass_kernel, blocks, old is not None, new is not None),
        in_specs=in_specs,
        out_specs=out_specs,
        out_shape=out_shape,
        scratch_shapes=scratch,
        compiler_params=pltpu.CompilerParams(vmem_limit_bytes=60 * 2**20),
        cost_estimate=pl.CostEstimate(
            flops=6 * products * blocks * count * depth * width,
            bytes_accessed=4 * blocks * depth * (products * count + 2 * width),
            transcendentals=0,
        ),
    )(*operands)


def exchange_sum(values, axes):
    groups = lax.axis_size(axes)
    parts = lax.all_to_all(values, axes, split_axis=0, concat_axis=0, tiled=True)
    total = jnp.sum(parts.reshape(groups, -1, parts.shape[1]), axis=0)
    spread = jnp.broadcast_to(total[None], (groups,) + total.shape).reshape(parts.shape)
    return lax.all_to_all(spread, axes, split_axis=0, concat_axis=0, tiled=True)


def turn(sign):
    size = lax.axis_size("x")
    pairs = []
    for x in range(size):
        for core in range(2):
            step = sign if core == 0 else -sign
            pairs.append((x * 2 + core, (x + step) % size * 2 + core))
    return pairs


def x_ring(piece):
    near = lax.ppermute(piece, ("x", "core"), turn(1))
    other = lax.ppermute(piece, ("x", "core"), turn(-1))
    far = lax.ppermute(near, ("x", "core"), turn(1))
    return [piece, near, other, far]


def swap(piece, axis):
    return lax.ppermute(piece, axis, [(0, 1), (1, 0)])


def gather(piece, x_first):
    if x_first:
        held = x_ring(piece)
        held = held + [swap(part, "yhi") for part in held]
    else:
        held = x_ring(piece) + x_ring(swap(piece, "yhi"))
    return held + [swap(part, "core") for part in held]


def block_places():
    size = lax.axis_size("x")
    yhi, x, core = (lax.axis_index(name) for name in COL)
    places = []
    for c in (core, 1 - core):
        sign = 1 - 2 * c
        for y in (yhi, 1 - yhi):
            for step in (0, -1, 1, -2):
                places.append((y * size + lax.rem(x + sign * step + size, size)) * 2 + c)
    return jnp.stack(places).astype(jnp.int32)


def on_device(eigvecs, panels, tri_factors):
    count, block_size, depth = panels.shape
    start = (lax.axis_index(ROW) * lax.axis_size(COL) + lax.axis_index(COL)) * depth
    place = start + lax.broadcasted_iota(jnp.int32, (block_size, depth), 1)
    limit = lax.broadcasted_iota(jnp.int32, (block_size, depth), 0)
    vectors = []
    for j in reversed(range(count)):
        gap = place - limit - (j + 1) * block_size
        shaped = jnp.where(gap < 0, 0.0, jnp.where(gap == 0, 1.0, panels[j]))
        vectors.append(gather(shaped, j % 2 == 1))
    places = block_places()
    block = lax.all_to_all(eigvecs, COL, split_axis=1, concat_axis=0, tiled=True)
    (w,) = one_pass(places, block, new=vectors[0])
    for i in range(count):
        factor = tri_factors[count - 1 - i]
        total = exchange_sum(w, ROW)
        if i + 1 < count:
            block, w = one_pass(places, block, vectors[i], factor, total, vectors[i + 1])
        else:
            (block,) = one_pass(places, block, vectors[i], factor, total)
    return block


def solution(mesh):
    fine = Mesh(mesh.devices.reshape(2, 4, 2, 4, 2), AXES)
    in_specs = (P(AXES, None), P(None, None, AXES), P())
    out_specs = P(ROW, COL)
    return jax.shard_map(on_device, mesh=fine, in_specs=in_specs, out_specs=out_specs, check_vma=False)
```

time: 591 us -> 391 us (0.66)
  waiting for transfers between devices: 451 us -> 205 us
  matrix products: 98.1 us -> 0 us
  Pallas kernels: 0 us -> 78.7 us
  blocking collectives: 0 us -> 44.6 us
  starting transfers between devices: 7.81 us -> 44.2 us
  between operations: 13.7 us -> 0.75 us
    psum x3 -> x0, waiting for transfers between devices: 221 us -> none  [tile_single(): return lax.psum(values, 'row')]
    ppermute x0 -> x45, waiting for transfers between devices: none -> 194 us  [the longest x30 137 us: swap(): return lax.ppermute(piece, axis, [(0, 1), (1, 0)])]
    all_to_all x1 -> x3, waiting for transfers between devices: 128 us -> 11 us  [the longest x2 11 us: exchange_sum(): return lax.all_to_all(spread, axes, split_axis=0, concat_axis=0, tiled=True)]
    all_gather x1 -> x0, waiting for transfers between devices: 102 us -> none  [on_device(): gathered = lax.all_gather(panels, 'col', axis=2, tiled=True)]
    dot_general x9 -> x0, matrix products: 98.1 us -> none  [the longest x3 53.7 us: spread(): lax.dot_general(panel_t, right, (((0,), (0,)), ((), ())), precision=lax.P...]
    pallas_call x0 -> x4, Pallas kernels: none -> 78.7 us  [one_pass(): pl.pallas_call(functools.partial(pass_kernel, blocks, old is not None, ne...]
    all_to_all x0 -> x4, blocking collectives: none -> 44.6 us  [the longest x3 34.3 us: exchange_sum(): lax.all_to_all(values, axes, split_axis=0, concat_axis=0, tiled=True)]
    ppermute x0 -> x45, starting transfers between devices: none -> 29.8 us  [the longest x30 18.1 us: swap(): return lax.ppermute(piece, axis, [(0, 1), (1, 0)])]
  transfers between devices with their start and end apart: 5 -> 48, of which waited for: 5 -> 17; matrix products, arithmetic and copies ran while one was open for 1% -> 1% of each run, Pallas kernels for 0% -> 10%
where the time goes in v2:
time: 391 us; the launch traced here: 387 us
  waiting for transfers between devices  205 us (52%)
  Pallas kernels  78.7 us (20%)
  blocking collectives  44.6 us (11%)
  starting transfers between devices  44.2 us (11%)
  local copies, waits for them, and re-layouts  13.4 us (3%)
    ppermute x30, waiting for transfers between devices, swap(): return lax.ppermute(piece, axis, [(0, 1), (1, 0)])  137 us
    pallas_call x4, Pallas kernels, one_pass(): pl.pallas_call(functools.partial(pass_kernel, blocks, old is not None, ne...  78.7 us
    ppermute x5, waiting for transfers between devices, x_ring(): near = lax.ppermute(piece, ('x', 'core'), turn(1))  38.8 us
    all_to_all x3, blocking collectives, exchange_sum(): lax.all_to_all(values, axes, split_axis=0, concat_axis=0, tiled=True)  34.3 us
    ppermute x30, starting transfers between devices, swap(): return lax.ppermute(piece, axis, [(0, 1), (1, 0)])  18.1 us
    ppermute x5, waiting for transfers between devices, x_ring(): other = lax.ppermute(piece, ('x', 'core'), turn(-1))  12.8 us
    all_to_all x2, waiting for transfers between devices, exchange_sum(): return lax.all_to_all(spread, axes, split_axis=0, concat_axis=0, tiled=True)  11 us
    all_to_all x1, blocking collectives, exchange_sum(): return lax.all_to_all(spread, axes, split_axis=0, concat_axis=0, tiled=True)  10.3 us
  transfers between devices with their start and end apart: 48, of which 17 were waited for; matrix products, arithmetic and copies ran while one was open for 1% of the time, Pallas kernels for 10%

profile of v2, /device:TPU:2, one launch (start us, length us, event | category | flops | bytes accessed | tf_op | source)
XLA Modules:
  0.0 387.3 jit_solution(12589507564219700149)
XLA Ops:
  0.0 7.7 %copy.7 = f32[64,16,8,256]{3,2,0,1:T(8,128)} copy(f32[64,16,8,256]{3,2,1,0:T(8,128)} %bitcast.48) | data formatting | bytes 16777216 | tf_op jit(solution)/shard_map/all_to_all | solution.py:220
  7.7 7.6 %all-to-all-start = ((f32[512,16,256]{2,0,1:T(8,128)}), f32[512,16,256]{2,0,1:T(8,128)}, u32[]{:S(2)}, u32[]{:S(2)}) async-start(f32[512,16,256]{2,0,1:T(8,128)} %bitcast.47), calls=%async_computation | async-start | bytes 16777216 | tf_op jit(solution)/shard_map/all_to_all | solution.py:220
  15.6 3.1 collective-permute-start.3
  22.2 98.4 %collective-permute-done.3.rest_4_ = f32[256,512]{1,0:T(8,128)S(1)} collective-permute-done((f32[256,512]{1,0:T(8,128)S(1)}, f32[256,512]{1,0:T(8,128)S(1)}, u32[]{:S(2)}, u32[]{:S(2)}) %collective-permute-start.3) | collective-permute-done | bytes 524320 | tf_op jit(solution)/shard_map/ppermute | solution.py:185
  121.2 19.1 %collective-permute-done.rest_1_ = f32[256,512]{1,0:T(8,128)S(1)} collective-permute-done((f32[256,512]{1,0:T(8,128)S(1)}, f32[256,512]{1,0:T(8,128)S(1)}, u32[]{:S(2)}, u32[]{:S(2)}) %collective-permute-start) | collective-permute-done | bytes 524320 | tf_op jit(solution)/shard_map/ppermute | solution.py:178
  140.2 3.0 collective-permute-start.18
  143.9 7.4 %collective-permute-done.15.rest_17_.rest_1_ = f32[256,512]{1,0:T(8,128)S(1)} collective-permute-done((f32[256,512]{1,0:T(8,128)S(1)}, f32[256,512]{1,0:T(8,128)S(1)}, u32[]{:S(2)}, u32[]{:S(2)}) %collective-permute-start.15) | collective-permute-done | bytes 524320 | tf_op jit(solution)/shard_map/ppermute | solution.py:178
  151.3 2.1 collective-permute-start.31
  153.4 3.2 collective-permute-done.18.rest_20_.rest_4_
  156.7 7.1 %collective-permute-done.33.rest_20_.rest_4_ = f32[256,512]{1,0:T(8,128)S(1)} collective-permute-done((f32[256,512]{1,0:T(8,128)S(1)}, f32[256,512]{1,0:T(8,128)S(1)}, u32[]{:S(2)}, u32[]{:S(2)}) %collective-permute-start.33) | collective-permute-done | bytes 524320 | tf_op jit(solution)/shard_map/ppermute | solution.py:185
  163.8 2.3 collective-permute-done.30.rest_17_.rest_1_
  166.7 9.7 %collective-permute-done.4.rest_5_ = f32[256,512]{1,0:T(8,128)} collective-permute-done((f32[256,512]{1,0:T(8,128)S(1)}, f32[256,512]{1,0:T(8,128)}, u32[]{:S(2)}, u32[]{:S(2)}) %collective-permute-start.4) | collective-permute-done | bytes 524320 | tf_op jit(solution)/shard_map/ppermute | solution.py:178
  176.4 2.4 collective-permute-done.5.rest_6_
  178.8 3.2 collective-permute-done.2.rest_3_
  182.0 2.4 collective-permute-start.19
  188.0 10.3 %collective-permute-done.19.rest_21_.rest_5_ = f32[256,512]{1,0:T(8,128)S(1)} collective-permute-done((f32[256,512]{1,0:T(8,128)S(1)}, f32[256,512]{1,0:T(8,128)S(1)}, u32[]{:S(2)}, u32[]{:S(2)}) %collective-permute-start.19) | collective-permute-done | bytes 524320 | tf_op jit(solution)/shard_map/ppermute | solution.py:185
  198.7 7.6 %collective-permute-done.20.rest_22_.rest_6_ = f32[256,512]{1,0:T(8,128)S(1)} collective-permute-done((f32[256,512]{1,0:T(8,128)S(1)}, f32[256,512]{1,0:T(8,128)S(1)}, u32[]{:S(2)}, u32[]{:S(2)}) %collective-permute-start.20) | collective-permute-done | bytes 524320 | tf_op jit(solution)/shard_map/ppermute | solution.py:185
  210.7 10.4 %collective-permute-done.35.rest_22_.rest_6_ = f32[256,512]{1,0:T(8,128)S(1)} collective-permute-done((f32[256,512]{1,0:T(8,128)S(1)}, f32[256,512]{1,0:T(8,128)S(1)}, u32[]{:S(2)}, u32[]{:S(2)}) %collective-permute-start.35) | collective-permute-done | bytes 524320 | tf_op jit(solution)/shard_map/ppermute | solution.py:179
  221.9 3.3 collective-permute-start.21
  227.2 10.7 %collective-permute-done.21.rest_23_.rest_7_ = f32[256,512]{1,0:T(8,128)} collective-permute-done((f32[256,512]{1,0:T(8,128)}, f32[256,512]{1,0:T(8,128)}, u32[]{:S(2)}, u32[]{:S(2)}) %collective-permute-start.21) | collective-permute-done | bytes 524320 | tf_op jit(solution)/shard_map/ppermute | solution.py:185
  239.6 15.0 %shard_map.37 = f32[256,256]{1,0:T(8,128)} custom-call(s32[16]{0:T(128)} %stack.67.places, f32[8192,256]{1,0:T(8,128)} %bitcast.17.e_ref, f32[256,512]{1,0:T(8,128)} %copy-done.2, f32[256,512]{1,0:T(8,128)} %copy-done.12, f32[256,512]{1,0:T(8,128)} %copy-done.13, f32[256,512]{1,0:T(8,128)} %collective-permute-done.2.rest_3_, f32[256,512]{1,0:T(8,128)} %copy-done.11, ...), custom_call_target="tpu_custom_call" | custom-call | flops 3221225472 | bytes 25165824 | tf_op jit(solution)/shard_map/pallas_call | solution.py:144
  254.7 13.2 %all_to_all.70 = f32[8,32,256]{2,1,0:T(8,128)S(1)} all-to-all(f32[8,32,256]{2,1,0:T(8,128)} %bitcast.52), channel_id=1, replica_groups=mesh['ylo'=2,'z'=4,'yhi'=2,'x'=4,'core'=2] {'ylo','z'}, dimensions={0} | all-to-all | bytes 524288 | tf_op jit(solution)/shard_map/all_to_all | solution.py:161
  268.6 3.4 all-to-all-start.2
  275.2 4.0 %all-to-all-done.2 = f32[8,32,256]{2,1,0:T(8,128)S(1)} async-done(((f32[8,32,256]{2,1,0:T(8,128)}), f32[8,32,256]{2,1,0:T(8,128)S(1)}, u32[]{:S(2)}, u32[]{:S(2)}) %all-to-all-start.2) | async-done | bytes 262176 | tf_op jit(solution)/shard_map/all_to_all | solution.py:164
  279.9 23.1 %shard_map.38 = (f32[8192,256]{1,0:T(8,128)}, f32[256,256]{1,0:T(8,128)}) custom-call(s32[16]{0:T(128)} %stack.67.places, f32[8192,256]{1,0:T(8,128)} %bitcast.17.e_ref, f32[256,512]{1,0:T(8,128)} %copy-done.2, f32[256,512]{1,0:T(8,128)} %copy-done.12, f32[256,512]{1,0:T(8,128)} %copy-done.13, f32[256,512]{1,0:T(8,128)} %collective-permute-done.2.rest_3_, ...), custom_call_target="tpu_custom_call" | custom-call | flops 6442450944 | bytes 33554432 | tf_op jit(solution)/shard_map/pallas_call | solution.py:144
  303.0 10.6 %all_to_all.71 = f32[8,32,256]{2,1,0:T(8,128)S(1)} all-to-all(f32[8,32,256]{2,1,0:T(8,128)} %bitcast.53), channel_id=1, replica_groups=mesh['ylo'=2,'z'=4,'yhi'=2,'x'=4,'core'=2] {'ylo','z'}, dimensions={0} | all-to-all | bytes 524288 | tf_op jit(solution)/shard_map/all_to_all | solution.py:161
  314.3 3.4 all-to-all-start.4
  317.8 7.1 %all-to-all-done.4 = f32[8,32,256]{2,1,0:T(8,128)S(1)} async-done(((f32[8,32,256]{2,1,0:T(8,128)}), f32[8,32,256]{2,1,0:T(8,128)S(1)}, u32[]{:S(2)}, u32[]{:S(2)}) %all-to-all-start.4) | async-done | bytes 262176 | tf_op jit(solution)/shard_map/all_to_all | solution.py:164
  325.6 23.1 %shard_map.39 = (f32[8192,256]{1,0:T(8,128)}, f32[256,256]{1,0:T(8,128)}) custom-call(s32[16]{0:T(128)} %stack.67.places, f32[8192,256]{1,0:T(8,128)} %get-tuple-element.9.e_ref, f32[256,512]{1,0:T(8,128)} %copy-done.1, f32[256,512]{1,0:T(8,128)} %copy-done.4, f32[256,512]{1,0:T(8,128)} %copy-done.6, f32[256,512]{1,0:T(8,128)} %collective-permute-done.17.rest_19_.rest_3_, ...), custom_call_target="tpu_custom_call" | custom-call | flops 6442450944 | bytes 33554432 | tf_op jit(solution)/shard_map/pallas_call | solution.py:144
  348.6 10.6 %all_to_all.72 = f32[8,32,256]{2,1,0:T(8,128)S(1)} all-to-all(f32[8,32,256]{2,1,0:T(8,128)} %bitcast.54), channel_id=1, replica_groups=mesh['ylo'=2,'z'=4,'yhi'=2,'x'=4,'core'=2] {'ylo','z'}, dimensions={0} | all-to-all | bytes 524288 | tf_op jit(solution)/shard_map/all_to_all | solution.py:161
  359.2 10.3 %all_to_all.73 = f32[8,32,256]{2,1,0:T(8,128)} all-to-all(f32[8,32,256]{2,1,0:T(8,128)S(1)} %broadcast_in_dim.33), channel_id=1, replica_groups=mesh['ylo'=2,'z'=4,'yhi'=2,'x'=4,'core'=2] {'ylo','z'}, dimensions={0} | all-to-all | bytes 524288 | tf_op jit(solution)/shard_map/all_to_all | solution.py:164
  369.5 17.6 %shard_map.40 = f32[8192,256]{1,0:T(8,128)} custom-call(s32[16]{0:T(128)} %stack.67.places, f32[8192,256]{1,0:T(8,128)} %get-tuple-element.11.e_ref, f32[256,512]{1,0:T(8,128)} %copy-done, f32[256,512]{1,0:T(8,128)} %copy-done.5, f32[256,512]{1,0:T(8,128)} %copy-done.7, f32[256,512]{1,0:T(8,128)} %copy-done.20, f32[256,512]{1,0:T(8,128)} %copy-done.3, ...), custom_call_target="tpu_custom_call" | custom-call | flops 3221225472 | bytes 25165824 | tf_op jit(solution)/shard_map/pallas_call | solution.py:144
  (155 shorter events, 24.5 us)
Async XLA Ops:
  7.7 231.9 %all-to-all-start = ((f32[512,16,256]{2,0,1:T(8,128)}), f32[512,16,256]{2,0,1:T(8,128)}, u32[]{:S(2)}, u32[]{:S(2)}) async-start(f32[512,16,256]{2,0,1:T(8,128)} %bitcast.47), calls=%async_computation | async-start | bytes 16777216 | tf_op jit(solution)/shard_map/all_to_all | solution.py:220
  15.6 105.0 %collective-permute-start.3 = (f32[256,512]{1,0:T(8,128)S(1)}, f32[256,512]{1,0:T(8,128)S(1)}, u32[]{:S(2)}, u32[]{:S(2)}) collective-permute-start(f32[256,512]{1,0:T(8,128)S(1)} %get-tuple-element.14.rest_0_), channel_id=1, source_target_pairs={{0,8},{8,0},{1,9},{9,1},{2,10},{10,2},{3,11},{11,3},{4,12},{12,4},... | collective-permute-start | bytes 1572872 | tf_op jit(solution)/shard_map/ppermute | solution.py:185
  18.7 121.5 %collective-permute-start = (f32[256,512]{1,0:T(8,128)S(1)}, f32[256,512]{1,0:T(8,128)S(1)}, u32[]{:S(2)}, u32[]{:S(2)}) collective-permute-start(f32[256,512]{1,0:T(8,128)S(1)} %get-tuple-element.14.rest_0_), channel_id=1, source_target_pairs={{0,2},{1,7},{2,4},{3,1},{4,6},{5,3},{6,0},{7,5},{8,10},{9,15},{10,... | collective-permute-start | bytes 1572872 | tf_op jit(solution)/shard_map/ppermute | solution.py:178
  20.2 123.0 %collective-permute-start.1 = (f32[256,512]{1,0:T(8,128)S(1)}, f32[256,512]{1,0:T(8,128)S(1)}, u32[]{:S(2)}, u32[]{:S(2)}) collective-permute-start(f32[256,512]{1,0:T(8,128)S(1)} %get-tuple-element.14.rest_0_), channel_id=1, source_target_pairs={{0,6},{1,3},{2,0},{3,5},{4,2},{5,7},{6,4},{7,1},{8,14},{9,11},{10,... | collective-permute-start | bytes 1572872 | tf_op jit(solution)/shard_map/ppermute | solution.py:179
  20.7 122.5 %collective-permute-start.7 = (f32[256,512]{1,0:T(8,128)S(1)}, f32[256,512]{1,0:T(8,128)S(1)}, u32[]{:S(2)}, u32[]{:S(2)}) collective-permute-start(f32[256,512]{1,0:T(8,128)S(1)} %get-tuple-element.14.rest_0_), channel_id=1, source_target_pairs={{0,1},{1,0},{2,3},{3,2},{4,5},{5,4},{6,7},{7,6},{8,9},{9,8},{10,11... | collective-permute-start | bytes 1572872 | tf_op jit(solution)/shard_map/ppermute | solution.py:185
  20.7 130.6 %collective-permute-start.15 = (f32[256,512]{1,0:T(8,128)S(1)}, f32[256,512]{1,0:T(8,128)S(1)}, u32[]{:S(2)}, u32[]{:S(2)}) collective-permute-start(f32[256,512]{1,0:T(8,128)S(1)} %get-tuple-element.15.rest_16_.rest_0_), channel_id=1, source_target_pairs={{0,2},{1,7},{2,4},{3,1},{4,6},{5,3},{6,0},{7,5},{8,10},{9,15},{10,... | collective-permute-start | bytes 1572872 | tf_op jit(solution)/shard_map/ppermute | solution.py:178
  120.6 30.7 %collective-permute-start.16 = (f32[256,512]{1,0:T(8,128)S(1)}, f32[256,512]{1,0:T(8,128)S(1)}, u32[]{:S(2)}, u32[]{:S(2)}) collective-permute-start(f32[256,512]{1,0:T(8,128)S(1)} %get-tuple-element.15.rest_16_.rest_0_), channel_id=1, source_target_pairs={{0,6},{1,3},{2,0},{3,5},{4,2},{5,7},{6,4},{7,1},{8,14},{9,11},{10,... | collective-permute-start | bytes 1572872 | tf_op jit(solution)/shard_map/ppermute | solution.py:179
  140.2 16.4 %collective-permute-start.18 = (f32[256,512]{1,0:T(8,128)S(1)}, f32[256,512]{1,0:T(8,128)S(1)}, u32[]{:S(2)}, u32[]{:S(2)}) collective-permute-start(f32[256,512]{1,0:T(8,128)S(1)} %get-tuple-element.15.rest_16_.rest_0_), channel_id=1, source_target_pairs={{0,8},{8,0},{1,9},{9,1},{2,10},{10,2},{3,11},{11,3},{4,12},{12,4},... | collective-permute-start | bytes 1572872 | tf_op jit(solution)/shard_map/ppermute | solution.py:185
  143.2 20.6 %collective-permute-start.33 = (f32[256,512]{1,0:T(8,128)S(1)}, f32[256,512]{1,0:T(8,128)S(1)}, u32[]{:S(2)}, u32[]{:S(2)}) collective-permute-start(f32[256,512]{1,0:T(8,128)S(1)} %get-tuple-element.13.rest_16_.rest_0_), channel_id=1, source_target_pairs={{0,8},{8,0},{1,9},{9,1},{2,10},{10,2},{3,11},{11,3},{4,12},{12,4},... | collective-permute-start | bytes 1572872 | tf_op jit(solution)/shard_map/ppermute | solution.py:185
  151.3 14.8 %collective-permute-start.30 = (f32[256,512]{1,0:T(8,128)S(1)}, f32[256,512]{1,0:T(8,128)S(1)}, u32[]{:S(2)}, u32[]{:S(2)}) collective-permute-start(f32[256,512]{1,0:T(8,128)S(1)} %get-tuple-element.13.rest_16_.rest_0_), channel_id=1, source_target_pairs={{0,2},{1,7},{2,4},{3,1},{4,6},{5,3},{6,0},{7,5},{8,10},{9,15},{10,... | collective-permute-start | bytes 1572872 | tf_op jit(solution)/shard_map/ppermute | solution.py:178
  156.6 19.8 %collective-permute-start.4 = (f32[256,512]{1,0:T(8,128)S(1)}, f32[256,512]{1,0:T(8,128)}, u32[]{:S(2)}, u32[]{:S(2)}) collective-permute-start(f32[256,512]{1,0:T(8,128)S(1)} %collective-permute-done.3.rest_4_), channel_id=1, source_target_pairs={{0,2},{1,7},{2,4},{3,1},{4,6},{5,3},{6,0},{7,5},{8,10},{9,15},{10,... | collective-permute-start | bytes 1572872 | tf_op jit(solution)/shard_map/ppermute | solution.py:178
  163.8 15.0 %collective-permute-start.5 = (f32[256,512]{1,0:T(8,128)S(1)}, f32[256,512]{1,0:T(8,128)}, u32[]{:S(2)}, u32[]{:S(2)}) collective-permute-start(f32[256,512]{1,0:T(8,128)S(1)} %collective-permute-done.3.rest_4_), channel_id=1, source_target_pairs={{0,6},{1,3},{2,0},{3,5},{4,2},{5,7},{6,4},{7,1},{8,14},{9,11},{10,... | collective-permute-start | bytes 1572872 | tf_op jit(solution)/shard_map/ppermute | solution.py:179
  166.1 15.9 %collective-permute-start.2 = (f32[256,512]{1,0:T(8,128)S(1)}, f32[256,512]{1,0:T(8,128)}, u32[]{:S(2)}, u32[]{:S(2)}) collective-permute-start(f32[256,512]{1,0:T(8,128)S(1)} %collective-permute-done.rest_1_), channel_id=1, source_target_pairs={{0,2},{1,7},{2,4},{3,1},{4,6},{5,3},{6,0},{7,5},{8,10},{9,15},{10,... | collective-permute-start | bytes 1572872 | tf_op jit(solution)/shard_map/ppermute | solution.py:180
  166.1 18.3 %collective-permute-start.11 = (f32[256,512]{1,0:T(8,128)S(1)}, f32[256,512]{1,0:T(8,128)S(1)}, u32[]{:S(2)}, u32[]{:S(2)}) collective-permute-start(f32[256,512]{1,0:T(8,128)S(1)} %collective-permute-done.3.rest_4_), channel_id=1, source_target_pairs={{0,1},{1,0},{2,3},{3,2},{4,5},{5,4},{6,7},{7,6},{8,9},{9,8},{10,11... | collective-permute-start | bytes 1572872 | tf_op jit(solution)/shard_map/ppermute | solution.py:185
  166.2 19.3 %collective-permute-start.8 = (f32[256,512]{1,0:T(8,128)S(1)}, f32[256,512]{1,0:T(8,128)S(1)}, u32[]{:S(2)}, u32[]{:S(2)}) collective-permute-start(f32[256,512]{1,0:T(8,128)S(1)} %collective-permute-done.rest_1_), channel_id=1, source_target_pairs={{0,1},{1,0},{2,3},{3,2},{4,5},{5,4},{6,7},{7,6},{8,9},{9,8},{10,11... | collective-permute-start | bytes 1572872 | tf_op jit(solution)/shard_map/ppermute | solution.py:185
  182.0 16.4 %collective-permute-start.19 = (f32[256,512]{1,0:T(8,128)S(1)}, f32[256,512]{1,0:T(8,128)S(1)}, u32[]{:S(2)}, u32[]{:S(2)}) collective-permute-start(f32[256,512]{1,0:T(8,128)S(1)} %collective-permute-done.15.rest_17_.rest_1_), channel_id=1, source_target_pairs={{0,8},{8,0},{1,9},{9,1},{2,10},{10,2},{3,11},{11,3},{4,12},{12,4},... | collective-permute-start | bytes 1572872 | tf_op jit(solution)/shard_map/ppermute | solution.py:185
  184.4 21.9 %collective-permute-start.20 = (f32[256,512]{1,0:T(8,128)S(1)}, f32[256,512]{1,0:T(8,128)S(1)}, u32[]{:S(2)}, u32[]{:S(2)}) collective-permute-start(f32[256,512]{1,0:T(8,128)S(1)} %collective-permute-done.16.rest_18_.rest_2_), channel_id=1, source_target_pairs={{0,8},{8,0},{1,9},{9,1},{2,10},{10,2},{3,11},{11,3},{4,12},{12,4},... | collective-permute-start | bytes 1572872 | tf_op jit(solution)/shard_map/ppermute | solution.py:185
  185.5 20.8 %collective-permute-start.23 = (f32[256,512]{1,0:T(8,128)S(1)}, f32[256,512]{1,0:T(8,128)S(1)}, u32[]{:S(2)}, u32[]{:S(2)}) collective-permute-start(f32[256,512]{1,0:T(8,128)S(1)} %collective-permute-done.15.rest_17_.rest_1_), channel_id=1, source_target_pairs={{0,1},{1,0},{2,3},{3,2},{4,5},{5,4},{6,7},{7,6},{8,9},{9,8},{10,11... | collective-permute-start | bytes 1572872 | tf_op jit(solution)/shard_map/ppermute | solution.py:185
  185.6 22.8 %collective-permute-start.24 = (f32[256,512]{1,0:T(8,128)S(1)}, f32[256,512]{1,0:T(8,128)S(1)}, u32[]{:S(2)}, u32[]{:S(2)}) collective-permute-start(f32[256,512]{1,0:T(8,128)S(1)} %collective-permute-done.16.rest_18_.rest_2_), channel_id=1, source_target_pairs={{0,1},{1,0},{2,3},{3,2},{4,5},{5,4},{6,7},{7,6},{8,9},{9,8},{10,11... | collective-permute-start | bytes 1572872 | tf_op jit(solution)/shard_map/ppermute | solution.py:185
  188.0 20.4 %collective-permute-start.26 = (f32[256,512]{1,0:T(8,128)S(1)}, f32[256,512]{1,0:T(8,128)S(1)}, u32[]{:S(2)}, u32[]{:S(2)}) collective-permute-start(f32[256,512]{1,0:T(8,128)S(1)} %collective-permute-done.18.rest_20_.rest_4_), channel_id=1, source_target_pairs={{0,1},{1,0},{2,3},{3,2},{4,5},{5,4},{6,7},{7,6},{8,9},{9,8},{10,11... | collective-permute-start | bytes 1572872 | tf_op jit(solution)/shard_map/ppermute | solution.py:185
  209.2 16.0 %collective-permute-start.6 = (f32[256,512]{1,0:T(8,128)}, f32[256,512]{1,0:T(8,128)}, u32[]{:S(2)}, u32[]{:S(2)}) collective-permute-start(f32[256,512]{1,0:T(8,128)} %collective-permute-done.4.rest_5_), channel_id=1, source_target_pairs={{0,2},{1,7},{2,4},{3,1},{4,6},{5,3},{6,0},{7,5},{8,10},{9,15},{10,... | collective-permute-start | bytes 1572872 | tf_op jit(solution)/shard_map/ppermute | solution.py:180
  221.9 16.0 %collective-permute-start.21 = (f32[256,512]{1,0:T(8,128)}, f32[256,512]{1,0:T(8,128)}, u32[]{:S(2)}, u32[]{:S(2)}) collective-permute-start(f32[256,512]{1,0:T(8,128)} %collective-permute-done.17.rest_19_.rest_3_), channel_id=1, source_target_pairs={{0,8},{8,0},{1,9},{9,1},{2,10},{10,2},{3,11},{11,3},{4,12},{12,4},... | collective-permute-start | bytes 1572872 | tf_op jit(solution)/shard_map/ppermute | solution.py:185
  226.5 47.6 %collective-permute-start.25 = (f32[256,512]{1,0:T(8,128)}, f32[256,512]{1,0:T(8,128)}, u32[]{:S(2)}, u32[]{:S(2)}) collective-permute-start(f32[256,512]{1,0:T(8,128)} %collective-permute-done.17.rest_19_.rest_3_), channel_id=1, source_target_pairs={{0,1},{1,0},{2,3},{3,2},{4,5},{5,4},{6,7},{7,6},{8,9},{9,8},{10,11... | collective-permute-start | bytes 1572872 | tf_op jit(solution)/shard_map/ppermute | solution.py:185
  226.6 47.5 %collective-permute-start.27 = (f32[256,512]{1,0:T(8,128)}, f32[256,512]{1,0:T(8,128)}, u32[]{:S(2)}, u32[]{:S(2)}) collective-permute-start(f32[256,512]{1,0:T(8,128)} %copy-done.15), channel_id=1, source_target_pairs={{0,1},{1,0},{2,3},{3,2},{4,5},{5,4},{6,7},{7,6},{8,9},{9,8},{10,11... | collective-permute-start | bytes 1572872 | tf_op jit(solution)/shard_map/ppermute | solution.py:185
  227.0 47.6 %collective-permute-start.28 = (f32[256,512]{1,0:T(8,128)}, f32[256,512]{1,0:T(8,128)}, u32[]{:S(2)}, u32[]{:S(2)}) collective-permute-start(f32[256,512]{1,0:T(8,128)} %copy-done.17), channel_id=1, source_target_pairs={{0,1},{1,0},{2,3},{3,2},{4,5},{5,4},{6,7},{7,6},{8,9},{9,8},{10,11... | collective-permute-start | bytes 1572872 | tf_op jit(solution)/shard_map/ppermute | solution.py:185
  237.8 36.9 %collective-permute-start.36 = (f32[256,512]{1,0:T(8,128)}, f32[256,512]{1,0:T(8,128)}, u32[]{:S(2)}, u32[]{:S(2)}) collective-permute-start(f32[256,512]{1,0:T(8,128)} %copy-done.16), channel_id=1, source_target_pairs={{0,2},{1,7},{2,4},{3,1},{4,6},{5,3},{6,0},{7,5},{8,10},{9,15},{10,... | collective-permute-start | bytes 1572872 | tf_op jit(solution)/shard_map/ppermute | solution.py:180
  239.6 35.5 %collective-permute-start.29 = (f32[256,512]{1,0:T(8,128)}, f32[256,512]{1,0:T(8,128)}, u32[]{:S(2)}, u32[]{:S(2)}) collective-permute-start(f32[256,512]{1,0:T(8,128)} %collective-permute-done.21.rest_23_.rest_7_), channel_id=1, source_target_pairs={{0,1},{1,0},{2,3},{3,2},{4,5},{5,4},{6,7},{7,6},{8,9},{9,8},{10,11... | collective-permute-start | bytes 1572872 | tf_op jit(solution)/shard_map/ppermute | solution.py:185
  274.1 43.6 %collective-permute-start.39 = (f32[256,512]{1,0:T(8,128)}, f32[256,512]{1,0:T(8,128)S(1)}, u32[]{:S(2)}, u32[]{:S(2)}) collective-permute-start(f32[256,512]{1,0:T(8,128)} %copy-done.7), channel_id=1, source_target_pairs={{0,1},{1,0},{2,3},{3,2},{4,5},{5,4},{6,7},{7,6},{8,9},{9,8},{10,11... | collective-permute-start | bytes 1572872 | tf_op jit(solution)/shard_map/ppermute | solution.py:185
  274.1 43.6 %collective-permute-start.42 = (f32[256,512]{1,0:T(8,128)}, f32[256,512]{1,0:T(8,128)S(1)}, u32[]{:S(2)}, u32[]{:S(2)}) collective-permute-start(f32[256,512]{1,0:T(8,128)} %copy-done.16), channel_id=1, source_target_pairs={{0,1},{1,0},{2,3},{3,2},{4,5},{5,4},{6,7},{7,6},{8,9},{9,8},{10,11... | collective-permute-start | bytes 1572872 | tf_op jit(solution)/shard_map/ppermute | solution.py:185
  274.6 43.1 %collective-permute-start.43 = (f32[256,512]{1,0:T(8,128)}, f32[256,512]{1,0:T(8,128)S(1)}, u32[]{:S(2)}, u32[]{:S(2)}) collective-permute-start(f32[256,512]{1,0:T(8,128)} %copy-done.18), channel_id=1, source_target_pairs={{0,1},{1,0},{2,3},{3,2},{4,5},{5,4},{6,7},{7,6},{8,9},{9,8},{10,11... | collective-permute-start | bytes 1572872 | tf_op jit(solution)/shard_map/ppermute | solution.py:185
  274.7 43.1 %collective-permute-start.40 = (f32[256,512]{1,0:T(8,128)}, f32[256,512]{1,0:T(8,128)S(1)}, u32[]{:S(2)}, u32[]{:S(2)}) collective-permute-start(f32[256,512]{1,0:T(8,128)} %copy-done.20), channel_id=1, source_target_pairs={{0,1},{1,0},{2,3},{3,2},{4,5},{5,4},{6,7},{7,6},{8,9},{9,8},{10,11... | collective-permute-start | bytes 1572872 | tf_op jit(solution)/shard_map/ppermute | solution.py:185
  275.1 42.6 %collective-permute-start.44 = (f32[256,512]{1,0:T(8,128)}, f32[256,512]{1,0:T(8,128)S(1)}, u32[]{:S(2)}, u32[]{:S(2)}) collective-permute-start(f32[256,512]{1,0:T(8,128)} %collective-permute-done.36.rest_23_.rest_7_), channel_id=1, source_target_pairs={{0,1},{1,0},{2,3},{3,2},{4,5},{5,4},{6,7},{7,6},{8,9},{9,8},{10,11... | collective-permute-start | bytes 1572872 | tf_op jit(solution)/shard_map/ppermute | solution.py:185
  (52 other events, 1978.7 us)

commit v3 on v0

v3 whole, which is shorter than its diff:
```python
import functools

import jax
import jax.numpy as jnp
from jax import lax
from jax.experimental import pallas as pl
from jax.experimental.pallas import tpu as pltpu
from jax.sharding import Mesh
from jax.sharding import PartitionSpec as P

AXES = ("ylo", "z", "yhi", "x", "core")
ROW = ("ylo", "z")
COL = ("yhi", "x", "core")


def halves(values):
    high = values.astype(jnp.bfloat16)
    low = (values - high.astype(jnp.float32)).astype(jnp.bfloat16)
    return high, low


def triple(left, right, dims):
    left_high, left_low = halves(left)
    right_high, right_low = halves(right)

    def dot(a, b):
        return lax.dot_general(a, b, (dims, ((), ())), preferred_element_type=jnp.float32)

    return dot(left_high, right_high) + (dot(left_high, right_low) + dot(left_low, right_high))


LIMIT = pltpu.CompilerParams(vmem_limit_bytes=60 * 2**20)


def fetch(parts, buffer, sem):
    start = 0
    for part in parts:
        rows = part.shape[0]
        pltpu.make_async_copy(part, buffer.at[pl.ds(start, rows)], sem).start()
        start += rows


def arrive(buffer, sem):
    pltpu.make_async_copy(buffer, buffer, sem).wait()


def block_rows(ref, places, k, depth):
    return ref.at[pl.ds(pl.multiple_of(places[k] * depth, depth), depth)]


def grouped(flat, blocks):
    size = len(flat) // blocks
    return [flat[k * size : (k + 1) * size] for k in range(blocks)]


def gram_kernel(blocks, size, *refs):
    flat, (g_ref, v_buf, v_sems) = refs[:-3], refs[-3:]
    for k, parts in enumerate(grouped(flat, blocks)):
        fetch(parts, v_buf.at[k], v_sems.at[k])
    g_ref[...] = jnp.zeros_like(g_ref)

    @pl.loop(0, blocks)
    def _(k):
        arrive(v_buf.at[k], v_sems.at[k])
        first, second, third = (v_buf[k, pl.ds(j * size, size)] for j in range(3))
        across = ((1,), (1,))
        g_ref[0] += triple(first, second, across)
        g_ref[1] += triple(first, third, across)
        g_ref[2] += triple(second, third, across)


def project_kernel(blocks, places, e_ref, *refs):
    flat, (w_ref, e_buf, v_buf, e_sems, v_sems) = refs[:-5], refs[-5:]
    depth = e_buf.shape[1]
    for k, parts in enumerate(grouped(flat, blocks)):
        pltpu.make_async_copy(block_rows(e_ref, places, k, depth), e_buf.at[k], e_sems.at[k]).start()
        fetch(parts, v_buf.at[k], v_sems.at[k])
    w_ref[...] = jnp.zeros_like(w_ref)

    @pl.loop(0, blocks)
    def _(k):
        arrive(e_buf.at[k], e_sems.at[k])
        arrive(v_buf.at[k], v_sems.at[k])
        w_ref[...] += triple(v_buf[k], e_buf[k], ((1,), (0,)))


def apply_kernel(blocks, places, e_ref, m_ref, w_ref, *refs):
    flat, (o_ref, e_buf, v_buf, y_ref, e_sems, v_sems, o_sems) = refs[:-7], refs[-7:]
    depth = e_buf.shape[1]
    for k, parts in enumerate(grouped(flat, blocks)):
        pltpu.make_async_copy(block_rows(e_ref, places, k, depth), e_buf.at[k], e_sems.at[k]).start()
        fetch(parts, v_buf.at[k], v_sems.at[k])
    y_ref[...] = triple(m_ref[...], w_ref[...], ((1,), (0,)))

    def leave(k):
        return pltpu.make_async_copy(e_buf.at[k], block_rows(o_ref, places, k, depth), o_sems.at[k])

    @pl.loop(0, blocks)
    def _(k):
        arrive(e_buf.at[k], e_sems.at[k])
        arrive(v_buf.at[k], v_sems.at[k])
        e_buf[k] = e_buf[k] - triple(v_buf[k], y_ref[...], ((0,), (0,)))
        leave(k).start()

    @pl.loop(0, blocks)
    def _(k):
        leave(k).wait()


FAR = pl.BlockSpec(memory_space=pltpu.HBM)
NEAR = pl.BlockSpec(memory_space=pltpu.VMEM)
SCALARS = pl.BlockSpec(memory_space=pltpu.SMEM)


def cost(blocks, count, depth, width, passes):
    return pl.CostEstimate(
        flops=6 * blocks * count * depth * width,
        bytes_accessed=4 * blocks * depth * (count + passes * width),
        transcendentals=0,
    )


def sizes_of(pieces):
    return len(pieces), sum(part.shape[0] for part in pieces[0]), pieces[0][0].shape[1]


def gram_of(pieces, size):
    blocks, count, depth = sizes_of(pieces)
    flat = [part for parts in pieces for part in parts]
    return pl.pallas_call(
        functools.partial(gram_kernel, blocks, size),
        in_specs=[FAR] * len(flat),
        out_specs=NEAR,
        out_shape=jax.ShapeDtypeStruct((3, size, size), jnp.float32),
        scratch_shapes=[pltpu.VMEM((blocks, count, depth), jnp.float32), pltpu.SemaphoreType.DMA((blocks,))],
        compiler_params=LIMIT,
        cost_estimate=cost(blocks, count, depth, size, 0),
    )(*flat)


def project(places, block, pieces):
    blocks, count, depth = sizes_of(pieces)
    width = block.shape[1]
    flat = [part for parts in pieces for part in parts]
    return pl.pallas_call(
        functools.partial(project_kernel, blocks),
        in_specs=[SCALARS, FAR] + [FAR] * len(flat),
        out_specs=NEAR,
        out_shape=jax.ShapeDtypeStruct((count, width), jnp.float32),
        scratch_shapes=[
            pltpu.VMEM((blocks, depth, width), jnp.float32),
            pltpu.VMEM((blocks, count, depth), jnp.float32),
            pltpu.SemaphoreType.DMA((blocks,)),
            pltpu.SemaphoreType.DMA((blocks,)),
        ],
        compiler_params=LIMIT,
        cost_estimate=cost(blocks, count, depth, width, 1),
    )(places, block, *flat)


def apply(places, block, mixer, w, pieces):
    blocks, count, depth = sizes_of(pieces)
    width = block.shape[1]
    flat = [part for parts in pieces for part in parts]
    return pl.pallas_call(
        functools.partial(apply_kernel, blocks),
        in_specs=[SCALARS, FAR, NEAR, NEAR] + [FAR] * len(flat),
        out_specs=FAR,
        out_shape=jax.ShapeDtypeStruct(block.shape, jnp.float32),
        scratch_shapes=[
            pltpu.VMEM((blocks, depth, width), jnp.float32),
            pltpu.VMEM((blocks, count, depth), jnp.float32),
            pltpu.VMEM((count, width), jnp.float32),
            pltpu.SemaphoreType.DMA((blocks,)),
            pltpu.SemaphoreType.DMA((blocks,)),
            pltpu.SemaphoreType.DMA((blocks,)),
        ],
        compiler_params=LIMIT,
        cost_estimate=cost(blocks, count, depth, width, 2),
    )(places, block, mixer, w, *flat)


def mix_kernel(t_ref, g_ref, m_ref):
    size = t_ref.shape[1]

    def times(left, right):
        return triple(left, right, ((1,), (0,)))

    m_ref[...] = jnp.zeros_like(m_ref)
    for j in range(3):
        m_ref[pl.ds(j * size, size), pl.ds(j * size, size)] = t_ref[j]
    middle = -times(t_ref[1], times(g_ref[2], t_ref[2]))
    m_ref[pl.ds(size, size), pl.ds(2 * size, size)] = middle
    m_ref[pl.ds(0, size), pl.ds(size, size)] = -times(t_ref[0], times(g_ref[0], t_ref[1]))
    far = times(g_ref[1], t_ref[2]) + times(g_ref[0], middle)
    m_ref[pl.ds(0, size), pl.ds(2 * size, size)] = -times(t_ref[0], far)


def mix(tri_factors, gram):
    size = 3 * tri_factors.shape[1]
    return pl.pallas_call(
        mix_kernel,
        in_specs=[NEAR, NEAR],
        out_specs=NEAR,
        out_shape=jax.ShapeDtypeStruct((size, size), jnp.float32),
        compiler_params=LIMIT,
    )(tri_factors, gram)


def columns_kernel(e_ref, o_ref, buf, in_sems, out_sems):
    blocks, depth, width = buf.shape
    arrivals = [
        pltpu.make_async_copy(e_ref.at[:, pl.ds(k * width, width)], buf.at[k], in_sems.at[k]) for k in range(blocks)
    ]
    leaves = [
        pltpu.make_async_copy(buf.at[k], o_ref.at[pl.ds(k * depth, depth)], out_sems.at[k]) for k in range(blocks)
    ]
    for copy in arrivals:
        copy.start()
    for arrival, leave in zip(arrivals, leaves):
        arrival.wait()
        leave.start()
    for leave in leaves:
        leave.wait()


def columns_apart(eigvecs, blocks):
    depth, width = eigvecs.shape[0], eigvecs.shape[1] // blocks
    return pl.pallas_call(
        columns_kernel,
        in_specs=[pl.BlockSpec(memory_space=pltpu.HBM)],
        out_specs=pl.BlockSpec(memory_space=pltpu.HBM),
        out_shape=jax.ShapeDtypeStruct((blocks * depth, width), jnp.float32),
        scratch_shapes=[
            pltpu.VMEM((blocks, depth, width), jnp.float32),
            pltpu.SemaphoreType.DMA((blocks,)),
            pltpu.SemaphoreType.DMA((blocks,)),
        ],
        compiler_params=LIMIT,
        cost_estimate=pl.CostEstimate(flops=0, bytes_accessed=8 * blocks * depth * width, transcendentals=0),
    )(eigvecs)


def scattered(values, axes):
    return lax.all_to_all(values, axes, split_axis=0, concat_axis=0, tiled=True)


def collected(parts, axes):
    groups = lax.axis_size(axes)
    total = jnp.sum(parts.reshape(groups, -1, parts.shape[1]), axis=0)
    spread = jnp.broadcast_to(total[None], (groups,) + total.shape).reshape(parts.shape)
    return lax.all_to_all(spread, axes, split_axis=0, concat_axis=0, tiled=True)


def turn(sign):
    size = lax.axis_size("x")
    pairs = []
    for x in range(size):
        for core in range(2):
            step = sign if core == 0 else -sign
            pairs.append((x * 2 + core, (x + step) % size * 2 + core))
    return pairs


def send(piece, sign):
    return lax.ppermute(piece, ("x", "core"), turn(sign))


def swap(piece, axis):
    return lax.ppermute(piece, axis, [(0, 1), (1, 0)])


def block_places():
    size = lax.axis_size("x")
    yhi, x, core = (lax.axis_index(name) for name in COL)
    places = []
    for c in (core, 1 - core):
        sign = 1 - 2 * c
        for y in (yhi, 1 - yhi):
            for step in (0, -1, 1, -2):
                places.append((y * size + lax.rem(x + sign * step + size, size)) * 2 + c)
    return jnp.stack(places).astype(jnp.int32)


def after(values, *done):
    tied = lax.optimization_barrier((*values, *done))
    return tied[: len(values)], tied[len(values) :]


def on_device(eigvecs, panels, tri_factors):
    count, block_size, depth = panels.shape
    start = (lax.axis_index(ROW) * lax.axis_size(COL) + lax.axis_index(COL)) * depth
    place = start + lax.broadcasted_iota(jnp.int32, (block_size, depth), 1)
    limit = lax.broadcasted_iota(jnp.int32, (block_size, depth), 0)
    shaped = []
    for j in range(count):
        gap = place - limit - (j + 1) * block_size
        shaped.append(jnp.where(gap < 0, 0.0, jnp.where(gap == 0, 1.0, panels[j])))
    places = block_places()
    block = columns_apart(eigvecs, lax.axis_size(COL))

    wide = jnp.concatenate(shaped[:2], axis=0)
    slim = shaped[2]
    wide_there = swap(wide, "yhi")
    slim_near, slim_other = send(slim, 1), send(slim, -1)
    wide_near, wide_other = send(wide, 1), send(wide, -1)
    slim_held = [slim, slim_near, slim_other, send(slim_near, 1)]
    wide_far = send(wide_near, 1)
    wide_held = [wide, wide_near, wide_other, wide_far, wide_there, send(wide_there, 1), send(wide_there, -1)]
    slim_held += [swap(part, "yhi") for part in slim_held]
    wide_held += [send(wide_held[5], 1)]
    (block,), held = after((block,), *wide_held[1:], *slim_held[1:])
    wide_held[1:], slim_held[1:] = held[:7], held[7:]
    block = lax.all_to_all(block, COL, split_axis=0, concat_axis=0, tiled=True)
    pieces = list(zip(wide_held, slim_held))
    pieces += [tuple(swap(part, "core") for part in parts) for parts in pieces]

    gram = gram_of(pieces, block_size)
    size = lax.axis_size("z")
    for step in (1, 2):
        gram = gram + lax.ppermute(gram, "z", [(i, i ^ step) for i in range(size)])
    (gram,), (block,) = after((gram,), block)
    gram = gram + swap(gram, "ylo")
    mixer = mix(tri_factors, gram)
    w = collected(scattered(project(places, block, pieces), ROW), ROW)
    return apply(places, block, mixer, w, pieces)


def solution(mesh):
    fine = Mesh(mesh.devices.reshape(2, 4, 2, 4, 2), AXES)
    in_specs = (P(AXES, None), P(None, None, AXES), P())
    out_specs = P(ROW, COL)
    return jax.shard_map(on_device, mesh=fine, in_specs=in_specs, out_specs=out_specs, check_vma=False)
```

time: 591 us -> 310 us (0.52)
  waiting for transfers between devices: 451 us -> 178 us
  matrix products: 98.1 us -> 0 us
  Pallas kernels: 0 us -> 67.8 us
  starting transfers between devices: 7.81 us -> 54.7 us
  between operations: 13.7 us -> 0.34 us
  local copies, waits for them, and re-layouts: 14.5 us -> 4.43 us
    psum x3 -> x0, waiting for transfers between devices: 221 us -> none  [tile_single(): return lax.psum(values, 'row')]
    ppermute x0 -> x33, waiting for transfers between devices: none -> 131 us  [the longest x22 78.9 us: swap(): return lax.ppermute(piece, axis, [(0, 1), (1, 0)])]
    all_gather x1 -> x0, waiting for transfers between devices: 102 us -> none  [on_device(): gathered = lax.all_gather(panels, 'col', axis=2, tiled=True)]
    dot_general x9 -> x0, matrix products: 98.1 us -> none  [the longest x3 53.7 us: spread(): lax.dot_general(panel_t, right, (((0,), (0,)), ((), ())), precision=lax.P...]
    all_to_all x1 -> x3, waiting for transfers between devices: 128 us -> 47.6 us  [the longest x1 34.3 us: on_device(): block = lax.all_to_all(block, COL, split_axis=0, concat_axis=0, tiled=True)]
    pallas_call x0 -> x5, Pallas kernels: none -> 67.8 us  [the longest x1 22 us: apply(): pl.pallas_call(functools.partial(apply_kernel, blocks), in_specs=[SCALARS...]
    ppermute x0 -> x33, starting transfers between devices: none -> 36 us  [the longest x22 19.9 us: swap(): return lax.ppermute(piece, axis, [(0, 1), (1, 0)])]
    all_to_all x1 -> x3, starting transfers between devices: 7.48 us -> 18.7 us  [the longest x1 9 us: on_device(): block = lax.all_to_all(block, COL, split_axis=0, concat_axis=0, tiled=True)]
  transfers between devices with their start and end apart: 5 -> 36, of which waited for: 5 -> 22; matrix products, arithmetic and copies ran while one was open for 1% -> 1% of each run, Pallas kernels for 0% -> 9%
where the time goes in v3:
time: 310 us
  waiting for transfers between devices  178 us (57%)
  Pallas kernels  67.8 us (22%)
  starting transfers between devices  54.7 us (18%)
  local copies, waits for them, and re-layouts  4.43 us (1%)
  other arithmetic  4.09 us (1%)
    ppermute x22, waiting for transfers between devices, swap(): return lax.ppermute(piece, axis, [(0, 1), (1, 0)])  78.9 us
    ppermute x2, waiting for transfers between devices, on_device(): gram = gram + lax.ppermute(gram, 'z', [(i, i ^ step) for i in range(size)])  35 us
    all_to_all x1, waiting for transfers between devices, on_device(): block = lax.all_to_all(block, COL, split_axis=0, concat_axis=0, tiled=True)  34.3 us
    pallas_call x1, Pallas kernels, apply(): pl.pallas_call(functools.partial(apply_kernel, blocks), in_specs=[SCALARS...  22 us
    ppermute x22, starting transfers between devices, swap(): return lax.ppermute(piece, axis, [(0, 1), (1, 0)])  19.9 us
    pallas_call x1, Pallas kernels, project(): pl.pallas_call(functools.partial(project_kernel, blocks), in_specs=[SCALA...  19.5 us
    ppermute x9, waiting for transfers between devices, send(): return lax.ppermute(piece, ('x', 'core'), turn(sign))  16.7 us
    pallas_call x1, Pallas kernels, gram_of(): pl.pallas_call(functools.partial(gram_kernel, blocks, size), in_specs=[FA...  15.6 us
  transfers between devices with their start and end apart: 36, of which 22 were waited for; matrix products, arithmetic and copies ran while one was open for 1% of the time, Pallas kernels for 9%

profile of v3, /device:TPU:2, one launch (start us, length us, event | category | flops | bytes accessed | tf_op | source)
XLA Modules:
  0.0 309.7 jit_solution(18249211802373143322)
XLA Ops:
  1.8 3.3 %collective-permute-start.3 = (f32[512,512]{1,0:T(8,128)S(1)}, f32[512,512]{1,0:T(8,128)S(1)}, u32[]{:S(2)}, u32[]{:S(2)}) collective-permute-start(f32[512,512]{1,0:T(8,128)S(1)} %pad_maximum_fusion.refs_0_), channel_id=1, source_target_pairs={{0,8},{8,0},{1,9},{9,1},{2,10},{10,2},{3,11},{11,3},{4,12},{12,4},... | collective-permute-start | bytes 3145736 | tf_op jit(solution)/shard_map/ppermute | solution.py:270
  8.6 19.7 %collective-permute-done.3.refs_8_ = f32[512,512]{1,0:T(8,128)S(1)} collective-permute-done((f32[512,512]{1,0:T(8,128)S(1)}, f32[512,512]{1,0:T(8,128)S(1)}, u32[]{:S(2)}, u32[]{:S(2)}) %collective-permute-start.3) | collective-permute-done | bytes 1048608 | tf_op jit(solution)/shard_map/ppermute | solution.py:270
  29.7 3.2 %collective-permute-start.10 = (f32[256,512]{1,0:T(8,128)S(1)}, f32[256,512]{1,0:T(8,128)S(1)}, u32[]{:S(2)}, u32[]{:S(2)}) collective-permute-start(f32[256,512]{1,0:T(8,128)S(1)} %get-tuple-element.39.refs_1_), channel_id=1, source_target_pairs={{0,8},{8,0},{1,9},{9,1},{2,10},{10,2},{3,11},{11,3},{4,12},{12,4},... | collective-permute-start | bytes 1572872 | tf_op jit(solution)/shard_map/ppermute | solution.py:270
  33.3 3.2 %collective-permute-start.11 = (f32[256,512]{1,0:T(8,128)S(1)}, f32[256,512]{1,0:T(8,128)S(1)}, u32[]{:S(2)}, u32[]{:S(2)}) collective-permute-start(f32[256,512]{1,0:T(8,128)S(1)} %collective-permute-done.7.refs_3_), channel_id=1, source_target_pairs={{0,8},{8,0},{1,9},{9,1},{2,10},{10,2},{3,11},{11,3},{4,12},{12,4},... | collective-permute-start | bytes 1572872 | tf_op jit(solution)/shard_map/ppermute | solution.py:270
  36.5 9.6 %collective-permute-done.10.refs_9_ = f32[256,512]{1,0:T(8,128)S(1)} collective-permute-done((f32[256,512]{1,0:T(8,128)S(1)}, f32[256,512]{1,0:T(8,128)S(1)}, u32[]{:S(2)}, u32[]{:S(2)}) %collective-permute-start.10) | collective-permute-done | bytes 524320 | tf_op jit(solution)/shard_map/ppermute | solution.py:270
  46.6 10.8 %collective-permute-done.12.refs_13_ = f32[256,512]{1,0:T(8,128)S(1)} collective-permute-done((f32[256,512]{1,0:T(8,128)}, f32[256,512]{1,0:T(8,128)S(1)}, u32[]{:S(2)}, u32[]{:S(2)}) %collective-permute-start.12) | collective-permute-done | bytes 524320 | tf_op jit(solution)/shard_map/ppermute | solution.py:270
  58.5 6.8 %collective-permute-done.11.refs_11_ = f32[256,512]{1,0:T(8,128)S(1)} collective-permute-done((f32[256,512]{1,0:T(8,128)S(1)}, f32[256,512]{1,0:T(8,128)S(1)}, u32[]{:S(2)}, u32[]{:S(2)}) %collective-permute-start.11) | collective-permute-done | bytes 524320 | tf_op jit(solution)/shard_map/ppermute | solution.py:270
  65.3 2.7 collective-permute-start.5
  68.8 3.3 %collective-permute-start.13 = (f32[256,512]{1,0:T(8,128)S(1)}, f32[256,512]{1,0:T(8,128)}, u32[]{:S(2)}, u32[]{:S(2)}) collective-permute-start(f32[256,512]{1,0:T(8,128)S(1)} %collective-permute-done.9.refs_7_), channel_id=1, source_target_pairs={{0,8},{8,0},{1,9},{9,1},{2,10},{10,2},{3,11},{11,3},{4,12},{12,4},... | collective-permute-start | bytes 1572872 | tf_op jit(solution)/shard_map/ppermute | solution.py:270
  72.1 6.7 %shard_map.37 = f32[8192,256]{1,0:T(8,128)} custom-call(f32[512,4096]{1,0:T(8,128)} %e_ref.1), custom_call_target="tpu_custom_call" | custom-call | bytes 16777216 | tf_op jit(solution)/shard_map/pallas_call | solution.py:229
  78.8 6.3 %collective-permute-done.13.refs_15_ = f32[256,512]{1,0:T(8,128)} collective-permute-done((f32[256,512]{1,0:T(8,128)S(1)}, f32[256,512]{1,0:T(8,128)}, u32[]{:S(2)}, u32[]{:S(2)}) %collective-permute-start.13) | collective-permute-done | bytes 524320 | tf_op jit(solution)/shard_map/ppermute | solution.py:270
  85.1 6.6 %collective-permute-done.5.refs_12_ = f32[512,512]{1,0:T(8,128)} collective-permute-done((f32[512,512]{1,0:T(8,128)S(1)}, f32[512,512]{1,0:T(8,128)}, u32[]{:S(2)}, u32[]{:S(2)}) %collective-permute-start.5) | collective-permute-done | bytes 1048608 | tf_op jit(solution)/shard_map/ppermute | solution.py:266
  91.7 10.1 %collective-permute-done.6.refs_14_ = f32[512,512]{1,0:T(8,128)} collective-permute-done((f32[512,512]{1,0:T(8,128)}, f32[512,512]{1,0:T(8,128)}, u32[]{:S(2)}, u32[]{:S(2)}) %collective-permute-start.6) | collective-permute-done | bytes 1048608 | tf_op jit(solution)/shard_map/ppermute | solution.py:266
  101.8 9.0 %all-to-all-start = ((f32[16,512,256]{2,1,0:T(8,128)}), f32[16,512,256]{2,1,0:T(8,128)}, u32[]{:S(2)}, u32[]{:S(2)}) async-start(f32[16,512,256]{2,1,0:T(8,128)} %bitcast.32), calls=%async_computation | async-start | bytes 16777216 | tf_op jit(solution)/shard_map/all_to_all | solution.py:314
  112.1 3.3 %collective-permute-done.15.refs_17_ = f32[256,512]{1,0:T(8,128)S(1)} collective-permute-done((f32[256,512]{1,0:T(8,128)S(1)}, f32[256,512]{1,0:T(8,128)S(1)}, u32[]{:S(2)}, u32[]{:S(2)}) %collective-permute-start.15) | collective-permute-done | bytes 524320 | tf_op jit(solution)/shard_map/ppermute | solution.py:270
  118.2 3.4 %collective-permute-done.25.refs_27_ = f32[256,512]{1,0:T(8,128)S(1)} collective-permute-done((f32[256,512]{1,0:T(8,128)}, f32[256,512]{1,0:T(8,128)S(1)}, u32[]{:S(2)}, u32[]{:S(2)}) %collective-permute-start.25) | collective-permute-done | bytes 524320 | tf_op jit(solution)/shard_map/ppermute | solution.py:270
  124.5 2.8 collective-permute-done.22.refs_24_
  127.5 3.0 collective-permute-done.26.refs_28_
  131.5 15.6 %shard_map.38 = f32[3,256,256]{2,1,0:T(8,128)} custom-call(f32[512,512]{1,0:T(8,128)} %copy-done, f32[256,512]{1,0:T(8,128)} %copy-done.2, f32[512,512]{1,0:T(8,128)} %collective-permute-done.refs_2_, f32[256,512]{1,0:T(8,128)} %copy-done.11, f32[512,512]{1,0:T(8,128)} %collective-permute-done.1.refs_4_, f32[256,512]{1,0:T(8,128)} %collective-permute-done.8.refs_5_, ...), custom_call_target="tpu_custom_call" | custom-call | flops 9663676416 | bytes 25165824 | tf_op jit(solution)/shard_map/pallas_call | solution.py:130
  149.2 18.3 %collective-permute-done.30 = f32[3,256,256]{2,1,0:T(8,128)S(1)} collective-permute-done((f32[3,256,256]{2,1,0:T(8,128)}, f32[3,256,256]{2,1,0:T(8,128)S(1)}, u32[]{:S(2)}, u32[]{:S(2)}) %collective-permute-start.30) | collective-permute-done | bytes 786464 | tf_op jit(solution)/shard_map/ppermute | solution.py:321
  168.7 4.0 %collective-permute-start.31 = (f32[3,256,256]{2,1,0:T(8,128)S(1)}, f32[3,256,256]{2,1,0:T(8,128)S(1)}, u32[]{:S(2)}, u32[]{:S(2)}) collective-permute-start(f32[3,256,256]{2,1,0:T(8,128)S(1)} %add.226), channel_id=1, source_target_pairs={{0,32},{16,48},{32,0},{48,16},{1,33},{17,49},{33,1},{49,17},{2,34}... | collective-permute-start | bytes 2359304 | tf_op jit(solution)/shard_map/ppermute | solution.py:321
  173.3 16.7 %collective-permute-done.31 = f32[3,256,256]{2,1,0:T(8,128)S(1)} collective-permute-done((f32[3,256,256]{2,1,0:T(8,128)S(1)}, f32[3,256,256]{2,1,0:T(8,128)S(1)}, u32[]{:S(2)}, u32[]{:S(2)}) %collective-permute-start.31) | collective-permute-done | bytes 786464 | tf_op jit(solution)/shard_map/ppermute | solution.py:321
  190.1 34.3 %all-to-all-done = f32[16,512,256]{2,1,0:T(8,128)} async-done(((f32[16,512,256]{2,1,0:T(8,128)}), f32[16,512,256]{2,1,0:T(8,128)}, u32[]{:S(2)}, u32[]{:S(2)}) %all-to-all-start) | async-done | bytes 8388640 | tf_op jit(solution)/shard_map/all_to_all | solution.py:314
  224.4 19.5 %shard_map.40 = f32[768,256]{1,0:T(8,128)} custom-call(s32[16]{0:T(128)} %stack.67.places, f32[8192,256]{1,0:T(8,128)} %bitcast.20.e_ref, f32[512,512]{1,0:T(8,128)} %copy-done, f32[256,512]{1,0:T(8,128)} %copy-done.2, f32[512,512]{1,0:T(8,128)} %collective-permute-done.refs_2_, f32[256,512]{1,0:T(8,128)} %copy-done.11, ...), custom_call_target="tpu_custom_call" | custom-call | flops 9663676416 | bytes 33554432 | tf_op jit(solution)/shard_map/pallas_call | solution.py:145
  243.9 5.5 %all-to-all-start.1 = ((f32[8,96,256]{2,1,0:T(8,128)}), f32[8,96,256]{2,1,0:T(8,128)S(1)}, u32[]{:S(2)}, u32[]{:S(2)}) async-start(f32[8,96,256]{2,1,0:T(8,128)} %bitcast.34), calls=%async_computation.1 | async-start | bytes 1572864 | tf_op jit(solution)/shard_map/all_to_all | solution.py:245
  249.3 2.0 collective-permute-start.32
  251.4 10.2 %all-to-all-done.1 = f32[8,96,256]{2,1,0:T(8,128)S(1)} async-done(((f32[8,96,256]{2,1,0:T(8,128)}), f32[8,96,256]{2,1,0:T(8,128)S(1)}, u32[]{:S(2)}, u32[]{:S(2)}) %all-to-all-start.1) | async-done | bytes 786464 | tf_op jit(solution)/shard_map/all_to_all | solution.py:245
  262.6 4.2 %all-to-all-start.2 = ((f32[8,96,256]{2,1,0:T(8,128)}), f32[8,96,256]{2,1,0:T(8,128)S(1)}, u32[]{:S(2)}, u32[]{:S(2)}) async-start(f32[8,96,256]{2,1,0:T(8,128)} %broadcast_in_dim.19), calls=%async_computation.2 | async-start | bytes 1572864 | tf_op jit(solution)/shard_map/all_to_all | solution.py:252
  266.9 11.6 %collective-permute-done.32 = f32[3,256,256]{2,1,0:T(8,128)S(1)} collective-permute-done((f32[3,256,256]{2,1,0:T(8,128)S(1)}, f32[3,256,256]{2,1,0:T(8,128)S(1)}, u32[]{:S(2)}, u32[]{:S(2)}) %collective-permute-start.32) | collective-permute-done | bytes 786464 | tf_op jit(solution)/shard_map/ppermute | solution.py:270
  279.4 4.1 %shard_map.39.m_ref = f32[768,768]{1,0:T(8,128)} custom-call(f32[3,256,256]{2,1,0:T(8,128)} %t_ref.1, f32[3,256,256]{2,1,0:T(8,128)} %add.228.g_ref), custom_call_target="tpu_custom_call" | custom-call | tf_op jit(solution)/shard_map/pallas_call | solution.py:201
  283.5 3.1 %all-to-all-done.2 = f32[8,96,256]{2,1,0:T(8,128)S(1)} async-done(((f32[8,96,256]{2,1,0:T(8,128)}), f32[8,96,256]{2,1,0:T(8,128)S(1)}, u32[]{:S(2)}, u32[]{:S(2)}) %all-to-all-start.2) | async-done | bytes 786464 | tf_op jit(solution)/shard_map/all_to_all | solution.py:252
  287.5 22.0 %shard_map.41 = f32[8192,256]{1,0:T(8,128)} custom-call(s32[16]{0:T(128)} %stack.67.places, f32[8192,256]{1,0:T(8,128)} %bitcast.20.e_ref, f32[768,768]{1,0:T(8,128)} %shard_map.39.m_ref, f32[768,256]{1,0:T(8,128)} %bitcast.33, f32[512,512]{1,0:T(8,128)} %copy-done, f32[256,512]{1,0:T(8,128)} %copy-done.2, f32[512,512]{1,0:T(8,128)} %collective-permute-done.refs_2_, ...), custom_call_target="tpu_custom_call" | custom-call | flops 9663676416 | bytes 41943040 | tf_op jit(solution)/shard_map/pallas_call | solution.py:165
  (102 shorter events, 24.6 us)
Async XLA Ops:
  1.8 26.5 %collective-permute-start.3 = (f32[512,512]{1,0:T(8,128)S(1)}, f32[512,512]{1,0:T(8,128)S(1)}, u32[]{:S(2)}, u32[]{:S(2)}) collective-permute-start(f32[512,512]{1,0:T(8,128)S(1)} %pad_maximum_fusion.refs_0_), channel_id=1, source_target_pairs={{0,8},{8,0},{1,9},{9,1},{2,10},{10,2},{3,11},{11,3},{4,12},{12,4},... | collective-permute-start | bytes 3145736 | tf_op jit(solution)/shard_map/ppermute | solution.py:270
  5.0 27.9 %collective-permute-start.8 = (f32[256,512]{1,0:T(8,128)S(1)}, f32[256,512]{1,0:T(8,128)}, u32[]{:S(2)}, u32[]{:S(2)}) collective-permute-start(f32[256,512]{1,0:T(8,128)S(1)} %get-tuple-element.39.refs_1_), channel_id=1, source_target_pairs={{0,6},{1,3},{2,0},{3,5},{4,2},{5,7},{6,4},{7,1},{8,14},{9,11},{10,... | collective-permute-start | bytes 1572872 | tf_op jit(solution)/shard_map/ppermute | solution.py:266
  5.6 27.7 %collective-permute-start.7 = (f32[256,512]{1,0:T(8,128)S(1)}, f32[256,512]{1,0:T(8,128)S(1)}, u32[]{:S(2)}, u32[]{:S(2)}) collective-permute-start(f32[256,512]{1,0:T(8,128)S(1)} %get-tuple-element.39.refs_1_), channel_id=1, source_target_pairs={{0,2},{1,7},{2,4},{3,1},{4,6},{5,3},{6,0},{7,5},{8,10},{9,15},{10,... | collective-permute-start | bytes 1572872 | tf_op jit(solution)/shard_map/ppermute | solution.py:266
  7.1 61.0 %collective-permute-start = (f32[512,512]{1,0:T(8,128)S(1)}, f32[512,512]{1,0:T(8,128)}, u32[]{:S(2)}, u32[]{:S(2)}) collective-permute-start(f32[512,512]{1,0:T(8,128)S(1)} %pad_maximum_fusion.refs_0_), channel_id=1, source_target_pairs={{0,2},{1,7},{2,4},{3,1},{4,6},{5,3},{6,0},{7,5},{8,10},{9,15},{10,... | collective-permute-start | bytes 3145736 | tf_op jit(solution)/shard_map/ppermute | solution.py:266
  28.2 39.8 %collective-permute-start.4 = (f32[512,512]{1,0:T(8,128)S(1)}, f32[512,512]{1,0:T(8,128)}, u32[]{:S(2)}, u32[]{:S(2)}) collective-permute-start(f32[512,512]{1,0:T(8,128)S(1)} %collective-permute-done.3.refs_8_), channel_id=1, source_target_pairs={{0,2},{1,7},{2,4},{3,1},{4,6},{5,3},{6,0},{7,5},{8,10},{9,15},{10,... | collective-permute-start | bytes 3145736 | tf_op jit(solution)/shard_map/ppermute | solution.py:266
  29.7 16.4 %collective-permute-start.10 = (f32[256,512]{1,0:T(8,128)S(1)}, f32[256,512]{1,0:T(8,128)S(1)}, u32[]{:S(2)}, u32[]{:S(2)}) collective-permute-start(f32[256,512]{1,0:T(8,128)S(1)} %get-tuple-element.39.refs_1_), channel_id=1, source_target_pairs={{0,8},{8,0},{1,9},{9,1},{2,10},{10,2},{3,11},{11,3},{4,12},{12,4},... | collective-permute-start | bytes 1572872 | tf_op jit(solution)/shard_map/ppermute | solution.py:270
  32.9 24.4 %collective-permute-start.12 = (f32[256,512]{1,0:T(8,128)}, f32[256,512]{1,0:T(8,128)S(1)}, u32[]{:S(2)}, u32[]{:S(2)}) collective-permute-start(f32[256,512]{1,0:T(8,128)} %collective-permute-done.8.refs_5_), channel_id=1, source_target_pairs={{0,8},{8,0},{1,9},{9,1},{2,10},{10,2},{3,11},{11,3},{4,12},{12,4},... | collective-permute-start | bytes 1572872 | tf_op jit(solution)/shard_map/ppermute | solution.py:270
  33.3 32.0 %collective-permute-start.11 = (f32[256,512]{1,0:T(8,128)S(1)}, f32[256,512]{1,0:T(8,128)S(1)}, u32[]{:S(2)}, u32[]{:S(2)}) collective-permute-start(f32[256,512]{1,0:T(8,128)S(1)} %collective-permute-done.7.refs_3_), channel_id=1, source_target_pairs={{0,8},{8,0},{1,9},{9,1},{2,10},{10,2},{3,11},{11,3},{4,12},{12,4},... | collective-permute-start | bytes 1572872 | tf_op jit(solution)/shard_map/ppermute | solution.py:270
  46.1 32.7 %collective-permute-start.1 = (f32[512,512]{1,0:T(8,128)S(1)}, f32[512,512]{1,0:T(8,128)}, u32[]{:S(2)}, u32[]{:S(2)}) collective-permute-start(f32[512,512]{1,0:T(8,128)S(1)} %pad_maximum_fusion.refs_0_), channel_id=1, source_target_pairs={{0,6},{1,3},{2,0},{3,5},{4,2},{5,7},{6,4},{7,1},{8,14},{9,11},{10,... | collective-permute-start | bytes 3145736 | tf_op jit(solution)/shard_map/ppermute | solution.py:266
  57.3 11.5 %collective-permute-start.9 = (f32[256,512]{1,0:T(8,128)S(1)}, f32[256,512]{1,0:T(8,128)S(1)}, u32[]{:S(2)}, u32[]{:S(2)}) collective-permute-start(f32[256,512]{1,0:T(8,128)S(1)} %collective-permute-done.7.refs_3_), channel_id=1, source_target_pairs={{0,2},{1,7},{2,4},{3,1},{4,6},{5,3},{6,0},{7,5},{8,10},{9,15},{10,... | collective-permute-start | bytes 1572872 | tf_op jit(solution)/shard_map/ppermute | solution.py:266
  65.3 26.3 %collective-permute-start.5 = (f32[512,512]{1,0:T(8,128)S(1)}, f32[512,512]{1,0:T(8,128)}, u32[]{:S(2)}, u32[]{:S(2)}) collective-permute-start(f32[512,512]{1,0:T(8,128)S(1)} %collective-permute-done.3.refs_8_), channel_id=1, source_target_pairs={{0,6},{1,3},{2,0},{3,5},{4,2},{5,7},{6,4},{7,1},{8,14},{9,11},{10,... | collective-permute-start | bytes 3145736 | tf_op jit(solution)/shard_map/ppermute | solution.py:266
  68.0 23.6 %collective-permute-start.2 = (f32[512,512]{1,0:T(8,128)}, f32[512,512]{1,0:T(8,128)}, u32[]{:S(2)}, u32[]{:S(2)}) collective-permute-start(f32[512,512]{1,0:T(8,128)} %collective-permute-done.refs_2_), channel_id=1, source_target_pairs={{0,2},{1,7},{2,4},{3,1},{4,6},{5,3},{6,0},{7,5},{8,10},{9,15},{10,... | collective-permute-start | bytes 3145736 | tf_op jit(solution)/shard_map/ppermute | solution.py:266
  68.0 33.7 %collective-permute-start.6 = (f32[512,512]{1,0:T(8,128)}, f32[512,512]{1,0:T(8,128)}, u32[]{:S(2)}, u32[]{:S(2)}) collective-permute-start(f32[512,512]{1,0:T(8,128)} %collective-permute-done.4.refs_10_), channel_id=1, source_target_pairs={{0,2},{1,7},{2,4},{3,1},{4,6},{5,3},{6,0},{7,5},{8,10},{9,15},{10,... | collective-permute-start | bytes 3145736 | tf_op jit(solution)/shard_map/ppermute | solution.py:266
  68.8 16.3 %collective-permute-start.13 = (f32[256,512]{1,0:T(8,128)S(1)}, f32[256,512]{1,0:T(8,128)}, u32[]{:S(2)}, u32[]{:S(2)}) collective-permute-start(f32[256,512]{1,0:T(8,128)S(1)} %collective-permute-done.9.refs_7_), channel_id=1, source_target_pairs={{0,8},{8,0},{1,9},{9,1},{2,10},{10,2},{3,11},{11,3},{4,12},{12,4},... | collective-permute-start | bytes 1572872 | tf_op jit(solution)/shard_map/ppermute | solution.py:270
  101.8 122.6 %all-to-all-start = ((f32[16,512,256]{2,1,0:T(8,128)}), f32[16,512,256]{2,1,0:T(8,128)}, u32[]{:S(2)}, u32[]{:S(2)}) async-start(f32[16,512,256]{2,1,0:T(8,128)} %bitcast.32), calls=%async_computation | async-start | bytes 16777216 | tf_op jit(solution)/shard_map/all_to_all | solution.py:314
  110.8 4.9 %collective-permute-start.14 = (f32[512,512]{1,0:T(8,128)S(1)}, f32[512,512]{1,0:T(8,128)S(1)}, u32[]{:S(2)}, u32[]{:S(2)}) collective-permute-start(f32[512,512]{1,0:T(8,128)S(1)} %pad_maximum_fusion.refs_0_), channel_id=1, source_target_pairs={{0,1},{1,0},{2,3},{3,2},{4,5},{5,4},{6,7},{7,6},{8,9},{9,8},{10,11... | collective-permute-start | bytes 3145736 | tf_op jit(solution)/shard_map/ppermute | solution.py:270
  111.4 5.4 %collective-permute-start.17 = (f32[256,512]{1,0:T(8,128)S(1)}, f32[256,512]{1,0:T(8,128)S(1)}, u32[]{:S(2)}, u32[]{:S(2)}) collective-permute-start(f32[256,512]{1,0:T(8,128)S(1)} %collective-permute-done.7.refs_3_), channel_id=1, source_target_pairs={{0,1},{1,0},{2,3},{3,2},{4,5},{5,4},{6,7},{7,6},{8,9},{9,8},{10,11... | collective-permute-start | bytes 1572872 | tf_op jit(solution)/shard_map/ppermute | solution.py:270
  111.5 5.7 %collective-permute-start.19 = (f32[256,512]{1,0:T(8,128)}, f32[256,512]{1,0:T(8,128)S(1)}, u32[]{:S(2)}, u32[]{:S(2)}) collective-permute-start(f32[256,512]{1,0:T(8,128)} %collective-permute-done.8.refs_5_), channel_id=1, source_target_pairs={{0,1},{1,0},{2,3},{3,2},{4,5},{5,4},{6,7},{7,6},{8,9},{9,8},{10,11... | collective-permute-start | bytes 1572872 | tf_op jit(solution)/shard_map/ppermute | solution.py:270
  111.9 5.5 %collective-permute-start.21 = (f32[256,512]{1,0:T(8,128)}, f32[256,512]{1,0:T(8,128)S(1)}, u32[]{:S(2)}, u32[]{:S(2)}) collective-permute-start(f32[256,512]{1,0:T(8,128)} %copy-done.15), channel_id=1, source_target_pairs={{0,1},{1,0},{2,3},{3,2},{4,5},{5,4},{6,7},{7,6},{8,9},{9,8},{10,11... | collective-permute-start | bytes 1572872 | tf_op jit(solution)/shard_map/ppermute | solution.py:270
  115.7 8.2 %collective-permute-start.16 = (f32[512,512]{1,0:T(8,128)}, f32[512,512]{1,0:T(8,128)S(1)}, u32[]{:S(2)}, u32[]{:S(2)}) collective-permute-start(f32[512,512]{1,0:T(8,128)} %collective-permute-done.refs_2_), channel_id=1, source_target_pairs={{0,1},{1,0},{2,3},{3,2},{4,5},{5,4},{6,7},{7,6},{8,9},{9,8},{10,11... | collective-permute-start | bytes 3145736 | tf_op jit(solution)/shard_map/ppermute | solution.py:270
  116.8 7.4 %collective-permute-start.18 = (f32[512,512]{1,0:T(8,128)}, f32[512,512]{1,0:T(8,128)S(1)}, u32[]{:S(2)}, u32[]{:S(2)}) collective-permute-start(f32[512,512]{1,0:T(8,128)} %collective-permute-done.1.refs_4_), channel_id=1, source_target_pairs={{0,1},{1,0},{2,3},{3,2},{4,5},{5,4},{6,7},{7,6},{8,9},{9,8},{10,11... | collective-permute-start | bytes 3145736 | tf_op jit(solution)/shard_map/ppermute | solution.py:270
  117.4 4.9 %collective-permute-start.27 = (f32[256,512]{1,0:T(8,128)}, f32[256,512]{1,0:T(8,128)S(1)}, u32[]{:S(2)}, u32[]{:S(2)}) collective-permute-start(f32[256,512]{1,0:T(8,128)} %copy-done.13), channel_id=1, source_target_pairs={{0,1},{1,0},{2,3},{3,2},{4,5},{5,4},{6,7},{7,6},{8,9},{9,8},{10,11... | collective-permute-start | bytes 1572872 | tf_op jit(solution)/shard_map/ppermute | solution.py:270
  117.8 5.3 %collective-permute-start.29 = (f32[256,512]{1,0:T(8,128)}, f32[256,512]{1,0:T(8,128)S(1)}, u32[]{:S(2)}, u32[]{:S(2)}) collective-permute-start(f32[256,512]{1,0:T(8,128)} %collective-permute-done.13.refs_15_), channel_id=1, source_target_pairs={{0,1},{1,0},{2,3},{3,2},{4,5},{5,4},{6,7},{7,6},{8,9},{9,8},{10,11... | collective-permute-start | bytes 1572872 | tf_op jit(solution)/shard_map/ppermute | solution.py:270
  122.3 5.0 %collective-permute-start.22 = (f32[512,512]{1,0:T(8,128)S(1)}, f32[512,512]{1,0:T(8,128)S(1)}, u32[]{:S(2)}, u32[]{:S(2)}) collective-permute-start(f32[512,512]{1,0:T(8,128)S(1)} %collective-permute-done.3.refs_8_), channel_id=1, source_target_pairs={{0,1},{1,0},{2,3},{3,2},{4,5},{5,4},{6,7},{7,6},{8,9},{9,8},{10,11... | collective-permute-start | bytes 3145736 | tf_op jit(solution)/shard_map/ppermute | solution.py:270
  123.1 4.4 %collective-permute-start.24 = (f32[512,512]{1,0:T(8,128)}, f32[512,512]{1,0:T(8,128)S(1)}, u32[]{:S(2)}, u32[]{:S(2)}) collective-permute-start(f32[512,512]{1,0:T(8,128)} %collective-permute-done.4.refs_10_), channel_id=1, source_target_pairs={{0,1},{1,0},{2,3},{3,2},{4,5},{5,4},{6,7},{7,6},{8,9},{9,8},{10,11... | collective-permute-start | bytes 3145736 | tf_op jit(solution)/shard_map/ppermute | solution.py:270
  123.9 6.6 %collective-permute-start.26 = (f32[512,512]{1,0:T(8,128)}, f32[512,512]{1,0:T(8,128)S(1)}, u32[]{:S(2)}, u32[]{:S(2)}) collective-permute-start(f32[512,512]{1,0:T(8,128)} %collective-permute-done.5.refs_12_), channel_id=1, source_target_pairs={{0,1},{1,0},{2,3},{3,2},{4,5},{5,4},{6,7},{7,6},{8,9},{9,8},{10,11... | collective-permute-start | bytes 3145736 | tf_op jit(solution)/shard_map/ppermute | solution.py:270
  124.3 7.2 %collective-permute-start.28 = (f32[512,512]{1,0:T(8,128)}, f32[512,512]{1,0:T(8,128)}, u32[]{:S(2)}, u32[]{:S(2)}) collective-permute-start(f32[512,512]{1,0:T(8,128)} %collective-permute-done.6.refs_14_), channel_id=1, source_target_pairs={{0,1},{1,0},{2,3},{3,2},{4,5},{5,4},{6,7},{7,6},{8,9},{9,8},{10,11... | collective-permute-start | bytes 3145736 | tf_op jit(solution)/shard_map/ppermute | solution.py:270
  147.2 20.3 %collective-permute-start.30 = (f32[3,256,256]{2,1,0:T(8,128)}, f32[3,256,256]{2,1,0:T(8,128)S(1)}, u32[]{:S(2)}, u32[]{:S(2)}) collective-permute-start(f32[3,256,256]{2,1,0:T(8,128)} %shard_map.38), channel_id=1, source_target_pairs={{0,16},{16,0},{32,48},{48,32},{1,17},{17,1},{33,49},{49,33},{2,18}... | collective-permute-start | bytes 2359304 | tf_op jit(solution)/shard_map/ppermute | solution.py:321
  168.7 21.3 %collective-permute-start.31 = (f32[3,256,256]{2,1,0:T(8,128)S(1)}, f32[3,256,256]{2,1,0:T(8,128)S(1)}, u32[]{:S(2)}, u32[]{:S(2)}) collective-permute-start(f32[3,256,256]{2,1,0:T(8,128)S(1)} %add.226), channel_id=1, source_target_pairs={{0,32},{16,48},{32,0},{48,16},{1,33},{17,49},{33,1},{49,17},{2,34}... | collective-permute-start | bytes 2359304 | tf_op jit(solution)/shard_map/ppermute | solution.py:321
  243.9 17.7 %all-to-all-start.1 = ((f32[8,96,256]{2,1,0:T(8,128)}), f32[8,96,256]{2,1,0:T(8,128)S(1)}, u32[]{:S(2)}, u32[]{:S(2)}) async-start(f32[8,96,256]{2,1,0:T(8,128)} %bitcast.34), calls=%async_computation.1 | async-start | bytes 1572864 | tf_op jit(solution)/shard_map/all_to_all | solution.py:245
  249.3 29.1 %collective-permute-start.32 = (f32[3,256,256]{2,1,0:T(8,128)S(1)}, f32[3,256,256]{2,1,0:T(8,128)S(1)}, u32[]{:S(2)}, u32[]{:S(2)}) collective-permute-start(f32[3,256,256]{2,1,0:T(8,128)S(1)} %add.227), channel_id=1, source_target_pairs={{0,64},{64,0},{1,65},{65,1},{2,66},{66,2},{3,67},{67,3},{4,68},{68... | collective-permute-start | bytes 2359304 | tf_op jit(solution)/shard_map/ppermute | solution.py:270
  262.6 24.0 %all-to-all-start.2 = ((f32[8,96,256]{2,1,0:T(8,128)}), f32[8,96,256]{2,1,0:T(8,128)S(1)}, u32[]{:S(2)}, u32[]{:S(2)}) async-start(f32[8,96,256]{2,1,0:T(8,128)} %broadcast_in_dim.19), calls=%async_computation.2 | async-start | bytes 1572864 | tf_op jit(solution)/shard_map/all_to_all | solution.py:252
  (28 other events, 519.7 us)

commit v4 on v3

--- a/solution.py
+++ b/solution.py
@@ -29,6 +29,7 @@
     return dot(left_high, right_high) + (dot(left_high, right_low) + dot(left_low, right_high))
 
 
+AHEAD = 3
 LIMIT = pltpu.CompilerParams(vmem_limit_bytes=60 * 2**20)
 
 
@@ -53,14 +54,36 @@
     return [flat[k * size : (k + 1) * size] for k in range(blocks)]
 
 
+def fetch_block(pieces, places, k, e_ref, e_buf, e_sems, v_buf, v_sems):
+    pltpu.make_async_copy(block_rows(e_ref, places, k, e_buf.shape[1]), e_buf.at[k], e_sems.at[k]).start()
+    fetch_pieces(pieces, k, v_buf, v_sems)
+
+
+def fetch_pieces(pieces, k, v_buf, v_sems):
+    for i, parts in enumerate(pieces):
+        if isinstance(k, int):
+            if k == i:
+                fetch(parts, v_buf.at[i], v_sems.at[i])
+        else:
+
+            @pl.when(k == i)
+            def _(parts=parts, i=i):
+                fetch(parts, v_buf.at[i], v_sems.at[i])
+
+
 def gram_kernel(blocks, size, *refs):
     flat, (g_ref, v_buf, v_sems) = refs[:-3], refs[-3:]
-    for k, parts in enumerate(grouped(flat, blocks)):
-        fetch(parts, v_buf.at[k], v_sems.at[k])
+    pieces = grouped(flat, blocks)
+    for k in range(AHEAD):
+        fetch_pieces(pieces, k, v_buf, v_sems)
     g_ref[...] = jnp.zeros_like(g_ref)
 
     @pl.loop(0, blocks)
     def _(k):
+        @pl.when(k + AHEAD < blocks)
+        def _():
+            fetch_pieces(pieces, k + AHEAD, v_buf, v_sems)
+
         arrive(v_buf.at[k], v_sems.at[k])
         first, second, third = (v_buf[k, pl.ds(j * size, size)] for j in range(3))
         across = ((1,), (1,))
@@ -71,14 +94,17 @@
 
 def project_kernel(blocks, places, e_ref, *refs):
     flat, (w_ref, e_buf, v_buf, e_sems, v_sems) = refs[:-5], refs[-5:]
-    depth = e_buf.shape[1]
-    for k, parts in enumerate(grouped(flat, blocks)):
-        pltpu.make_async_copy(block_rows(e_ref, places, k, depth), e_buf.at[k], e_sems.at[k]).start()
-        fetch(parts, v_buf.at[k], v_sems.at[k])
+    pieces = grouped(flat, blocks)
+    for k in range(AHEAD):
+        fetch_block(pieces, places, k, e_ref, e_buf, e_sems, v_buf, v_sems)
     w_ref[...] = jnp.zeros_like(w_ref)
 
     @pl.loop(0, blocks)
     def _(k):
+        @pl.when(k + AHEAD < blocks)
+        def _():
+            fetch_block(pieces, places, k + AHEAD, e_ref, e_buf, e_sems, v_buf, v_sems)
+
         arrive(e_buf.at[k], e_sems.at[k])
         arrive(v_buf.at[k], v_sems.at[k])
         w_ref[...] += triple(v_buf[k], e_buf[k], ((1,), (0,)))
@@ -87,9 +113,9 @@
 def apply_kernel(blocks, places, e_ref, m_ref, w_ref, *refs):
     flat, (o_ref, e_buf, v_buf, y_ref, e_sems, v_sems, o_sems) = refs[:-7], refs[-7:]
     depth = e_buf.shape[1]
-    for k, parts in enumerate(grouped(flat, blocks)):
-        pltpu.make_async_copy(block_rows(e_ref, places, k, depth), e_buf.at[k], e_sems.at[k]).start()
-        fetch(parts, v_buf.at[k], v_sems.at[k])
+    pieces = grouped(flat, blocks)
+    for k in range(AHEAD):
+        fetch_block(pieces, places, k, e_ref, e_buf, e_sems, v_buf, v_sems)
     y_ref[...] = triple(m_ref[...], w_ref[...], ((1,), (0,)))
 
     def leave(k):
@@ -97,6 +123,10 @@
 
     @pl.loop(0, blocks)
     def _(k):
+        @pl.when(k + AHEAD < blocks)
+        def _():
+            fetch_block(pieces, places, k + AHEAD, e_ref, e_buf, e_sems, v_buf, v_sems)
+
         arrive(e_buf.at[k], e_sems.at[k])
         arrive(v_buf.at[k], v_sems.at[k])
         e_buf[k] = e_buf[k] - triple(v_buf[k], y_ref[...], ((0,), (0,)))
@@ -297,18 +327,20 @@
         gap = place - limit - (j + 1) * block_size
         shaped.append(jnp.where(gap < 0, 0.0, jnp.where(gap == 0, 1.0, panels[j])))
     places = block_places()
-    block = columns_apart(eigvecs, lax.axis_size(COL))
 
     wide = jnp.concatenate(shaped[:2], axis=0)
     slim = shaped[2]
     wide_there = swap(wide, "yhi")
+    wide_near, wide_other = send(wide, 1), send(wide, -1)
     slim_near, slim_other = send(slim, 1), send(slim, -1)
-    wide_near, wide_other = send(wide, 1), send(wide, -1)
+    early, (wide_there, wide_other) = after((slim, slim_near, slim_other), wide_there, wide_other)
+    there_near, there_other = send(wide_there, 1), send(wide_there, -1)
     slim_held = [slim, slim_near, slim_other, send(slim_near, 1)]
-    wide_far = send(wide_near, 1)
-    wide_held = [wide, wide_near, wide_other, wide_far, wide_there, send(wide_there, 1), send(wide_there, -1)]
-    slim_held += [swap(part, "yhi") for part in slim_held]
-    wide_held += [send(wide_held[5], 1)]
+    slim_held += [swap(part, "yhi") for part in early]
+    slim_held.append(send(slim_held[5], 1))
+    wide_held = [wide, wide_near, wide_other, send(wide_near, 1), wide_there, there_near, there_other]
+    wide_held.append(send(there_near, 1))
+    block = columns_apart(eigvecs, lax.axis_size(COL))
     (block,), held = after((block,), *wide_held[1:], *slim_held[1:])
     wide_held[1:], slim_held[1:] = held[:7], held[7:]
     block = lax.all_to_all(block, COL, split_axis=0, concat_axis=0, tiled=True)
@@ -319,11 +351,11 @@
     size = lax.axis_size("z")
     for step in (1, 2):
         gram = gram + lax.ppermute(gram, "z", [(i, i ^ step) for i in range(size)])
-    (gram,), (block,) = after((gram,), block)
-    gram = gram + swap(gram, "ylo")
-    mixer = mix(tri_factors, gram)
-    w = collected(scattered(project(places, block, pieces), ROW), ROW)
-    return apply(places, block, mixer, w, pieces)
+    other = swap(gram, "ylo")
+    parts = scattered(project(places, block, pieces), ROW)
+    (other,), (parts,) = after((other,), parts)
+    mixer = mix(tri_factors, gram + other)
+    return apply(places, block, mixer, collected(parts, ROW), pieces)
 
 
 def solution(mesh):

time: 310 us -> 293 us (0.945)
  waiting for transfers between devices: 178 us -> 159 us
  starting transfers between devices: 54.7 us -> 62.6 us
  Pallas kernels: 67.8 us -> 63.3 us
    ppermute x22 -> x21, waiting for transfers between devices: 78.9 us -> 15.2 us  [swap(): return lax.ppermute(piece, axis, [(0, 1), (1, 0)])]
    ppermute x9 -> x10, waiting for transfers between devices: 16.7 us -> 56.8 us  [send(): return lax.ppermute(piece, ('x', 'core'), turn(sign))]
    ppermute x9 -> x10, starting transfers between devices: 10.1 us -> 16.6 us  [send(): return lax.ppermute(piece, ('x', 'core'), turn(sign))]
    all_to_all x1, waiting for transfers between devices: 3.1 us -> 7.13 us  [collected(): return lax.all_to_all(spread, axes, split_axis=0, concat_axis=0, tiled=True)]
    ppermute x22 -> x21, starting transfers between devices: 19.9 us -> 21.8 us  [swap(): return lax.ppermute(piece, axis, [(0, 1), (1, 0)])]
  transfers between devices with their start and end apart: 36 -> 36, of which waited for: 22 -> 17; matrix products, arithmetic and copies ran while one was open for 1% -> 1% of each run, Pallas kernels for 9% -> 15%
where the time goes in v4:
time: 293 us
  waiting for transfers between devices  159 us (54%)
  Pallas kernels  63.3 us (22%)
  starting transfers between devices  62.6 us (21%)
  other arithmetic  4.09 us (1%)
  local copies, waits for them, and re-layouts  3.54 us (1%)
    ppermute x10, waiting for transfers between devices, send(): return lax.ppermute(piece, ('x', 'core'), turn(sign))  56.8 us
    ppermute x2, waiting for transfers between devices, on_device(): gram = gram + lax.ppermute(gram, 'z', [(i, i ^ step) for i in range(size)])  35 us
    all_to_all x1, waiting for transfers between devices, on_device(): block = lax.all_to_all(block, COL, split_axis=0, concat_axis=0, tiled=True)  32.8 us
    ppermute x21, starting transfers between devices, swap(): return lax.ppermute(piece, axis, [(0, 1), (1, 0)])  21.8 us
    pallas_call x1, Pallas kernels, apply(): pl.pallas_call(functools.partial(apply_kernel, blocks), in_specs=[SCALARS...  19.4 us
    pallas_call x1, Pallas kernels, project(): pl.pallas_call(functools.partial(project_kernel, blocks), in_specs=[SCALA...  16.9 us
    ppermute x10, starting transfers between devices, send(): return lax.ppermute(piece, ('x', 'core'), turn(sign))  16.6 us
    pallas_call x1, Pallas kernels, gram_of(): pl.pallas_call(functools.partial(gram_kernel, blocks, size), in_specs=[FA...  16.2 us
  transfers between devices with their start and end apart: 36, of which 17 were waited for; matrix products, arithmetic and copies ran while one was open for 1% of the time, Pallas kernels for 15%

profile of v4, /device:TPU:2, one launch (start us, length us, event | category | flops | bytes accessed | tf_op | source)
XLA Modules:
  0.0 292.8 jit_solution(2263500873275310407)
XLA Ops:
  0.0 1.7 fusion
  2.3 3.3 %collective-permute-start.3 = (f32[512,512]{1,0:T(8,128)S(1)}, f32[512,512]{1,0:T(8,128)}, u32[]{:S(2)}, u32[]{:S(2)}) collective-permute-start(f32[512,512]{1,0:T(8,128)S(1)} %pad_maximum_fusion.refs_0_), channel_id=1, source_target_pairs={{0,8},{8,0},{1,9},{9,1},{2,10},{10,2},{3,11},{11,3},{4,12},{12,4},... | collective-permute-start | bytes 3145736 | tf_op jit(solution)/shard_map/ppermute | solution.py:300
  5.6 2.8 collective-permute-start.2
  9.1 26.1 %collective-permute-done.2.refs_5_ = f32[256,512]{1,0:T(8,128)} collective-permute-done((f32[256,512]{1,0:T(8,128)S(1)}, f32[256,512]{1,0:T(8,128)}, u32[]{:S(2)}, u32[]{:S(2)}) %collective-permute-start.2) | collective-permute-done | bytes 524320 | tf_op jit(solution)/shard_map/ppermute | solution.py:296
  35.3 2.6 collective-permute-start.6
  37.8 2.1 collective-permute-start.9
  39.9 6.1 %collective-permute-start.10 = (f32[256,512]{1,0:T(8,128)S(1)}, f32[256,512]{1,0:T(8,128)S(1)}, u32[]{:S(2)}, u32[]{:S(2)}) collective-permute-start(f32[256,512]{1,0:T(8,128)S(1)} %get-tuple-element.29.refs_1_), channel_id=1, source_target_pairs={{0,8},{8,0},{1,9},{9,1},{2,10},{10,2},{3,11},{11,3},{4,12},{12,4},... | collective-permute-start | bytes 1572872 | tf_op jit(solution)/shard_map/ppermute | solution.py:300
  46.1 9.9 %collective-permute-done.9.refs_7_ = f32[256,512]{1,0:T(8,128)S(1)} collective-permute-done((f32[256,512]{1,0:T(8,128)S(1)}, f32[256,512]{1,0:T(8,128)S(1)}, u32[]{:S(2)}, u32[]{:S(2)}) %collective-permute-start.9) | collective-permute-done | bytes 524320 | tf_op jit(solution)/shard_map/ppermute | solution.py:296
  56.0 3.2 %collective-permute-start.7 = (f32[512,512]{1,0:T(8,128)}, f32[512,512]{1,0:T(8,128)}, u32[]{:S(2)}, u32[]{:S(2)}) collective-permute-start(f32[512,512]{1,0:T(8,128)} %collective-permute-done.3.refs_8_), channel_id=1, source_target_pairs={{0,6},{1,3},{2,0},{3,5},{4,2},{5,7},{6,4},{7,1},{8,14},{9,11},{10,... | collective-permute-start | bytes 3145736 | tf_op jit(solution)/shard_map/ppermute | solution.py:296
  59.2 1.5 collective-permute-start.8
  60.7 7.0 %collective-permute-start.12 = (f32[256,512]{1,0:T(8,128)}, f32[256,512]{1,0:T(8,128)}, u32[]{:S(2)}, u32[]{:S(2)}) collective-permute-start(f32[256,512]{1,0:T(8,128)} %collective-permute-done.2.refs_5_), channel_id=1, source_target_pairs={{0,8},{8,0},{1,9},{9,1},{2,10},{10,2},{3,11},{11,3},{4,12},{12,4},... | collective-permute-start | bytes 1572872 | tf_op jit(solution)/shard_map/ppermute | solution.py:300
  67.7 3.2 %collective-permute-start.13 = (f32[256,512]{1,0:T(8,128)S(1)}, f32[256,512]{1,0:T(8,128)}, u32[]{:S(2)}, u32[]{:S(2)}) collective-permute-start(f32[256,512]{1,0:T(8,128)S(1)} %collective-permute-done.11.refs_11_), channel_id=1, source_target_pairs={{0,2},{1,7},{2,4},{3,1},{4,6},{5,3},{6,0},{7,5},{8,10},{9,15},{10,... | collective-permute-start | bytes 1572872 | tf_op jit(solution)/shard_map/ppermute | solution.py:296
  70.8 6.7 %shard_map.37 = f32[8192,256]{1,0:T(8,128)} custom-call(f32[512,4096]{1,0:T(8,128)} %e_ref.1), custom_call_target="tpu_custom_call" | custom-call | bytes 16777216 | tf_op jit(solution)/shard_map/pallas_call | solution.py:259
  77.5 20.8 %collective-permute-done.13.refs_15_ = f32[256,512]{1,0:T(8,128)} collective-permute-done((f32[256,512]{1,0:T(8,128)S(1)}, f32[256,512]{1,0:T(8,128)}, u32[]{:S(2)}, u32[]{:S(2)}) %collective-permute-start.13) | collective-permute-done | bytes 524320 | tf_op jit(solution)/shard_map/ppermute | solution.py:296
  98.3 9.2 %all-to-all-start = ((f32[16,512,256]{2,1,0:T(8,128)}), f32[16,512,256]{2,1,0:T(8,128)}, u32[]{:S(2)}, u32[]{:S(2)}) async-start(f32[16,512,256]{2,1,0:T(8,128)} %bitcast.34), calls=%async_computation | async-start | bytes 16777216 | tf_op jit(solution)/shard_map/all_to_all | solution.py:346
  108.7 3.3 %collective-permute-done.15.refs_17_ = f32[256,512]{1,0:T(8,128)S(1)} collective-permute-done((f32[256,512]{1,0:T(8,128)S(1)}, f32[256,512]{1,0:T(8,128)S(1)}, u32[]{:S(2)}, u32[]{:S(2)}) %collective-permute-start.15) | collective-permute-done | bytes 524320 | tf_op jit(solution)/shard_map/ppermute | solution.py:300
  114.8 2.6 collective-permute-done.25.refs_27_
  122.9 3.0 %collective-permute-done.24.refs_26_ = f32[512,512]{1,0:T(8,128)} collective-permute-done((f32[512,512]{1,0:T(8,128)}, f32[512,512]{1,0:T(8,128)}, u32[]{:S(2)}, u32[]{:S(2)}) %collective-permute-start.24) | collective-permute-done | bytes 1048608 | tf_op jit(solution)/shard_map/ppermute | solution.py:300
  125.9 1.5 collective-permute-done.26.refs_28_
  128.4 16.2 %shard_map.38 = f32[3,256,256]{2,1,0:T(8,128)} custom-call(f32[512,512]{1,0:T(8,128)} %copy-done, f32[256,512]{1,0:T(8,128)} %copy-done.2, f32[512,512]{1,0:T(8,128)} %collective-permute-done.refs_2_, f32[256,512]{1,0:T(8,128)} %copy-done.8, f32[512,512]{1,0:T(8,128)} %copy-done.3, f32[256,512]{1,0:T(8,128)} %collective-permute-done.2.refs_5_, ...), custom_call_target="tpu_custom_call" | custom-call | flops 9663676416 | bytes 25165824 | tf_op jit(solution)/shard_map/pallas_call | solution.py:160
  144.6 2.0 collective-permute-start.30
  146.6 18.3 %collective-permute-done.30 = f32[3,256,256]{2,1,0:T(8,128)S(1)} collective-permute-done((f32[3,256,256]{2,1,0:T(8,128)}, f32[3,256,256]{2,1,0:T(8,128)S(1)}, u32[]{:S(2)}, u32[]{:S(2)}) %collective-permute-start.30) | collective-permute-done | bytes 786464 | tf_op jit(solution)/shard_map/ppermute | solution.py:353
  166.1 4.0 %collective-permute-start.31 = (f32[3,256,256]{2,1,0:T(8,128)S(1)}, f32[3,256,256]{2,1,0:T(8,128)S(1)}, u32[]{:S(2)}, u32[]{:S(2)}) collective-permute-start(f32[3,256,256]{2,1,0:T(8,128)S(1)} %add.226), channel_id=1, source_target_pairs={{0,32},{16,48},{32,0},{48,16},{1,33},{17,49},{33,1},{49,17},{2,34}... | collective-permute-start | bytes 2359304 | tf_op jit(solution)/shard_map/ppermute | solution.py:353
  170.8 16.7 %collective-permute-done.31 = f32[3,256,256]{2,1,0:T(8,128)S(1)} collective-permute-done((f32[3,256,256]{2,1,0:T(8,128)S(1)}, f32[3,256,256]{2,1,0:T(8,128)S(1)}, u32[]{:S(2)}, u32[]{:S(2)}) %collective-permute-start.31) | collective-permute-done | bytes 786464 | tf_op jit(solution)/shard_map/ppermute | solution.py:353
  188.3 32.8 %all-to-all-done = f32[16,512,256]{2,1,0:T(8,128)} async-done(((f32[16,512,256]{2,1,0:T(8,128)}), f32[16,512,256]{2,1,0:T(8,128)}, u32[]{:S(2)}, u32[]{:S(2)}) %all-to-all-start) | async-done | bytes 8388640 | tf_op jit(solution)/shard_map/all_to_all | solution.py:346
  221.1 16.9 %shard_map.39 = f32[768,256]{1,0:T(8,128)} custom-call(s32[16]{0:T(128)} %stack.67.places, f32[8192,256]{1,0:T(8,128)} %bitcast.20.e_ref, f32[512,512]{1,0:T(8,128)} %copy-done, f32[256,512]{1,0:T(8,128)} %copy-done.2, f32[512,512]{1,0:T(8,128)} %collective-permute-done.refs_2_, f32[256,512]{1,0:T(8,128)} %copy-done.8, f32[512,512]{1,0:T(8,128)} %copy-done.3, ...), custom_call_target="tpu_custom_call" | custom-call | flops 9663676416 | bytes 33554432 | tf_op jit(solution)/shard_map/pallas_call | solution.py:175
  238.0 5.4 %all-to-all-start.1 = ((f32[8,96,256]{2,1,0:T(8,128)}), f32[8,96,256]{2,1,0:T(8,128)S(1)}, u32[]{:S(2)}, u32[]{:S(2)}) async-start(f32[8,96,256]{2,1,0:T(8,128)} %bitcast.36), calls=%async_computation.1 | async-start | bytes 1572864 | tf_op jit(solution)/shard_map/all_to_all | solution.py:275
  243.4 12.1 %all-to-all-done.1 = f32[8,96,256]{2,1,0:T(8,128)S(1)} async-done(((f32[8,96,256]{2,1,0:T(8,128)}), f32[8,96,256]{2,1,0:T(8,128)S(1)}, u32[]{:S(2)}, u32[]{:S(2)}) %all-to-all-start.1) | async-done | bytes 786464 | tf_op jit(solution)/shard_map/all_to_all | solution.py:275
  256.5 3.6 %all-to-all-start.2 = ((f32[8,96,256]{2,1,0:T(8,128)}), f32[8,96,256]{2,1,0:T(8,128)S(1)}, u32[]{:S(2)}, u32[]{:S(2)}) async-start(f32[8,96,256]{2,1,0:T(8,128)} %broadcast_in_dim.19), calls=%async_computation.2 | async-start | bytes 1572864 | tf_op jit(solution)/shard_map/all_to_all | solution.py:282
  261.1 4.1 %shard_map.40.m_ref = f32[768,768]{1,0:T(8,128)} custom-call(f32[3,256,256]{2,1,0:T(8,128)} %t_ref.1, f32[3,256,256]{2,1,0:T(8,128)} %add.228.g_ref), custom_call_target="tpu_custom_call" | custom-call | tf_op jit(solution)/shard_map/pallas_call | solution.py:231
  265.2 7.1 %all-to-all-done.2 = f32[8,96,256]{2,1,0:T(8,128)S(1)} async-done(((f32[8,96,256]{2,1,0:T(8,128)}), f32[8,96,256]{2,1,0:T(8,128)S(1)}, u32[]{:S(2)}, u32[]{:S(2)}) %all-to-all-start.2) | async-done | bytes 786464 | tf_op jit(solution)/shard_map/all_to_all | solution.py:282
  273.2 19.4 %shard_map.41 = f32[8192,256]{1,0:T(8,128)} custom-call(s32[16]{0:T(128)} %stack.67.places, f32[8192,256]{1,0:T(8,128)} %bitcast.20.e_ref, f32[768,768]{1,0:T(8,128)} %shard_map.40.m_ref, f32[768,256]{1,0:T(8,128)} %bitcast.35, f32[512,512]{1,0:T(8,128)} %copy-done, f32[256,512]{1,0:T(8,128)} %copy-done.2, f32[512,512]{1,0:T(8,128)} %collective-permute-done.refs_2_, ...), custom_call_target="tpu_custom_call" | custom-call | flops 9663676416 | bytes 41943040 | tf_op jit(solution)/shard_map/pallas_call | solution.py:195
  (94 shorter events, 17.5 us)
Async XLA Ops:
  1.8 33.5 %collective-permute-start.4 = (f32[512,512]{1,0:T(8,128)S(1)}, f32[512,512]{1,0:T(8,128)S(1)}, u32[]{:S(2)}, u32[]{:S(2)}) collective-permute-start(f32[512,512]{1,0:T(8,128)S(1)} %pad_maximum_fusion.refs_0_), channel_id=1, source_target_pairs={{0,6},{1,3},{2,0},{3,5},{4,2},{5,7},{6,4},{7,1},{8,14},{9,11},{10,... | collective-permute-start | bytes 3145736 | tf_op jit(solution)/shard_map/ppermute | solution.py:296
  2.3 33.0 %collective-permute-start.3 = (f32[512,512]{1,0:T(8,128)S(1)}, f32[512,512]{1,0:T(8,128)}, u32[]{:S(2)}, u32[]{:S(2)}) collective-permute-start(f32[512,512]{1,0:T(8,128)S(1)} %pad_maximum_fusion.refs_0_), channel_id=1, source_target_pairs={{0,8},{8,0},{1,9},{9,1},{2,10},{10,2},{3,11},{11,3},{4,12},{12,4},... | collective-permute-start | bytes 3145736 | tf_op jit(solution)/shard_map/ppermute | solution.py:300
  5.6 29.7 %collective-permute-start.2 = (f32[256,512]{1,0:T(8,128)S(1)}, f32[256,512]{1,0:T(8,128)}, u32[]{:S(2)}, u32[]{:S(2)}) collective-permute-start(f32[256,512]{1,0:T(8,128)S(1)} %get-tuple-element.29.refs_1_), channel_id=1, source_target_pairs={{0,6},{1,3},{2,0},{3,5},{4,2},{5,7},{6,4},{7,1},{8,14},{9,11},{10,... | collective-permute-start | bytes 1572872 | tf_op jit(solution)/shard_map/ppermute | solution.py:296
  8.3 26.9 %collective-permute-start.1 = (f32[256,512]{1,0:T(8,128)S(1)}, f32[256,512]{1,0:T(8,128)S(1)}, u32[]{:S(2)}, u32[]{:S(2)}) collective-permute-start(f32[256,512]{1,0:T(8,128)S(1)} %get-tuple-element.29.refs_1_), channel_id=1, source_target_pairs={{0,2},{1,7},{2,4},{3,1},{4,6},{5,3},{6,0},{7,5},{8,10},{9,15},{10,... | collective-permute-start | bytes 1572872 | tf_op jit(solution)/shard_map/ppermute | solution.py:296
  8.3 50.8 %collective-permute-start = (f32[512,512]{1,0:T(8,128)S(1)}, f32[512,512]{1,0:T(8,128)}, u32[]{:S(2)}, u32[]{:S(2)}) collective-permute-start(f32[512,512]{1,0:T(8,128)S(1)} %pad_maximum_fusion.refs_0_), channel_id=1, source_target_pairs={{0,2},{1,7},{2,4},{3,1},{4,6},{5,3},{6,0},{7,5},{8,10},{9,15},{10,... | collective-permute-start | bytes 3145736 | tf_op jit(solution)/shard_map/ppermute | solution.py:296
  35.3 23.9 %collective-permute-start.6 = (f32[512,512]{1,0:T(8,128)}, f32[512,512]{1,0:T(8,128)}, u32[]{:S(2)}, u32[]{:S(2)}) collective-permute-start(f32[512,512]{1,0:T(8,128)} %collective-permute-done.3.refs_8_), channel_id=1, source_target_pairs={{0,2},{1,7},{2,4},{3,1},{4,6},{5,3},{6,0},{7,5},{8,10},{9,15},{10,... | collective-permute-start | bytes 3145736 | tf_op jit(solution)/shard_map/ppermute | solution.py:296
  37.8 18.1 %collective-permute-start.9 = (f32[256,512]{1,0:T(8,128)S(1)}, f32[256,512]{1,0:T(8,128)S(1)}, u32[]{:S(2)}, u32[]{:S(2)}) collective-permute-start(f32[256,512]{1,0:T(8,128)S(1)} %collective-permute-done.1.refs_3_), channel_id=1, source_target_pairs={{0,2},{1,7},{2,4},{3,1},{4,6},{5,3},{6,0},{7,5},{8,10},{9,15},{10,... | collective-permute-start | bytes 1572872 | tf_op jit(solution)/shard_map/ppermute | solution.py:296
  39.9 20.7 %collective-permute-start.10 = (f32[256,512]{1,0:T(8,128)S(1)}, f32[256,512]{1,0:T(8,128)S(1)}, u32[]{:S(2)}, u32[]{:S(2)}) collective-permute-start(f32[256,512]{1,0:T(8,128)S(1)} %get-tuple-element.29.refs_1_), channel_id=1, source_target_pairs={{0,8},{8,0},{1,9},{9,1},{2,10},{10,2},{3,11},{11,3},{4,12},{12,4},... | collective-permute-start | bytes 1572872 | tf_op jit(solution)/shard_map/ppermute | solution.py:300
  46.1 21.6 %collective-permute-start.11 = (f32[256,512]{1,0:T(8,128)S(1)}, f32[256,512]{1,0:T(8,128)S(1)}, u32[]{:S(2)}, u32[]{:S(2)}) collective-permute-start(f32[256,512]{1,0:T(8,128)S(1)} %collective-permute-done.1.refs_3_), channel_id=1, source_target_pairs={{0,8},{8,0},{1,9},{9,1},{2,10},{10,2},{3,11},{11,3},{4,12},{12,4},... | collective-permute-start | bytes 1572872 | tf_op jit(solution)/shard_map/ppermute | solution.py:300
  56.0 42.3 %collective-permute-start.7 = (f32[512,512]{1,0:T(8,128)}, f32[512,512]{1,0:T(8,128)}, u32[]{:S(2)}, u32[]{:S(2)}) collective-permute-start(f32[512,512]{1,0:T(8,128)} %collective-permute-done.3.refs_8_), channel_id=1, source_target_pairs={{0,6},{1,3},{2,0},{3,5},{4,2},{5,7},{6,4},{7,1},{8,14},{9,11},{10,... | collective-permute-start | bytes 3145736 | tf_op jit(solution)/shard_map/ppermute | solution.py:296
  59.2 39.1 %collective-permute-start.5 = (f32[512,512]{1,0:T(8,128)}, f32[512,512]{1,0:T(8,128)}, u32[]{:S(2)}, u32[]{:S(2)}) collective-permute-start(f32[512,512]{1,0:T(8,128)} %collective-permute-done.refs_2_), channel_id=1, source_target_pairs={{0,2},{1,7},{2,4},{3,1},{4,6},{5,3},{6,0},{7,5},{8,10},{9,15},{10,... | collective-permute-start | bytes 3145736 | tf_op jit(solution)/shard_map/ppermute | solution.py:296
  59.2 39.1 %collective-permute-start.8 = (f32[512,512]{1,0:T(8,128)}, f32[512,512]{1,0:T(8,128)}, u32[]{:S(2)}, u32[]{:S(2)}) collective-permute-start(f32[512,512]{1,0:T(8,128)} %collective-permute-done.6.refs_10_), channel_id=1, source_target_pairs={{0,2},{1,7},{2,4},{3,1},{4,6},{5,3},{6,0},{7,5},{8,10},{9,15},{10,... | collective-permute-start | bytes 3145736 | tf_op jit(solution)/shard_map/ppermute | solution.py:296
  60.7 16.9 %collective-permute-start.12 = (f32[256,512]{1,0:T(8,128)}, f32[256,512]{1,0:T(8,128)}, u32[]{:S(2)}, u32[]{:S(2)}) collective-permute-start(f32[256,512]{1,0:T(8,128)} %collective-permute-done.2.refs_5_), channel_id=1, source_target_pairs={{0,8},{8,0},{1,9},{9,1},{2,10},{10,2},{3,11},{11,3},{4,12},{12,4},... | collective-permute-start | bytes 1572872 | tf_op jit(solution)/shard_map/ppermute | solution.py:300
  67.7 30.6 %collective-permute-start.13 = (f32[256,512]{1,0:T(8,128)S(1)}, f32[256,512]{1,0:T(8,128)}, u32[]{:S(2)}, u32[]{:S(2)}) collective-permute-start(f32[256,512]{1,0:T(8,128)S(1)} %collective-permute-done.11.refs_11_), channel_id=1, source_target_pairs={{0,2},{1,7},{2,4},{3,1},{4,6},{5,3},{6,0},{7,5},{8,10},{9,15},{10,... | collective-permute-start | bytes 1572872 | tf_op jit(solution)/shard_map/ppermute | solution.py:296
  98.3 122.8 %all-to-all-start = ((f32[16,512,256]{2,1,0:T(8,128)}), f32[16,512,256]{2,1,0:T(8,128)}, u32[]{:S(2)}, u32[]{:S(2)}) async-start(f32[16,512,256]{2,1,0:T(8,128)} %bitcast.34), calls=%async_computation | async-start | bytes 16777216 | tf_op jit(solution)/shard_map/all_to_all | solution.py:346
  107.5 4.9 %collective-permute-start.14 = (f32[512,512]{1,0:T(8,128)S(1)}, f32[512,512]{1,0:T(8,128)S(1)}, u32[]{:S(2)}, u32[]{:S(2)}) collective-permute-start(f32[512,512]{1,0:T(8,128)S(1)} %pad_maximum_fusion.refs_0_), channel_id=1, source_target_pairs={{0,1},{1,0},{2,3},{3,2},{4,5},{5,4},{6,7},{7,6},{8,9},{9,8},{10,11... | collective-permute-start | bytes 3145736 | tf_op jit(solution)/shard_map/ppermute | solution.py:300
  107.7 4.3 %collective-permute-start.15 = (f32[256,512]{1,0:T(8,128)S(1)}, f32[256,512]{1,0:T(8,128)S(1)}, u32[]{:S(2)}, u32[]{:S(2)}) collective-permute-start(f32[256,512]{1,0:T(8,128)S(1)} %get-tuple-element.29.refs_1_), channel_id=1, source_target_pairs={{0,1},{1,0},{2,3},{3,2},{4,5},{5,4},{6,7},{7,6},{8,9},{9,8},{10,11... | collective-permute-start | bytes 1572872 | tf_op jit(solution)/shard_map/ppermute | solution.py:300
  108.1 5.4 %collective-permute-start.17 = (f32[256,512]{1,0:T(8,128)S(1)}, f32[256,512]{1,0:T(8,128)S(1)}, u32[]{:S(2)}, u32[]{:S(2)}) collective-permute-start(f32[256,512]{1,0:T(8,128)S(1)} %collective-permute-done.1.refs_3_), channel_id=1, source_target_pairs={{0,1},{1,0},{2,3},{3,2},{4,5},{5,4},{6,7},{7,6},{8,9},{9,8},{10,11... | collective-permute-start | bytes 1572872 | tf_op jit(solution)/shard_map/ppermute | solution.py:300
  108.2 5.7 %collective-permute-start.19 = (f32[256,512]{1,0:T(8,128)}, f32[256,512]{1,0:T(8,128)S(1)}, u32[]{:S(2)}, u32[]{:S(2)}) collective-permute-start(f32[256,512]{1,0:T(8,128)} %collective-permute-done.2.refs_5_), channel_id=1, source_target_pairs={{0,1},{1,0},{2,3},{3,2},{4,5},{5,4},{6,7},{7,6},{8,9},{9,8},{10,11... | collective-permute-start | bytes 1572872 | tf_op jit(solution)/shard_map/ppermute | solution.py:300
  108.6 5.5 %collective-permute-start.21 = (f32[256,512]{1,0:T(8,128)}, f32[256,512]{1,0:T(8,128)S(1)}, u32[]{:S(2)}, u32[]{:S(2)}) collective-permute-start(f32[256,512]{1,0:T(8,128)} %copy-done.9), channel_id=1, source_target_pairs={{0,1},{1,0},{2,3},{3,2},{4,5},{5,4},{6,7},{7,6},{8,9},{9,8},{10,11... | collective-permute-start | bytes 1572872 | tf_op jit(solution)/shard_map/ppermute | solution.py:300
  112.4 8.5 %collective-permute-start.16 = (f32[512,512]{1,0:T(8,128)}, f32[512,512]{1,0:T(8,128)S(1)}, u32[]{:S(2)}, u32[]{:S(2)}) collective-permute-start(f32[512,512]{1,0:T(8,128)} %collective-permute-done.refs_2_), channel_id=1, source_target_pairs={{0,1},{1,0},{2,3},{3,2},{4,5},{5,4},{6,7},{7,6},{8,9},{9,8},{10,11... | collective-permute-start | bytes 3145736 | tf_op jit(solution)/shard_map/ppermute | solution.py:300
  113.5 7.5 %collective-permute-start.18 = (f32[512,512]{1,0:T(8,128)S(1)}, f32[512,512]{1,0:T(8,128)S(1)}, u32[]{:S(2)}, u32[]{:S(2)}) collective-permute-start(f32[512,512]{1,0:T(8,128)S(1)} %collective-permute-done.4.refs_4_), channel_id=1, source_target_pairs={{0,1},{1,0},{2,3},{3,2},{4,5},{5,4},{6,7},{7,6},{8,9},{9,8},{10,11... | collective-permute-start | bytes 3145736 | tf_op jit(solution)/shard_map/ppermute | solution.py:300
  114.1 4.9 %collective-permute-start.27 = (f32[256,512]{1,0:T(8,128)}, f32[256,512]{1,0:T(8,128)S(1)}, u32[]{:S(2)}, u32[]{:S(2)}) collective-permute-start(f32[256,512]{1,0:T(8,128)} %collective-permute-done.12.refs_13_), channel_id=1, source_target_pairs={{0,1},{1,0},{2,3},{3,2},{4,5},{5,4},{6,7},{7,6},{8,9},{9,8},{10,11... | collective-permute-start | bytes 1572872 | tf_op jit(solution)/shard_map/ppermute | solution.py:300
  114.5 6.0 %collective-permute-start.29 = (f32[256,512]{1,0:T(8,128)}, f32[256,512]{1,0:T(8,128)S(1)}, u32[]{:S(2)}, u32[]{:S(2)}) collective-permute-start(f32[256,512]{1,0:T(8,128)} %collective-permute-done.13.refs_15_), channel_id=1, source_target_pairs={{0,1},{1,0},{2,3},{3,2},{4,5},{5,4},{6,7},{7,6},{8,9},{9,8},{10,11... | collective-permute-start | bytes 1572872 | tf_op jit(solution)/shard_map/ppermute | solution.py:300
  120.5 5.4 %collective-permute-start.24 = (f32[512,512]{1,0:T(8,128)}, f32[512,512]{1,0:T(8,128)}, u32[]{:S(2)}, u32[]{:S(2)}) collective-permute-start(f32[512,512]{1,0:T(8,128)} %collective-permute-done.6.refs_10_), channel_id=1, source_target_pairs={{0,1},{1,0},{2,3},{3,2},{4,5},{5,4},{6,7},{7,6},{8,9},{9,8},{10,11... | collective-permute-start | bytes 3145736 | tf_op jit(solution)/shard_map/ppermute | solution.py:300
  120.8 6.5 %collective-permute-start.26 = (f32[512,512]{1,0:T(8,128)}, f32[512,512]{1,0:T(8,128)}, u32[]{:S(2)}, u32[]{:S(2)}) collective-permute-start(f32[512,512]{1,0:T(8,128)} %collective-permute-done.7.refs_12_), channel_id=1, source_target_pairs={{0,1},{1,0},{2,3},{3,2},{4,5},{5,4},{6,7},{7,6},{8,9},{9,8},{10,11... | collective-permute-start | bytes 3145736 | tf_op jit(solution)/shard_map/ppermute | solution.py:300
  121.0 6.4 %collective-permute-start.28 = (f32[512,512]{1,0:T(8,128)}, f32[512,512]{1,0:T(8,128)S(1)}, u32[]{:S(2)}, u32[]{:S(2)}) collective-permute-start(f32[512,512]{1,0:T(8,128)} %collective-permute-done.8.refs_14_), channel_id=1, source_target_pairs={{0,1},{1,0},{2,3},{3,2},{4,5},{5,4},{6,7},{7,6},{8,9},{9,8},{10,11... | collective-permute-start | bytes 3145736 | tf_op jit(solution)/shard_map/ppermute | solution.py:300
  144.6 20.3 %collective-permute-start.30 = (f32[3,256,256]{2,1,0:T(8,128)}, f32[3,256,256]{2,1,0:T(8,128)S(1)}, u32[]{:S(2)}, u32[]{:S(2)}) collective-permute-start(f32[3,256,256]{2,1,0:T(8,128)} %shard_map.38), channel_id=1, source_target_pairs={{0,16},{16,0},{32,48},{48,32},{1,17},{17,1},{33,49},{49,33},{2,18}... | collective-permute-start | bytes 2359304 | tf_op jit(solution)/shard_map/ppermute | solution.py:353
  166.1 21.3 %collective-permute-start.31 = (f32[3,256,256]{2,1,0:T(8,128)S(1)}, f32[3,256,256]{2,1,0:T(8,128)S(1)}, u32[]{:S(2)}, u32[]{:S(2)}) collective-permute-start(f32[3,256,256]{2,1,0:T(8,128)S(1)} %add.226), channel_id=1, source_target_pairs={{0,32},{16,48},{32,0},{48,16},{1,33},{17,49},{33,1},{49,17},{2,34}... | collective-permute-start | bytes 2359304 | tf_op jit(solution)/shard_map/ppermute | solution.py:353
  187.6 55.8 %collective-permute-start.32 = (f32[3,256,256]{2,1,0:T(8,128)S(1)}, f32[3,256,256]{2,1,0:T(8,128)S(1)}, u32[]{:S(2)}, u32[]{:S(2)}) collective-permute-start(f32[3,256,256]{2,1,0:T(8,128)S(1)} %add.227), channel_id=1, source_target_pairs={{0,64},{64,0},{1,65},{65,1},{2,66},{66,2},{3,67},{67,3},{4,68},{68... | collective-permute-start | bytes 2359304 | tf_op jit(solution)/shard_map/ppermute | solution.py:300
  238.0 17.5 %all-to-all-start.1 = ((f32[8,96,256]{2,1,0:T(8,128)}), f32[8,96,256]{2,1,0:T(8,128)S(1)}, u32[]{:S(2)}, u32[]{:S(2)}) async-start(f32[8,96,256]{2,1,0:T(8,128)} %bitcast.36), calls=%async_computation.1 | async-start | bytes 1572864 | tf_op jit(solution)/shard_map/all_to_all | solution.py:275
  256.5 15.8 %all-to-all-start.2 = ((f32[8,96,256]{2,1,0:T(8,128)}), f32[8,96,256]{2,1,0:T(8,128)S(1)}, u32[]{:S(2)}, u32[]{:S(2)}) async-start(f32[8,96,256]{2,1,0:T(8,128)} %broadcast_in_dim.19), calls=%async_computation.2 | async-start | bytes 1572864 | tf_op jit(solution)/shard_map/all_to_all | solution.py:282
  (24 other events, 521.4 us)

commit v5 on v4

--- a/solution.py
+++ b/solution.py
@@ -29,16 +29,21 @@
     return dot(left_high, right_high) + (dot(left_high, right_low) + dot(left_low, right_high))
 
 
-AHEAD = 3
+SLOTS = 4
 LIMIT = pltpu.CompilerParams(vmem_limit_bytes=60 * 2**20)
 
 
-def fetch(parts, buffer, sem):
-    start = 0
-    for part in parts:
-        rows = part.shape[0]
-        pltpu.make_async_copy(part, buffer.at[pl.ds(start, rows)], sem).start()
-        start += rows
+def fetch_pieces(pieces, k, v_buf, v_sems):
+    for i, parts in enumerate(pieces):
+
+        @pl.when(k == i)
+        def _(parts=parts, i=i):
+            start = 0
+            for part in parts:
+                rows = part.shape[0]
+                target = v_buf.at[i % SLOTS, pl.ds(start, rows)]
+                pltpu.make_async_copy(part, target, v_sems.at[i % SLOTS]).start()
+                start += rows
 
 
 def arrive(buffer, sem):
@@ -47,6 +52,12 @@
 
 def block_rows(ref, places, k, depth):
     return ref.at[pl.ds(pl.multiple_of(places[k] * depth, depth), depth)]
+
+
+def fetch_block(places, k, e_ref, e_buf, e_sems, v_ref, v_buf, v_sems):
+    slot = lax.rem(k, SLOTS)
+    pltpu.make_async_copy(v_ref.at[k], v_buf.at[slot], v_sems.at[slot]).start()
+    pltpu.make_async_copy(block_rows(e_ref, places, k, e_buf.shape[1]), e_buf.at[slot], e_sems.at[slot]).start()
 
 
 def grouped(flat, blocks):
@@ -54,85 +65,101 @@
     return [flat[k * size : (k + 1) * size] for k in range(blocks)]
 
 
-def fetch_block(pieces, places, k, e_ref, e_buf, e_sems, v_buf, v_sems):
-    pltpu.make_async_copy(block_rows(e_ref, places, k, e_buf.shape[1]), e_buf.at[k], e_sems.at[k]).start()
-    fetch_pieces(pieces, k, v_buf, v_sems)
-
-
-def fetch_pieces(pieces, k, v_buf, v_sems):
-    for i, parts in enumerate(pieces):
-        if isinstance(k, int):
-            if k == i:
-                fetch(parts, v_buf.at[i], v_sems.at[i])
-        else:
-
-            @pl.when(k == i)
-            def _(parts=parts, i=i):
-                fetch(parts, v_buf.at[i], v_sems.at[i])
+def dot(left, right, dims):
+    return lax.dot_general(left, right, (dims, ((), ())), preferred_element_type=jnp.float32)
+
+
+def split_triple(left, right, dims):
+    return dot(left[0], right[0], dims) + (dot(left[0], right[1], dims) + dot(left[1], right[0], dims))
 
 
 def gram_kernel(blocks, size, *refs):
-    flat, (g_ref, v_buf, v_sems) = refs[:-3], refs[-3:]
+    flat, (g_ref, halves_ref, v_buf, h_buf, v_sems, h_sems) = refs[:-6], refs[-6:]
     pieces = grouped(flat, blocks)
-    for k in range(AHEAD):
+
+    def leave(k):
+        slot = lax.rem(k, SLOTS)
+        return pltpu.make_async_copy(h_buf.at[slot], halves_ref.at[k], h_sems.at[slot])
+
+    for k in range(SLOTS - 1):
         fetch_pieces(pieces, k, v_buf, v_sems)
     g_ref[...] = jnp.zeros_like(g_ref)
 
     @pl.loop(0, blocks)
     def _(k):
-        @pl.when(k + AHEAD < blocks)
-        def _():
-            fetch_pieces(pieces, k + AHEAD, v_buf, v_sems)
-
-        arrive(v_buf.at[k], v_sems.at[k])
-        first, second, third = (v_buf[k, pl.ds(j * size, size)] for j in range(3))
+        @pl.when(k + SLOTS - 1 < blocks)
+        def _():
+            fetch_pieces(pieces, k + SLOTS - 1, v_buf, v_sems)
+
+        slot = lax.rem(k, SLOTS)
+        arrive(v_buf.at[slot], v_sems.at[slot])
+
+        @pl.when(k >= SLOTS)
+        def _():
+            leave(k - SLOTS).wait()
+
+        h_buf[slot, 0], h_buf[slot, 1] = halves(v_buf[slot])
+        leave(k).start()
+        first, second, third = (
+            (h_buf[slot, 0, pl.ds(j * size, size)], h_buf[slot, 1, pl.ds(j * size, size)]) for j in range(3)
+        )
         across = ((1,), (1,))
-        g_ref[0] += triple(first, second, across)
-        g_ref[1] += triple(first, third, across)
-        g_ref[2] += triple(second, third, across)
-
-
-def project_kernel(blocks, places, e_ref, *refs):
-    flat, (w_ref, e_buf, v_buf, e_sems, v_sems) = refs[:-5], refs[-5:]
-    pieces = grouped(flat, blocks)
-    for k in range(AHEAD):
-        fetch_block(pieces, places, k, e_ref, e_buf, e_sems, v_buf, v_sems)
+        g_ref[0] += split_triple(first, second, across)
+        g_ref[1] += split_triple(first, third, across)
+        g_ref[2] += split_triple(second, third, across)
+
+    @pl.loop(blocks - SLOTS, blocks)
+    def _(k):
+        leave(k).wait()
+
+
+def project_kernel(places, e_ref, v_ref, w_ref, e_buf, v_buf, e_sems, v_sems):
+    blocks = v_ref.shape[0]
+    for k in range(SLOTS - 1):
+        fetch_block(places, k, e_ref, e_buf, e_sems, v_ref, v_buf, v_sems)
     w_ref[...] = jnp.zeros_like(w_ref)
 
     @pl.loop(0, blocks)
     def _(k):
-        @pl.when(k + AHEAD < blocks)
-        def _():
-            fetch_block(pieces, places, k + AHEAD, e_ref, e_buf, e_sems, v_buf, v_sems)
-
-        arrive(e_buf.at[k], e_sems.at[k])
-        arrive(v_buf.at[k], v_sems.at[k])
-        w_ref[...] += triple(v_buf[k], e_buf[k], ((1,), (0,)))
-
-
-def apply_kernel(blocks, places, e_ref, m_ref, w_ref, *refs):
-    flat, (o_ref, e_buf, v_buf, y_ref, e_sems, v_sems, o_sems) = refs[:-7], refs[-7:]
+        @pl.when(k + SLOTS - 1 < blocks)
+        def _():
+            fetch_block(places, k + SLOTS - 1, e_ref, e_buf, e_sems, v_ref, v_buf, v_sems)
+
+        slot = lax.rem(k, SLOTS)
+        arrive(e_buf.at[slot], e_sems.at[slot])
+        arrive(v_buf.at[slot], v_sems.at[slot])
+        w_ref[...] += split_triple((v_buf[slot, 0], v_buf[slot, 1]), halves(e_buf[slot]), ((1,), (0,)))
+
+
+def apply_kernel(places, e_ref, m_ref, w_ref, v_ref, o_ref, e_buf, v_buf, o_buf, y_ref, e_sems, v_sems, o_sems):
+    blocks = v_ref.shape[0]
     depth = e_buf.shape[1]
-    pieces = grouped(flat, blocks)
-    for k in range(AHEAD):
-        fetch_block(pieces, places, k, e_ref, e_buf, e_sems, v_buf, v_sems)
-    y_ref[...] = triple(m_ref[...], w_ref[...], ((1,), (0,)))
+    for k in range(SLOTS - 1):
+        fetch_block(places, k, e_ref, e_buf, e_sems, v_ref, v_buf, v_sems)
+    y_ref[0], y_ref[1] = halves(triple(m_ref[...], w_ref[...], ((1,), (0,))))
 
     def leave(k):
-        return pltpu.make_async_copy(e_buf.at[k], block_rows(o_ref, places, k, depth), o_sems.at[k])
+        slot = lax.rem(k, SLOTS)
+        return pltpu.make_async_copy(o_buf.at[slot], block_rows(o_ref, places, k, depth), o_sems.at[slot])
 
     @pl.loop(0, blocks)
     def _(k):
-        @pl.when(k + AHEAD < blocks)
-        def _():
-            fetch_block(pieces, places, k + AHEAD, e_ref, e_buf, e_sems, v_buf, v_sems)
-
-        arrive(e_buf.at[k], e_sems.at[k])
-        arrive(v_buf.at[k], v_sems.at[k])
-        e_buf[k] = e_buf[k] - triple(v_buf[k], y_ref[...], ((0,), (0,)))
+        @pl.when(k + SLOTS - 1 < blocks)
+        def _():
+            fetch_block(places, k + SLOTS - 1, e_ref, e_buf, e_sems, v_ref, v_buf, v_sems)
+
+        slot = lax.rem(k, SLOTS)
+        arrive(e_buf.at[slot], e_sems.at[slot])
+        arrive(v_buf.at[slot], v_sems.at[slot])
+
+        @pl.when(k >= SLOTS)
+        def _():
+            leave(k - SLOTS).wait()
+
+        o_buf[slot] = e_buf[slot] - split_triple((v_buf[slot, 0], v_buf[slot, 1]), (y_ref[0], y_ref[1]), ((0,), (0,)))
         leave(k).start()
 
-    @pl.loop(0, blocks)
+    @pl.loop(blocks - SLOTS, blocks)
     def _(k):
         leave(k).wait()
 
@@ -145,69 +172,72 @@
 def cost(blocks, count, depth, width, passes):
     return pl.CostEstimate(
         flops=6 * blocks * count * depth * width,
-        bytes_accessed=4 * blocks * depth * (count + passes * width),
+        bytes_accessed=4 * blocks * depth * passes * width,
         transcendentals=0,
     )
 
 
-def sizes_of(pieces):
-    return len(pieces), sum(part.shape[0] for part in pieces[0]), pieces[0][0].shape[1]
-
-
 def gram_of(pieces, size):
-    blocks, count, depth = sizes_of(pieces)
+    blocks, count, depth = len(pieces), sum(part.shape[0] for part in pieces[0]), pieces[0][0].shape[1]
     flat = [part for parts in pieces for part in parts]
     return pl.pallas_call(
         functools.partial(gram_kernel, blocks, size),
         in_specs=[FAR] * len(flat),
-        out_specs=NEAR,
-        out_shape=jax.ShapeDtypeStruct((3, size, size), jnp.float32),
-        scratch_shapes=[pltpu.VMEM((blocks, count, depth), jnp.float32), pltpu.SemaphoreType.DMA((blocks,))],
-        compiler_params=LIMIT,
-        cost_estimate=cost(blocks, count, depth, size, 0),
+        out_specs=[NEAR, FAR],
+        out_shape=[
+            jax.ShapeDtypeStruct((3, size, size), jnp.float32),
+            jax.ShapeDtypeStruct((blocks, 2, count, depth), jnp.bfloat16),
+        ],
+        scratch_shapes=[
+            pltpu.VMEM((SLOTS, count, depth), jnp.float32),
+            pltpu.VMEM((SLOTS, 2, count, depth), jnp.bfloat16),
+            pltpu.SemaphoreType.DMA((SLOTS,)),
+            pltpu.SemaphoreType.DMA((SLOTS,)),
+        ],
+        compiler_params=LIMIT,
+        cost_estimate=cost(blocks, count, depth, size, 3),
     )(*flat)
 
 
-def project(places, block, pieces):
-    blocks, count, depth = sizes_of(pieces)
+def project(places, block, vectors):
+    blocks, _, count, depth = vectors.shape
     width = block.shape[1]
-    flat = [part for parts in pieces for part in parts]
-    return pl.pallas_call(
-        functools.partial(project_kernel, blocks),
-        in_specs=[SCALARS, FAR] + [FAR] * len(flat),
+    return pl.pallas_call(
+        project_kernel,
+        in_specs=[SCALARS, FAR, FAR],
         out_specs=NEAR,
         out_shape=jax.ShapeDtypeStruct((count, width), jnp.float32),
         scratch_shapes=[
-            pltpu.VMEM((blocks, depth, width), jnp.float32),
-            pltpu.VMEM((blocks, count, depth), jnp.float32),
-            pltpu.SemaphoreType.DMA((blocks,)),
-            pltpu.SemaphoreType.DMA((blocks,)),
+            pltpu.VMEM((SLOTS, depth, width), jnp.float32),
+            pltpu.VMEM((SLOTS, 2, count, depth), jnp.bfloat16),
+            pltpu.SemaphoreType.DMA((SLOTS,)),
+            pltpu.SemaphoreType.DMA((SLOTS,)),
         ],
         compiler_params=LIMIT,
         cost_estimate=cost(blocks, count, depth, width, 1),
-    )(places, block, *flat)
-
-
-def apply(places, block, mixer, w, pieces):
-    blocks, count, depth = sizes_of(pieces)
+    )(places, block, vectors)
+
+
+def apply(places, block, mixer, w, vectors):
+    blocks, _, count, depth = vectors.shape
     width = block.shape[1]
-    flat = [part for parts in pieces for part in parts]
-    return pl.pallas_call(
-        functools.partial(apply_kernel, blocks),
-        in_specs=[SCALARS, FAR, NEAR, NEAR] + [FAR] * len(flat),
+    return pl.pallas_call(
+        apply_kernel,
+        in_specs=[SCALARS, FAR, NEAR, NEAR, FAR],
         out_specs=FAR,
         out_shape=jax.ShapeDtypeStruct(block.shape, jnp.float32),
         scratch_shapes=[
-            pltpu.VMEM((blocks, depth, width), jnp.float32),
-            pltpu.VMEM((blocks, count, depth), jnp.float32),
-            pltpu.VMEM((count, width), jnp.float32),
-            pltpu.SemaphoreType.DMA((blocks,)),
-            pltpu.SemaphoreType.DMA((blocks,)),
-            pltpu.SemaphoreType.DMA((blocks,)),
+            pltpu.VMEM((SLOTS, depth, width), jnp.float32),
+            pltpu.VMEM((SLOTS, 2, count, depth), jnp.bfloat16),
+            pltpu.VMEM((SLOTS, depth, width), jnp.float32),
+            pltpu.VMEM((2, count, width), jnp.bfloat16),
+            pltpu.SemaphoreType.DMA((SLOTS,)),
+            pltpu.SemaphoreType.DMA((SLOTS,)),
+            pltpu.SemaphoreType.DMA((SLOTS,)),
         ],
         compiler_params=LIMIT,
         cost_estimate=cost(blocks, count, depth, width, 2),
-    )(places, block, mixer, w, *flat)
+    )(places, block, mixer, w, vectors)
 
 
 def mix_kernel(t_ref, g_ref, m_ref):
@@ -331,13 +361,14 @@
     wide = jnp.concatenate(shaped[:2], axis=0)
     slim = shaped[2]
     wide_there = swap(wide, "yhi")
+    slim_near, slim_other = send(slim, 1), send(slim, -1)
     wide_near, wide_other = send(wide, 1), send(wide, -1)
-    slim_near, slim_other = send(slim, 1), send(slim, -1)
+    slim_far = send(slim_near, 1)
     early, (wide_there, wide_other) = after((slim, slim_near, slim_other), wide_there, wide_other)
+    (wide_there,), (slim_far,) = after((wide_there,), slim_far)
     there_near, there_other = send(wide_there, 1), send(wide_there, -1)
-    slim_held = [slim, slim_near, slim_other, send(slim_near, 1)]
-    slim_held += [swap(part, "yhi") for part in early]
-    slim_held.append(send(slim_held[5], 1))
+    slim_held = [slim, slim_near, slim_other, slim_far]
+    slim_held += [swap(part, "yhi") for part in (*early, slim_far)]
     wide_held = [wide, wide_near, wide_other, send(wide_near, 1), wide_there, there_near, there_other]
     wide_held.append(send(there_near, 1))
     block = columns_apart(eigvecs, lax.axis_size(COL))
@@ -347,15 +378,15 @@
     pieces = list(zip(wide_held, slim_held))
     pieces += [tuple(swap(part, "core") for part in parts) for parts in pieces]
 
-    gram = gram_of(pieces, block_size)
+    gram, vectors = gram_of(pieces, block_size)
     size = lax.axis_size("z")
     for step in (1, 2):
         gram = gram + lax.ppermute(gram, "z", [(i, i ^ step) for i in range(size)])
     other = swap(gram, "ylo")
-    parts = scattered(project(places, block, pieces), ROW)
+    parts = scattered(project(places, block, vectors), ROW)
     (other,), (parts,) = after((other,), parts)
     mixer = mix(tri_factors, gram + other)
-    return apply(places, block, mixer, collected(parts, ROW), pieces)
+    return apply(places, block, mixer, collected(parts, ROW), vectors)
 
 
 def solution(mesh):

time: 293 us -> 285 us (0.973)
  starting transfers between devices: 62.6 us -> 54.1 us
    ppermute x21 -> x22, waiting for transfers between devices: 15.2 us -> 30.7 us  [swap(): return lax.ppermute(piece, axis, [(0, 1), (1, 0)])]
    ppermute x10 -> x9, waiting for transfers between devices: 56.8 us -> 44.7 us  [send(): return lax.ppermute(piece, ('x', 'core'), turn(sign))]
    ppermute x10 -> x9, starting transfers between devices: 16.6 us -> 11.9 us  [send(): return lax.ppermute(piece, ('x', 'core'), turn(sign))]
    all_to_all x1, waiting for transfers between devices: 32.8 us -> 29.3 us  [on_device(): block = lax.all_to_all(block, COL, split_axis=0, concat_axis=0, tiled=True)]
    ppermute x21 -> x22, starting transfers between devices: 21.8 us -> 19.4 us  [swap(): return lax.ppermute(piece, axis, [(0, 1), (1, 0)])]
  transfers between devices with their start and end apart: 36 -> 36, of which waited for: 17 -> 20; matrix products, arithmetic and copies ran while one was open for 1% -> 1% of each run, Pallas kernels for 15% -> 16%
where the time goes in v5:
time: 285 us
  waiting for transfers between devices  159 us (56%)
  Pallas kernels  63.1 us (22%)
  starting transfers between devices  54.1 us (19%)
  local copies, waits for them, and re-layouts  4.36 us (2%)
  other arithmetic  4.09 us (1%)
    ppermute x9, waiting for transfers between devices, send(): return lax.ppermute(piece, ('x', 'core'), turn(sign))  44.7 us
    ppermute x2, waiting for transfers between devices, on_device(): gram = gram + lax.ppermute(gram, 'z', [(i, i ^ step) for i in range(size)])  35 us
    ppermute x22, waiting for transfers between devices, swap(): return lax.ppermute(piece, axis, [(0, 1), (1, 0)])  30.7 us
    all_to_all x1, waiting for transfers between devices, on_device(): block = lax.all_to_all(block, COL, split_axis=0, concat_axis=0, tiled=True)  29.3 us
    ppermute x22, starting transfers between devices, swap(): return lax.ppermute(piece, axis, [(0, 1), (1, 0)])  19.4 us
    pallas_call x1, Pallas kernels, gram_of(): pl.pallas_call(functools.partial(gram_kernel, blocks, size), in_specs=[FA...  18.8 us
    pallas_call x1, Pallas kernels, apply(): pl.pallas_call(apply_kernel, in_specs=[SCALARS, FAR, NEAR, NEAR, FAR], ou...  17.7 us
    pallas_call x1, Pallas kernels, project(): pl.pallas_call(project_kernel, in_specs=[SCALARS, FAR, FAR], out_specs=NE...  15.8 us
  transfers between devices with their start and end apart: 36, of which 20 were waited for; matrix products, arithmetic and copies ran while one was open for 1% of the time, Pallas kernels for 16%

profile of v5, /device:TPU:2, one launch (start us, length us, event | category | flops | bytes accessed | tf_op | source)
XLA Modules:
  0.0 285.0 jit_solution(10288531705781788397)
XLA Ops:
  0.0 1.7 fusion
  2.3 3.3 %collective-permute-start.3 = (f32[512,512]{1,0:T(8,128)S(1)}, f32[512,512]{1,0:T(8,128)}, u32[]{:S(2)}, u32[]{:S(2)}) collective-permute-start(f32[512,512]{1,0:T(8,128)S(1)} %pad_maximum_fusion.refs_0_), channel_id=1, source_target_pairs={{0,8},{8,0},{1,9},{9,1},{2,10},{10,2},{3,11},{11,3},{4,12},{12,4},... | collective-permute-start | bytes 3145736 | tf_op jit(solution)/shard_map/ppermute | solution.py:330
  8.3 12.8 %collective-permute-done.1.refs_3_ = f32[256,512]{1,0:T(8,128)S(1)} collective-permute-done((f32[256,512]{1,0:T(8,128)S(1)}, f32[256,512]{1,0:T(8,128)S(1)}, u32[]{:S(2)}, u32[]{:S(2)}) %collective-permute-start.1) | collective-permute-done | bytes 524320 | tf_op jit(solution)/shard_map/ppermute | solution.py:326
  23.4 9.8 %collective-permute-done.2.refs_5_ = f32[256,512]{1,0:T(8,128)S(1)} collective-permute-done((f32[256,512]{1,0:T(8,128)S(1)}, f32[256,512]{1,0:T(8,128)S(1)}, u32[]{:S(2)}, u32[]{:S(2)}) %collective-permute-start.2) | collective-permute-done | bytes 524320 | tf_op jit(solution)/shard_map/ppermute | solution.py:326
  33.2 1.9 collective-permute-start.7
  35.0 6.0 %collective-permute-start.13 = (f32[256,512]{1,0:T(8,128)S(1)}, f32[256,512]{1,0:T(8,128)S(1)}, u32[]{:S(2)}, u32[]{:S(2)}) collective-permute-start(f32[256,512]{1,0:T(8,128)S(1)} %collective-permute-done.6.refs_7_), channel_id=1, source_target_pairs={{0,8},{8,0},{1,9},{9,1},{2,10},{10,2},{3,11},{11,3},{4,12},{12,4},... | collective-permute-start | bytes 1572872 | tf_op jit(solution)/shard_map/ppermute | solution.py:330
  41.4 4.9 %collective-permute-done.refs_2_ = f32[512,512]{1,0:T(8,128)} collective-permute-done((f32[512,512]{1,0:T(8,128)S(1)}, f32[512,512]{1,0:T(8,128)}, u32[]{:S(2)}, u32[]{:S(2)}) %collective-permute-start) | collective-permute-done | bytes 1048608 | tf_op jit(solution)/shard_map/ppermute | solution.py:326
  46.4 2.6 collective-permute-start.5
  49.0 17.2 %collective-permute-done.7.refs_10_ = f32[512,512]{1,0:T(8,128)} collective-permute-done((f32[512,512]{1,0:T(8,128)}, f32[512,512]{1,0:T(8,128)}, u32[]{:S(2)}, u32[]{:S(2)}) %collective-permute-start.7) | collective-permute-done | bytes 1048608 | tf_op jit(solution)/shard_map/ppermute | solution.py:326
  67.7 3.2 %collective-permute-start.11 = (f32[256,512]{1,0:T(8,128)S(1)}, f32[256,512]{1,0:T(8,128)}, u32[]{:S(2)}, u32[]{:S(2)}) collective-permute-start(f32[256,512]{1,0:T(8,128)S(1)} %collective-permute-done.1.refs_3_), channel_id=1, source_target_pairs={{0,8},{8,0},{1,9},{9,1},{2,10},{10,2},{3,11},{11,3},{4,12},{12,4},... | collective-permute-start | bytes 1572872 | tf_op jit(solution)/shard_map/ppermute | solution.py:330
  72.4 6.7 %shard_map.37 = f32[8192,256]{1,0:T(8,128)} custom-call(f32[512,4096]{1,0:T(8,128)} %e_ref.1), custom_call_target="tpu_custom_call" | custom-call | bytes 16777216 | tf_op jit(solution)/shard_map/pallas_call | solution.py:289
  79.1 4.9 %collective-permute-done.11.refs_11_ = f32[256,512]{1,0:T(8,128)} collective-permute-done((f32[256,512]{1,0:T(8,128)S(1)}, f32[256,512]{1,0:T(8,128)}, u32[]{:S(2)}, u32[]{:S(2)}) %collective-permute-start.11) | collective-permute-done | bytes 524320 | tf_op jit(solution)/shard_map/ppermute | solution.py:330
  84.0 10.6 %collective-permute-done.12.refs_13_ = f32[256,512]{1,0:T(8,128)} collective-permute-done((f32[256,512]{1,0:T(8,128)S(1)}, f32[256,512]{1,0:T(8,128)}, u32[]{:S(2)}, u32[]{:S(2)}) %collective-permute-start.12) | collective-permute-done | bytes 524320 | tf_op jit(solution)/shard_map/ppermute | solution.py:330
  94.6 6.8 %all-to-all-start = ((f32[16,512,256]{2,1,0:T(8,128)}), f32[16,512,256]{2,1,0:T(8,128)}, u32[]{:S(2)}, u32[]{:S(2)}) async-start(f32[16,512,256]{2,1,0:T(8,128)} %bitcast.34), calls=%async_computation | async-start | bytes 16777216 | tf_op jit(solution)/shard_map/all_to_all | solution.py:377
  102.7 3.3 %collective-permute-done.15.refs_17_ = f32[256,512]{1,0:T(8,128)S(1)} collective-permute-done((f32[256,512]{1,0:T(8,128)S(1)}, f32[256,512]{1,0:T(8,128)S(1)}, u32[]{:S(2)}, u32[]{:S(2)}) %collective-permute-start.15) | collective-permute-done | bytes 524320 | tf_op jit(solution)/shard_map/ppermute | solution.py:330
  108.8 2.6 collective-permute-done.25.refs_27_
  116.8 3.0 %collective-permute-done.24.refs_26_ = f32[512,512]{1,0:T(8,128)} collective-permute-done((f32[512,512]{1,0:T(8,128)}, f32[512,512]{1,0:T(8,128)}, u32[]{:S(2)}, u32[]{:S(2)}) %collective-permute-start.24) | collective-permute-done | bytes 1048608 | tf_op jit(solution)/shard_map/ppermute | solution.py:330
  119.8 1.5 collective-permute-done.26.refs_28_
  122.4 18.8 %shard_map.38 = (f32[3,256,256]{2,1,0:T(8,128)}, bf16[16,2,768,512]{3,2,1,0:T(8,128)(2,1)}) custom-call(f32[512,512]{1,0:T(8,128)} %copy-done.1, f32[256,512]{1,0:T(8,128)} %copy-done.2, f32[512,512]{1,0:T(8,128)} %collective-permute-done.refs_2_, f32[256,512]{1,0:T(8,128)} %copy-done.8, f32[512,512]{1,0:T(8,128)} %copy-done.3, f32[256,512]{1,0:T(8,128)} %copy-done.9, ...), custom_call_target="tpu_custom_call" | custom-call | flops 9663676416 | bytes 25165824 | tf_op jit(solution)/shard_map/pallas_call | solution.py:183
  141.1 2.1 collective-permute-start.30
  143.3 18.3 %collective-permute-done.30 = f32[3,256,256]{2,1,0:T(8,128)S(1)} collective-permute-done((f32[3,256,256]{2,1,0:T(8,128)}, f32[3,256,256]{2,1,0:T(8,128)S(1)}, u32[]{:S(2)}, u32[]{:S(2)}) %collective-permute-start.30) | collective-permute-done | bytes 786464 | tf_op jit(solution)/shard_map/ppermute | solution.py:384
  162.8 4.0 %collective-permute-start.31 = (f32[3,256,256]{2,1,0:T(8,128)S(1)}, f32[3,256,256]{2,1,0:T(8,128)S(1)}, u32[]{:S(2)}, u32[]{:S(2)}) collective-permute-start(f32[3,256,256]{2,1,0:T(8,128)S(1)} %add.226), channel_id=1, source_target_pairs={{0,32},{16,48},{32,0},{48,16},{1,33},{17,49},{33,1},{49,17},{2,34}... | collective-permute-start | bytes 2359304 | tf_op jit(solution)/shard_map/ppermute | solution.py:384
  167.3 16.7 %collective-permute-done.31 = f32[3,256,256]{2,1,0:T(8,128)S(1)} collective-permute-done((f32[3,256,256]{2,1,0:T(8,128)S(1)}, f32[3,256,256]{2,1,0:T(8,128)S(1)}, u32[]{:S(2)}, u32[]{:S(2)}) %collective-permute-start.31) | collective-permute-done | bytes 786464 | tf_op jit(solution)/shard_map/ppermute | solution.py:384
  184.2 1.5 collective-permute-start.32
  185.7 29.3 %all-to-all-done = f32[16,512,256]{2,1,0:T(8,128)} async-done(((f32[16,512,256]{2,1,0:T(8,128)}), f32[16,512,256]{2,1,0:T(8,128)}, u32[]{:S(2)}, u32[]{:S(2)}) %all-to-all-start) | async-done | bytes 8388640 | tf_op jit(solution)/shard_map/all_to_all | solution.py:377
  215.1 15.8 %shard_map.39 = f32[768,256]{1,0:T(8,128)} custom-call(s32[16]{0:T(128)} %stack.67.places, f32[8192,256]{1,0:T(8,128)} %bitcast.20.e_ref, bf16[16,2,768,512]{3,2,1,0:T(8,128)(2,1)} %get-tuple-element.54.v_ref), custom_call_target="tpu_custom_call" | custom-call | flops 9663676416 | bytes 8388608 | tf_op jit(solution)/shard_map/pallas_call | solution.py:205
  230.9 6.3 %all-to-all-start.1 = ((f32[8,96,256]{2,1,0:T(8,128)}), f32[8,96,256]{2,1,0:T(8,128)S(1)}, u32[]{:S(2)}, u32[]{:S(2)}) async-start(f32[8,96,256]{2,1,0:T(8,128)} %bitcast.36), calls=%async_computation.1 | async-start | bytes 1572864 | tf_op jit(solution)/shard_map/all_to_all | solution.py:305
  237.2 12.1 %all-to-all-done.1 = f32[8,96,256]{2,1,0:T(8,128)S(1)} async-done(((f32[8,96,256]{2,1,0:T(8,128)}), f32[8,96,256]{2,1,0:T(8,128)S(1)}, u32[]{:S(2)}, u32[]{:S(2)}) %all-to-all-start.1) | async-done | bytes 786464 | tf_op jit(solution)/shard_map/all_to_all | solution.py:305
  250.4 3.6 %all-to-all-start.2 = ((f32[8,96,256]{2,1,0:T(8,128)}), f32[8,96,256]{2,1,0:T(8,128)S(1)}, u32[]{:S(2)}, u32[]{:S(2)}) async-start(f32[8,96,256]{2,1,0:T(8,128)} %broadcast_in_dim.19), calls=%async_computation.2 | async-start | bytes 1572864 | tf_op jit(solution)/shard_map/all_to_all | solution.py:312
  255.0 4.1 %shard_map.40.m_ref = f32[768,768]{1,0:T(8,128)} custom-call(f32[3,256,256]{2,1,0:T(8,128)} %t_ref.1, f32[3,256,256]{2,1,0:T(8,128)} %add.228.g_ref), custom_call_target="tpu_custom_call" | custom-call | tf_op jit(solution)/shard_map/pallas_call | solution.py:261
  259.1 7.1 %all-to-all-done.2 = f32[8,96,256]{2,1,0:T(8,128)S(1)} async-done(((f32[8,96,256]{2,1,0:T(8,128)}), f32[8,96,256]{2,1,0:T(8,128)S(1)}, u32[]{:S(2)}, u32[]{:S(2)}) %all-to-all-start.2) | async-done | bytes 786464 | tf_op jit(solution)/shard_map/all_to_all | solution.py:312
  267.1 17.7 %shard_map.41 = f32[8192,256]{1,0:T(8,128)} custom-call(s32[16]{0:T(128)} %stack.67.places, f32[8192,256]{1,0:T(8,128)} %bitcast.20.e_ref, f32[768,768]{1,0:T(8,128)} %shard_map.40.m_ref, f32[768,256]{1,0:T(8,128)} %bitcast.35, bf16[16,2,768,512]{3,2,1,0:T(8,128)(2,1)} %get-tuple-element.54.v_ref), custom_call_target="tpu_custom_call" | custom-call | flops 9663676416 | bytes 16777216 | tf_op jit(solution)/shard_map/pallas_call | solution.py:224
  (96 shorter events, 24.5 us)
Async XLA Ops:
  1.8 31.4 %collective-permute-start.4 = (f32[512,512]{1,0:T(8,128)S(1)}, f32[512,512]{1,0:T(8,128)S(1)}, u32[]{:S(2)}, u32[]{:S(2)}) collective-permute-start(f32[512,512]{1,0:T(8,128)S(1)} %pad_maximum_fusion.refs_0_), channel_id=1, source_target_pairs={{0,6},{1,3},{2,0},{3,5},{4,2},{5,7},{6,4},{7,1},{8,14},{9,11},{10,... | collective-permute-start | bytes 3145736 | tf_op jit(solution)/shard_map/ppermute | solution.py:326
  2.3 30.9 %collective-permute-start.3 = (f32[512,512]{1,0:T(8,128)S(1)}, f32[512,512]{1,0:T(8,128)}, u32[]{:S(2)}, u32[]{:S(2)}) collective-permute-start(f32[512,512]{1,0:T(8,128)S(1)} %pad_maximum_fusion.refs_0_), channel_id=1, source_target_pairs={{0,8},{8,0},{1,9},{9,1},{2,10},{10,2},{3,11},{11,3},{4,12},{12,4},... | collective-permute-start | bytes 3145736 | tf_op jit(solution)/shard_map/ppermute | solution.py:330
  5.6 15.6 %collective-permute-start.1 = (f32[256,512]{1,0:T(8,128)S(1)}, f32[256,512]{1,0:T(8,128)S(1)}, u32[]{:S(2)}, u32[]{:S(2)}) collective-permute-start(f32[256,512]{1,0:T(8,128)S(1)} %get-tuple-element.35.refs_1_), channel_id=1, source_target_pairs={{0,2},{1,7},{2,4},{3,1},{4,6},{5,3},{6,0},{7,5},{8,10},{9,15},{10,... | collective-permute-start | bytes 1572872 | tf_op jit(solution)/shard_map/ppermute | solution.py:326
  7.1 26.1 %collective-permute-start.2 = (f32[256,512]{1,0:T(8,128)S(1)}, f32[256,512]{1,0:T(8,128)S(1)}, u32[]{:S(2)}, u32[]{:S(2)}) collective-permute-start(f32[256,512]{1,0:T(8,128)S(1)} %get-tuple-element.35.refs_1_), channel_id=1, source_target_pairs={{0,6},{1,3},{2,0},{3,5},{4,2},{5,7},{6,4},{7,1},{8,14},{9,11},{10,... | collective-permute-start | bytes 1572872 | tf_op jit(solution)/shard_map/ppermute | solution.py:326
  21.2 12.0 %collective-permute-start.6 = (f32[256,512]{1,0:T(8,128)S(1)}, f32[256,512]{1,0:T(8,128)S(1)}, u32[]{:S(2)}, u32[]{:S(2)}) collective-permute-start(f32[256,512]{1,0:T(8,128)S(1)} %collective-permute-done.1.refs_3_), channel_id=1, source_target_pairs={{0,2},{1,7},{2,4},{3,1},{4,6},{5,3},{6,0},{7,5},{8,10},{9,15},{10,... | collective-permute-start | bytes 1572872 | tf_op jit(solution)/shard_map/ppermute | solution.py:326
  21.9 24.5 %collective-permute-start = (f32[512,512]{1,0:T(8,128)S(1)}, f32[512,512]{1,0:T(8,128)}, u32[]{:S(2)}, u32[]{:S(2)}) collective-permute-start(f32[512,512]{1,0:T(8,128)S(1)} %pad_maximum_fusion.refs_0_), channel_id=1, source_target_pairs={{0,2},{1,7},{2,4},{3,1},{4,6},{5,3},{6,0},{7,5},{8,10},{9,15},{10,... | collective-permute-start | bytes 3145736 | tf_op jit(solution)/shard_map/ppermute | solution.py:326
  33.2 33.0 %collective-permute-start.7 = (f32[512,512]{1,0:T(8,128)}, f32[512,512]{1,0:T(8,128)}, u32[]{:S(2)}, u32[]{:S(2)}) collective-permute-start(f32[512,512]{1,0:T(8,128)} %collective-permute-done.3.refs_8_), channel_id=1, source_target_pairs={{0,2},{1,7},{2,4},{3,1},{4,6},{5,3},{6,0},{7,5},{8,10},{9,15},{10,... | collective-permute-start | bytes 3145736 | tf_op jit(solution)/shard_map/ppermute | solution.py:326
  35.0 32.6 %collective-permute-start.13 = (f32[256,512]{1,0:T(8,128)S(1)}, f32[256,512]{1,0:T(8,128)S(1)}, u32[]{:S(2)}, u32[]{:S(2)}) collective-permute-start(f32[256,512]{1,0:T(8,128)S(1)} %collective-permute-done.6.refs_7_), channel_id=1, source_target_pairs={{0,8},{8,0},{1,9},{9,1},{2,10},{10,2},{3,11},{11,3},{4,12},{12,4},... | collective-permute-start | bytes 1572872 | tf_op jit(solution)/shard_map/ppermute | solution.py:330
  41.0 29.8 %collective-permute-start.10 = (f32[256,512]{1,0:T(8,128)S(1)}, f32[256,512]{1,0:T(8,128)S(1)}, u32[]{:S(2)}, u32[]{:S(2)}) collective-permute-start(f32[256,512]{1,0:T(8,128)S(1)} %get-tuple-element.35.refs_1_), channel_id=1, source_target_pairs={{0,8},{8,0},{1,9},{9,1},{2,10},{10,2},{3,11},{11,3},{4,12},{12,4},... | collective-permute-start | bytes 1572872 | tf_op jit(solution)/shard_map/ppermute | solution.py:330
  41.0 53.6 %collective-permute-start.8 = (f32[512,512]{1,0:T(8,128)}, f32[512,512]{1,0:T(8,128)}, u32[]{:S(2)}, u32[]{:S(2)}) collective-permute-start(f32[512,512]{1,0:T(8,128)} %collective-permute-done.3.refs_8_), channel_id=1, source_target_pairs={{0,6},{1,3},{2,0},{3,5},{4,2},{5,7},{6,4},{7,1},{8,14},{9,11},{10,... | collective-permute-start | bytes 3145736 | tf_op jit(solution)/shard_map/ppermute | solution.py:326
  46.4 48.3 %collective-permute-start.5 = (f32[512,512]{1,0:T(8,128)}, f32[512,512]{1,0:T(8,128)}, u32[]{:S(2)}, u32[]{:S(2)}) collective-permute-start(f32[512,512]{1,0:T(8,128)} %collective-permute-done.refs_2_), channel_id=1, source_target_pairs={{0,2},{1,7},{2,4},{3,1},{4,6},{5,3},{6,0},{7,5},{8,10},{9,15},{10,... | collective-permute-start | bytes 3145736 | tf_op jit(solution)/shard_map/ppermute | solution.py:326
  66.2 28.5 %collective-permute-start.9 = (f32[512,512]{1,0:T(8,128)}, f32[512,512]{1,0:T(8,128)}, u32[]{:S(2)}, u32[]{:S(2)}) collective-permute-start(f32[512,512]{1,0:T(8,128)} %collective-permute-done.7.refs_10_), channel_id=1, source_target_pairs={{0,2},{1,7},{2,4},{3,1},{4,6},{5,3},{6,0},{7,5},{8,10},{9,15},{10,... | collective-permute-start | bytes 3145736 | tf_op jit(solution)/shard_map/ppermute | solution.py:326
  67.7 16.4 %collective-permute-start.11 = (f32[256,512]{1,0:T(8,128)S(1)}, f32[256,512]{1,0:T(8,128)}, u32[]{:S(2)}, u32[]{:S(2)}) collective-permute-start(f32[256,512]{1,0:T(8,128)S(1)} %collective-permute-done.1.refs_3_), channel_id=1, source_target_pairs={{0,8},{8,0},{1,9},{9,1},{2,10},{10,2},{3,11},{11,3},{4,12},{12,4},... | collective-permute-start | bytes 1572872 | tf_op jit(solution)/shard_map/ppermute | solution.py:330
  71.6 23.0 %collective-permute-start.12 = (f32[256,512]{1,0:T(8,128)S(1)}, f32[256,512]{1,0:T(8,128)}, u32[]{:S(2)}, u32[]{:S(2)}) collective-permute-start(f32[256,512]{1,0:T(8,128)S(1)} %collective-permute-done.2.refs_5_), channel_id=1, source_target_pairs={{0,8},{8,0},{1,9},{9,1},{2,10},{10,2},{3,11},{11,3},{4,12},{12,4},... | collective-permute-start | bytes 1572872 | tf_op jit(solution)/shard_map/ppermute | solution.py:330
  94.6 120.4 %all-to-all-start = ((f32[16,512,256]{2,1,0:T(8,128)}), f32[16,512,256]{2,1,0:T(8,128)}, u32[]{:S(2)}, u32[]{:S(2)}) async-start(f32[16,512,256]{2,1,0:T(8,128)} %bitcast.34), calls=%async_computation | async-start | bytes 16777216 | tf_op jit(solution)/shard_map/all_to_all | solution.py:377
  101.4 4.9 %collective-permute-start.14 = (f32[512,512]{1,0:T(8,128)S(1)}, f32[512,512]{1,0:T(8,128)S(1)}, u32[]{:S(2)}, u32[]{:S(2)}) collective-permute-start(f32[512,512]{1,0:T(8,128)S(1)} %pad_maximum_fusion.refs_0_), channel_id=1, source_target_pairs={{0,1},{1,0},{2,3},{3,2},{4,5},{5,4},{6,7},{7,6},{8,9},{9,8},{10,11... | collective-permute-start | bytes 3145736 | tf_op jit(solution)/shard_map/ppermute | solution.py:330
  101.7 4.3 %collective-permute-start.15 = (f32[256,512]{1,0:T(8,128)S(1)}, f32[256,512]{1,0:T(8,128)S(1)}, u32[]{:S(2)}, u32[]{:S(2)}) collective-permute-start(f32[256,512]{1,0:T(8,128)S(1)} %get-tuple-element.35.refs_1_), channel_id=1, source_target_pairs={{0,1},{1,0},{2,3},{3,2},{4,5},{5,4},{6,7},{7,6},{8,9},{9,8},{10,11... | collective-permute-start | bytes 1572872 | tf_op jit(solution)/shard_map/ppermute | solution.py:330
  102.0 5.4 %collective-permute-start.17 = (f32[256,512]{1,0:T(8,128)S(1)}, f32[256,512]{1,0:T(8,128)S(1)}, u32[]{:S(2)}, u32[]{:S(2)}) collective-permute-start(f32[256,512]{1,0:T(8,128)S(1)} %collective-permute-done.1.refs_3_), channel_id=1, source_target_pairs={{0,1},{1,0},{2,3},{3,2},{4,5},{5,4},{6,7},{7,6},{8,9},{9,8},{10,11... | collective-permute-start | bytes 1572872 | tf_op jit(solution)/shard_map/ppermute | solution.py:330
  102.2 5.7 %collective-permute-start.19 = (f32[256,512]{1,0:T(8,128)}, f32[256,512]{1,0:T(8,128)S(1)}, u32[]{:S(2)}, u32[]{:S(2)}) collective-permute-start(f32[256,512]{1,0:T(8,128)} %copy-done.9), channel_id=1, source_target_pairs={{0,1},{1,0},{2,3},{3,2},{4,5},{5,4},{6,7},{7,6},{8,9},{9,8},{10,11... | collective-permute-start | bytes 1572872 | tf_op jit(solution)/shard_map/ppermute | solution.py:330
  102.5 5.5 %collective-permute-start.21 = (f32[256,512]{1,0:T(8,128)}, f32[256,512]{1,0:T(8,128)S(1)}, u32[]{:S(2)}, u32[]{:S(2)}) collective-permute-start(f32[256,512]{1,0:T(8,128)} %copy-done.10), channel_id=1, source_target_pairs={{0,1},{1,0},{2,3},{3,2},{4,5},{5,4},{6,7},{7,6},{8,9},{9,8},{10,11... | collective-permute-start | bytes 1572872 | tf_op jit(solution)/shard_map/ppermute | solution.py:330
  106.3 8.5 %collective-permute-start.16 = (f32[512,512]{1,0:T(8,128)}, f32[512,512]{1,0:T(8,128)S(1)}, u32[]{:S(2)}, u32[]{:S(2)}) collective-permute-start(f32[512,512]{1,0:T(8,128)} %collective-permute-done.refs_2_), channel_id=1, source_target_pairs={{0,1},{1,0},{2,3},{3,2},{4,5},{5,4},{6,7},{7,6},{8,9},{9,8},{10,11... | collective-permute-start | bytes 3145736 | tf_op jit(solution)/shard_map/ppermute | solution.py:330
  107.5 7.5 %collective-permute-start.18 = (f32[512,512]{1,0:T(8,128)S(1)}, f32[512,512]{1,0:T(8,128)S(1)}, u32[]{:S(2)}, u32[]{:S(2)}) collective-permute-start(f32[512,512]{1,0:T(8,128)S(1)} %collective-permute-done.4.refs_4_), channel_id=1, source_target_pairs={{0,1},{1,0},{2,3},{3,2},{4,5},{5,4},{6,7},{7,6},{8,9},{9,8},{10,11... | collective-permute-start | bytes 3145736 | tf_op jit(solution)/shard_map/ppermute | solution.py:330
  108.0 4.9 %collective-permute-start.27 = (f32[256,512]{1,0:T(8,128)}, f32[256,512]{1,0:T(8,128)S(1)}, u32[]{:S(2)}, u32[]{:S(2)}) collective-permute-start(f32[256,512]{1,0:T(8,128)} %collective-permute-done.12.refs_13_), channel_id=1, source_target_pairs={{0,1},{1,0},{2,3},{3,2},{4,5},{5,4},{6,7},{7,6},{8,9},{9,8},{10,11... | collective-permute-start | bytes 1572872 | tf_op jit(solution)/shard_map/ppermute | solution.py:330
  108.4 6.0 %collective-permute-start.29 = (f32[256,512]{1,0:T(8,128)}, f32[256,512]{1,0:T(8,128)S(1)}, u32[]{:S(2)}, u32[]{:S(2)}) collective-permute-start(f32[256,512]{1,0:T(8,128)} %copy-done.11), channel_id=1, source_target_pairs={{0,1},{1,0},{2,3},{3,2},{4,5},{5,4},{6,7},{7,6},{8,9},{9,8},{10,11... | collective-permute-start | bytes 1572872 | tf_op jit(solution)/shard_map/ppermute | solution.py:330
  114.4 5.4 %collective-permute-start.24 = (f32[512,512]{1,0:T(8,128)}, f32[512,512]{1,0:T(8,128)}, u32[]{:S(2)}, u32[]{:S(2)}) collective-permute-start(f32[512,512]{1,0:T(8,128)} %collective-permute-done.7.refs_10_), channel_id=1, source_target_pairs={{0,1},{1,0},{2,3},{3,2},{4,5},{5,4},{6,7},{7,6},{8,9},{9,8},{10,11... | collective-permute-start | bytes 3145736 | tf_op jit(solution)/shard_map/ppermute | solution.py:330
  114.8 6.5 %collective-permute-start.26 = (f32[512,512]{1,0:T(8,128)}, f32[512,512]{1,0:T(8,128)}, u32[]{:S(2)}, u32[]{:S(2)}) collective-permute-start(f32[512,512]{1,0:T(8,128)} %collective-permute-done.8.refs_12_), channel_id=1, source_target_pairs={{0,1},{1,0},{2,3},{3,2},{4,5},{5,4},{6,7},{7,6},{8,9},{9,8},{10,11... | collective-permute-start | bytes 3145736 | tf_op jit(solution)/shard_map/ppermute | solution.py:330
  115.0 6.4 %collective-permute-start.28 = (f32[512,512]{1,0:T(8,128)}, f32[512,512]{1,0:T(8,128)S(1)}, u32[]{:S(2)}, u32[]{:S(2)}) collective-permute-start(f32[512,512]{1,0:T(8,128)} %collective-permute-done.9.refs_14_), channel_id=1, source_target_pairs={{0,1},{1,0},{2,3},{3,2},{4,5},{5,4},{6,7},{7,6},{8,9},{9,8},{10,11... | collective-permute-start | bytes 3145736 | tf_op jit(solution)/shard_map/ppermute | solution.py:330
  141.1 20.4 %collective-permute-start.30 = (f32[3,256,256]{2,1,0:T(8,128)}, f32[3,256,256]{2,1,0:T(8,128)S(1)}, u32[]{:S(2)}, u32[]{:S(2)}) collective-permute-start(f32[3,256,256]{2,1,0:T(8,128)} %get-tuple-element.53), channel_id=1, source_target_pairs={{0,16},{16,0},{32,48},{48,32},{1,17},{17,1},{33,49},{49,33},{2,18}... | collective-permute-start | bytes 2359304 | tf_op jit(solution)/shard_map/ppermute | solution.py:384
  162.8 21.3 %collective-permute-start.31 = (f32[3,256,256]{2,1,0:T(8,128)S(1)}, f32[3,256,256]{2,1,0:T(8,128)S(1)}, u32[]{:S(2)}, u32[]{:S(2)}) collective-permute-start(f32[3,256,256]{2,1,0:T(8,128)S(1)} %add.226), channel_id=1, source_target_pairs={{0,32},{16,48},{32,0},{48,16},{1,33},{17,49},{33,1},{49,17},{2,34}... | collective-permute-start | bytes 2359304 | tf_op jit(solution)/shard_map/ppermute | solution.py:384
  184.2 53.1 %collective-permute-start.32 = (f32[3,256,256]{2,1,0:T(8,128)S(1)}, f32[3,256,256]{2,1,0:T(8,128)S(1)}, u32[]{:S(2)}, u32[]{:S(2)}) collective-permute-start(f32[3,256,256]{2,1,0:T(8,128)S(1)} %add.227), channel_id=1, source_target_pairs={{0,64},{64,0},{1,65},{65,1},{2,66},{66,2},{3,67},{67,3},{4,68},{68... | collective-permute-start | bytes 2359304 | tf_op jit(solution)/shard_map/ppermute | solution.py:330
  230.9 18.4 %all-to-all-start.1 = ((f32[8,96,256]{2,1,0:T(8,128)}), f32[8,96,256]{2,1,0:T(8,128)S(1)}, u32[]{:S(2)}, u32[]{:S(2)}) async-start(f32[8,96,256]{2,1,0:T(8,128)} %bitcast.36), calls=%async_computation.1 | async-start | bytes 1572864 | tf_op jit(solution)/shard_map/all_to_all | solution.py:305
  250.4 15.8 %all-to-all-start.2 = ((f32[8,96,256]{2,1,0:T(8,128)}), f32[8,96,256]{2,1,0:T(8,128)S(1)}, u32[]{:S(2)}, u32[]{:S(2)}) async-start(f32[8,96,256]{2,1,0:T(8,128)} %broadcast_in_dim.19), calls=%async_computation.2 | async-start | bytes 1572864 | tf_op jit(solution)/shard_map/all_to_all | solution.py:312
  (25 other events, 572.5 us)

commit v6 on v5

--- a/solution.py
+++ b/solution.py
@@ -367,13 +367,16 @@
     early, (wide_there, wide_other) = after((slim, slim_near, slim_other), wide_there, wide_other)
     (wide_there,), (slim_far,) = after((wide_there,), slim_far)
     there_near, there_other = send(wide_there, 1), send(wide_there, -1)
+    both = swap(jnp.concatenate(early[1:], axis=0), "yhi")
+    slim_there, far_there = swap(early[0], "yhi"), swap(slim_far, "yhi")
     slim_held = [slim, slim_near, slim_other, slim_far]
-    slim_held += [swap(part, "yhi") for part in (*early, slim_far)]
     wide_held = [wide, wide_near, wide_other, send(wide_near, 1), wide_there, there_near, there_other]
     wide_held.append(send(there_near, 1))
     block = columns_apart(eigvecs, lax.axis_size(COL))
-    (block,), held = after((block,), *wide_held[1:], *slim_held[1:])
-    wide_held[1:], slim_held[1:] = held[:7], held[7:]
+    (block,), held = after((block,), *wide_held[1:], *slim_held[1:], slim_there, both, far_there)
+    wide_held[1:], slim_held[1:] = held[:7], held[7:10]
+    slim_there, both, far_there = held[10:]
+    slim_held += [slim_there, both[:block_size], both[block_size:], far_there]
     block = lax.all_to_all(block, COL, split_axis=0, concat_axis=0, tiled=True)
     pieces = list(zip(wide_held, slim_held))
     pieces += [tuple(swap(part, "core") for part in parts) for parts in pieces]

time: 285 us -> 281 us (0.986)
  waiting for transfers between devices: 159 us -> 154 us
    ppermute x22 -> x21, waiting for transfers between devices: 30.7 us -> 21.3 us  [swap(): return lax.ppermute(piece, axis, [(0, 1), (1, 0)])]
    ppermute x9, waiting for transfers between devices: 44.7 us -> 48.8 us  [send(): return lax.ppermute(piece, ('x', 'core'), turn(sign))]
    ppermute x22 -> x21, starting transfers between devices: 19.4 us -> 18.6 us  [swap(): return lax.ppermute(piece, axis, [(0, 1), (1, 0)])]
  transfers between devices with their start and end apart: 36 -> 35, of which waited for: 20 -> 19; matrix products, arithmetic and copies ran while one was open for 1% -> 1% of each run, Pallas kernels for 16% -> 16%
where the time goes in v6:
time: 281 us; the launch traced here: 280 us
  waiting for transfers between devices  154 us (55%)
  Pallas kernels  63.1 us (22%)
  starting transfers between devices  54.5 us (19%)
  local copies, waits for them, and re-layouts  4.35 us (2%)
  other arithmetic  4.15 us (1%)
    ppermute x9, waiting for transfers between devices, send(): return lax.ppermute(piece, ('x', 'core'), turn(sign))  48.8 us
    ppermute x2, waiting for transfers between devices, on_device(): gram = gram + lax.ppermute(gram, 'z', [(i, i ^ step) for i in range(size)])  35 us
    all_to_all x1, waiting for transfers between devices, on_device(): block = lax.all_to_all(block, COL, split_axis=0, concat_axis=0, tiled=True)  29.6 us
    ppermute x21, waiting for transfers between devices, swap(): return lax.ppermute(piece, axis, [(0, 1), (1, 0)])  21.3 us
    pallas_call x1, Pallas kernels, gram_of(): pl.pallas_call(functools.partial(gram_kernel, blocks, size), in_specs=[FA...  18.8 us
    ppermute x21, starting transfers between devices, swap(): return lax.ppermute(piece, axis, [(0, 1), (1, 0)])  18.6 us
    pallas_call x1, Pallas kernels, apply(): pl.pallas_call(apply_kernel, in_specs=[SCALARS, FAR, NEAR, NEAR, FAR], ou...  17.7 us
    pallas_call x1, Pallas kernels, project(): pl.pallas_call(project_kernel, in_specs=[SCALARS, FAR, FAR], out_specs=NE...  15.8 us
  transfers between devices with their start and end apart: 35, of which 19 were waited for; matrix products, arithmetic and copies ran while one was open for 1% of the time, Pallas kernels for 16%

profile of v6, /device:TPU:2, one launch (start us, length us, event | category | flops | bytes accessed | tf_op | source)
XLA Modules:
  0.0 280.4 jit_solution(1393158277451395891)
XLA Ops:
  0.0 1.6 fusion
  2.3 3.3 %collective-permute-start.3 = (f32[512,512]{1,0:T(8,128)S(1)}, f32[512,512]{1,0:T(8,128)}, u32[]{:S(2)}, u32[]{:S(2)}) collective-permute-start(f32[512,512]{1,0:T(8,128)S(1)} %pad_maximum_fusion.refs_0_), channel_id=1, source_target_pairs={{0,8},{8,0},{1,9},{9,1},{2,10},{10,2},{3,11},{11,3},{4,12},{12,4},... | collective-permute-start | bytes 3145736 | tf_op jit(solution)/shard_map/ppermute | solution.py:330
  8.3 12.8 %collective-permute-done.1.refs_3_ = f32[256,512]{1,0:T(8,128)S(1)} collective-permute-done((f32[256,512]{1,0:T(8,128)S(1)}, f32[256,512]{1,0:T(8,128)S(1)}, u32[]{:S(2)}, u32[]{:S(2)}) %collective-permute-start.1) | collective-permute-done | bytes 524320 | tf_op jit(solution)/shard_map/ppermute | solution.py:326
  23.4 9.8 %collective-permute-done.2.refs_5_ = f32[256,512]{1,0:T(8,128)S(1)} collective-permute-done((f32[256,512]{1,0:T(8,128)S(1)}, f32[256,512]{1,0:T(8,128)S(1)}, u32[]{:S(2)}, u32[]{:S(2)}) %collective-permute-start.2) | collective-permute-done | bytes 524320 | tf_op jit(solution)/shard_map/ppermute | solution.py:326
  33.2 1.9 collective-permute-start.7
  35.3 6.1 %collective-permute-start.12 = (f32[256,512]{1,0:T(8,128)S(1)}, f32[256,512]{1,0:T(8,128)S(1)}, u32[]{:S(2)}, u32[]{:S(2)}) collective-permute-start(f32[256,512]{1,0:T(8,128)S(1)} %collective-permute-done.6.refs_7_), channel_id=1, source_target_pairs={{0,8},{8,0},{1,9},{9,1},{2,10},{10,2},{3,11},{11,3},{4,12},{12,4},... | collective-permute-start | bytes 1572872 | tf_op jit(solution)/shard_map/ppermute | solution.py:330
  41.6 7.7 %collective-permute-done.refs_2_ = f32[512,512]{1,0:T(8,128)} collective-permute-done((f32[512,512]{1,0:T(8,128)S(1)}, f32[512,512]{1,0:T(8,128)}, u32[]{:S(2)}, u32[]{:S(2)}) %collective-permute-start) | collective-permute-done | bytes 1048608 | tf_op jit(solution)/shard_map/ppermute | solution.py:326
  49.3 2.6 collective-permute-start.5
  51.9 14.3 %collective-permute-done.7.refs_10_ = f32[512,512]{1,0:T(8,128)} collective-permute-done((f32[512,512]{1,0:T(8,128)}, f32[512,512]{1,0:T(8,128)}, u32[]{:S(2)}, u32[]{:S(2)}) %collective-permute-start.7) | collective-permute-done | bytes 1048608 | tf_op jit(solution)/shard_map/ppermute | solution.py:326
  68.4 3.2 %collective-permute-start.10 = (f32[256,512]{1,0:T(8,128)S(1)}, f32[256,512]{1,0:T(8,128)}, u32[]{:S(2)}, u32[]{:S(2)}) collective-permute-start(f32[256,512]{1,0:T(8,128)S(1)} %get-tuple-element.34.refs_1_), channel_id=1, source_target_pairs={{0,8},{8,0},{1,9},{9,1},{2,10},{10,2},{3,11},{11,3},{4,12},{12,4},... | collective-permute-start | bytes 1572872 | tf_op jit(solution)/shard_map/ppermute | solution.py:330
  71.6 6.7 %shard_map.37 = f32[8192,256]{1,0:T(8,128)} custom-call(f32[512,4096]{1,0:T(8,128)} %e_ref.1), custom_call_target="tpu_custom_call" | custom-call | bytes 16777216 | tf_op jit(solution)/shard_map/pallas_call | solution.py:289
  78.3 6.0 %collective-permute-done.10.refs_9_ = f32[256,512]{1,0:T(8,128)} collective-permute-done((f32[256,512]{1,0:T(8,128)S(1)}, f32[256,512]{1,0:T(8,128)}, u32[]{:S(2)}, u32[]{:S(2)}) %collective-permute-start.10) | collective-permute-done | bytes 524320 | tf_op jit(solution)/shard_map/ppermute | solution.py:330
  84.4 4.3 %collective-permute-done.9.refs_14_ = f32[512,512]{1,0:T(8,128)} collective-permute-done((f32[512,512]{1,0:T(8,128)}, f32[512,512]{1,0:T(8,128)}, u32[]{:S(2)}, u32[]{:S(2)}) %collective-permute-start.9) | collective-permute-done | bytes 1048608 | tf_op jit(solution)/shard_map/ppermute | solution.py:326
  88.6 8.2 %all-to-all-start = ((f32[16,512,256]{2,1,0:T(8,128)}), f32[16,512,256]{2,1,0:T(8,128)}, u32[]{:S(2)}, u32[]{:S(2)}) async-start(f32[16,512,256]{2,1,0:T(8,128)} %bitcast.34), calls=%async_computation | async-start | bytes 16777216 | tf_op jit(solution)/shard_map/all_to_all | solution.py:380
  98.1 3.3 %collective-permute-done.14.refs_17_ = f32[256,512]{1,0:T(8,128)S(1)} collective-permute-done((f32[256,512]{1,0:T(8,128)S(1)}, f32[256,512]{1,0:T(8,128)S(1)}, u32[]{:S(2)}, u32[]{:S(2)}) %collective-permute-start.14) | collective-permute-done | bytes 524320 | tf_op jit(solution)/shard_map/ppermute | solution.py:330
  105.0 3.4 %collective-permute-done.28.refs_31_ = f32[256,512]{1,0:T(8,128)S(1)} collective-permute-done((f32[256,512]{1,0:T(8,128)}, f32[256,512]{1,0:T(8,128)S(1)}, u32[]{:S(2)}, u32[]{:S(2)}) %collective-permute-start.28) | collective-permute-done | bytes 524320 | tf_op jit(solution)/shard_map/ppermute | solution.py:330
  111.2 1.6 collective-permute-done.21.refs_24_
  112.8 1.5 collective-permute-done.23.refs_26_
  117.4 18.8 %shard_map.38 = (f32[3,256,256]{2,1,0:T(8,128)}, bf16[16,2,768,512]{3,2,1,0:T(8,128)(2,1)}) custom-call(f32[512,512]{1,0:T(8,128)} %copy-done.1, f32[256,512]{1,0:T(8,128)} %copy-done.2, f32[512,512]{1,0:T(8,128)} %collective-permute-done.refs_2_, f32[256,512]{1,0:T(8,128)} %copy-done.4, f32[512,512]{1,0:T(8,128)} %copy-done.9, f32[256,512]{1,0:T(8,128)} %copy-done.6, ...), custom_call_target="tpu_custom_call" | custom-call | flops 9663676416 | bytes 25165824 | tf_op jit(solution)/shard_map/pallas_call | solution.py:183
  136.2 2.1 collective-permute-start.29
  138.2 18.3 %collective-permute-done.29 = f32[3,256,256]{2,1,0:T(8,128)S(1)} collective-permute-done((f32[3,256,256]{2,1,0:T(8,128)}, f32[3,256,256]{2,1,0:T(8,128)S(1)}, u32[]{:S(2)}, u32[]{:S(2)}) %collective-permute-start.29) | collective-permute-done | bytes 786464 | tf_op jit(solution)/shard_map/ppermute | solution.py:387
  157.7 3.9 %collective-permute-start.30 = (f32[3,256,256]{2,1,0:T(8,128)S(1)}, f32[3,256,256]{2,1,0:T(8,128)S(1)}, u32[]{:S(2)}, u32[]{:S(2)}) collective-permute-start(f32[3,256,256]{2,1,0:T(8,128)S(1)} %add.226), channel_id=1, source_target_pairs={{0,32},{16,48},{32,0},{48,16},{1,33},{17,49},{33,1},{49,17},{2,34}... | collective-permute-start | bytes 2359304 | tf_op jit(solution)/shard_map/ppermute | solution.py:387
  162.3 16.7 %collective-permute-done.30 = f32[3,256,256]{2,1,0:T(8,128)S(1)} collective-permute-done((f32[3,256,256]{2,1,0:T(8,128)S(1)}, f32[3,256,256]{2,1,0:T(8,128)S(1)}, u32[]{:S(2)}, u32[]{:S(2)}) %collective-permute-start.30) | collective-permute-done | bytes 786464 | tf_op jit(solution)/shard_map/ppermute | solution.py:387
  179.1 1.7 collective-permute-start.31
  180.8 29.6 %all-to-all-done = f32[16,512,256]{2,1,0:T(8,128)} async-done(((f32[16,512,256]{2,1,0:T(8,128)}), f32[16,512,256]{2,1,0:T(8,128)}, u32[]{:S(2)}, u32[]{:S(2)}) %all-to-all-start) | async-done | bytes 8388640 | tf_op jit(solution)/shard_map/all_to_all | solution.py:380
  210.4 15.8 %shard_map.39 = f32[768,256]{1,0:T(8,128)} custom-call(s32[16]{0:T(128)} %stack.67.places, f32[8192,256]{1,0:T(8,128)} %bitcast.20.e_ref, bf16[16,2,768,512]{3,2,1,0:T(8,128)(2,1)} %get-tuple-element.52.v_ref), custom_call_target="tpu_custom_call" | custom-call | flops 9663676416 | bytes 8388608 | tf_op jit(solution)/shard_map/pallas_call | solution.py:205
  226.3 6.4 %all-to-all-start.1 = ((f32[8,96,256]{2,1,0:T(8,128)}), f32[8,96,256]{2,1,0:T(8,128)S(1)}, u32[]{:S(2)}, u32[]{:S(2)}) async-start(f32[8,96,256]{2,1,0:T(8,128)} %bitcast.36), calls=%async_computation.1 | async-start | bytes 1572864 | tf_op jit(solution)/shard_map/all_to_all | solution.py:305
  232.7 12.1 %all-to-all-done.1 = f32[8,96,256]{2,1,0:T(8,128)S(1)} async-done(((f32[8,96,256]{2,1,0:T(8,128)}), f32[8,96,256]{2,1,0:T(8,128)S(1)}, u32[]{:S(2)}, u32[]{:S(2)}) %all-to-all-start.1) | async-done | bytes 786464 | tf_op jit(solution)/shard_map/all_to_all | solution.py:305
  245.8 3.6 %all-to-all-start.2 = ((f32[8,96,256]{2,1,0:T(8,128)}), f32[8,96,256]{2,1,0:T(8,128)S(1)}, u32[]{:S(2)}, u32[]{:S(2)}) async-start(f32[8,96,256]{2,1,0:T(8,128)} %broadcast_in_dim.19), calls=%async_computation.2 | async-start | bytes 1572864 | tf_op jit(solution)/shard_map/all_to_all | solution.py:312
  250.4 4.1 %shard_map.40.m_ref = f32[768,768]{1,0:T(8,128)} custom-call(f32[3,256,256]{2,1,0:T(8,128)} %t_ref.1, f32[3,256,256]{2,1,0:T(8,128)} %add.228.g_ref), custom_call_target="tpu_custom_call" | custom-call | tf_op jit(solution)/shard_map/pallas_call | solution.py:261
  254.5 7.1 %all-to-all-done.2 = f32[8,96,256]{2,1,0:T(8,128)S(1)} async-done(((f32[8,96,256]{2,1,0:T(8,128)}), f32[8,96,256]{2,1,0:T(8,128)S(1)}, u32[]{:S(2)}, u32[]{:S(2)}) %all-to-all-start.2) | async-done | bytes 786464 | tf_op jit(solution)/shard_map/all_to_all | solution.py:312
  262.5 17.7 %shard_map.41 = f32[8192,256]{1,0:T(8,128)} custom-call(s32[16]{0:T(128)} %stack.67.places, f32[8192,256]{1,0:T(8,128)} %bitcast.20.e_ref, f32[768,768]{1,0:T(8,128)} %shard_map.40.m_ref, f32[768,256]{1,0:T(8,128)} %bitcast.35, bf16[16,2,768,512]{3,2,1,0:T(8,128)(2,1)} %get-tuple-element.52.v_ref), custom_call_target="tpu_custom_call" | custom-call | flops 9663676416 | bytes 16777216 | tf_op jit(solution)/shard_map/pallas_call | solution.py:224
  (100 shorter events, 23.9 us)
Async XLA Ops:
  1.8 31.4 %collective-permute-start.4 = (f32[512,512]{1,0:T(8,128)S(1)}, f32[512,512]{1,0:T(8,128)S(1)}, u32[]{:S(2)}, u32[]{:S(2)}) collective-permute-start(f32[512,512]{1,0:T(8,128)S(1)} %pad_maximum_fusion.refs_0_), channel_id=1, source_target_pairs={{0,6},{1,3},{2,0},{3,5},{4,2},{5,7},{6,4},{7,1},{8,14},{9,11},{10,... | collective-permute-start | bytes 3145736 | tf_op jit(solution)/shard_map/ppermute | solution.py:326
  2.3 30.9 %collective-permute-start.3 = (f32[512,512]{1,0:T(8,128)S(1)}, f32[512,512]{1,0:T(8,128)}, u32[]{:S(2)}, u32[]{:S(2)}) collective-permute-start(f32[512,512]{1,0:T(8,128)S(1)} %pad_maximum_fusion.refs_0_), channel_id=1, source_target_pairs={{0,8},{8,0},{1,9},{9,1},{2,10},{10,2},{3,11},{11,3},{4,12},{12,4},... | collective-permute-start | bytes 3145736 | tf_op jit(solution)/shard_map/ppermute | solution.py:330
  5.6 15.6 %collective-permute-start.1 = (f32[256,512]{1,0:T(8,128)S(1)}, f32[256,512]{1,0:T(8,128)S(1)}, u32[]{:S(2)}, u32[]{:S(2)}) collective-permute-start(f32[256,512]{1,0:T(8,128)S(1)} %get-tuple-element.34.refs_1_), channel_id=1, source_target_pairs={{0,2},{1,7},{2,4},{3,1},{4,6},{5,3},{6,0},{7,5},{8,10},{9,15},{10,... | collective-permute-start | bytes 1572872 | tf_op jit(solution)/shard_map/ppermute | solution.py:326
  7.0 26.1 %collective-permute-start.2 = (f32[256,512]{1,0:T(8,128)S(1)}, f32[256,512]{1,0:T(8,128)S(1)}, u32[]{:S(2)}, u32[]{:S(2)}) collective-permute-start(f32[256,512]{1,0:T(8,128)S(1)} %get-tuple-element.34.refs_1_), channel_id=1, source_target_pairs={{0,6},{1,3},{2,0},{3,5},{4,2},{5,7},{6,4},{7,1},{8,14},{9,11},{10,... | collective-permute-start | bytes 1572872 | tf_op jit(solution)/shard_map/ppermute | solution.py:326
  21.2 12.0 %collective-permute-start.6 = (f32[256,512]{1,0:T(8,128)S(1)}, f32[256,512]{1,0:T(8,128)S(1)}, u32[]{:S(2)}, u32[]{:S(2)}) collective-permute-start(f32[256,512]{1,0:T(8,128)S(1)} %collective-permute-done.1.refs_3_), channel_id=1, source_target_pairs={{0,2},{1,7},{2,4},{3,1},{4,6},{5,3},{6,0},{7,5},{8,10},{9,15},{10,... | collective-permute-start | bytes 1572872 | tf_op jit(solution)/shard_map/ppermute | solution.py:326
  21.9 27.4 %collective-permute-start = (f32[512,512]{1,0:T(8,128)S(1)}, f32[512,512]{1,0:T(8,128)}, u32[]{:S(2)}, u32[]{:S(2)}) collective-permute-start(f32[512,512]{1,0:T(8,128)S(1)} %pad_maximum_fusion.refs_0_), channel_id=1, source_target_pairs={{0,2},{1,7},{2,4},{3,1},{4,6},{5,3},{6,0},{7,5},{8,10},{9,15},{10,... | collective-permute-start | bytes 3145736 | tf_op jit(solution)/shard_map/ppermute | solution.py:326
  33.2 33.0 %collective-permute-start.7 = (f32[512,512]{1,0:T(8,128)}, f32[512,512]{1,0:T(8,128)}, u32[]{:S(2)}, u32[]{:S(2)}) collective-permute-start(f32[512,512]{1,0:T(8,128)} %collective-permute-done.3.refs_8_), channel_id=1, source_target_pairs={{0,2},{1,7},{2,4},{3,1},{4,6},{5,3},{6,0},{7,5},{8,10},{9,15},{10,... | collective-permute-start | bytes 3145736 | tf_op jit(solution)/shard_map/ppermute | solution.py:326
  35.0 49.3 %collective-permute-start.8 = (f32[512,512]{1,0:T(8,128)}, f32[512,512]{1,0:T(8,128)}, u32[]{:S(2)}, u32[]{:S(2)}) collective-permute-start(f32[512,512]{1,0:T(8,128)} %collective-permute-done.3.refs_8_), channel_id=1, source_target_pairs={{0,6},{1,3},{2,0},{3,5},{4,2},{5,7},{6,4},{7,1},{8,14},{9,11},{10,... | collective-permute-start | bytes 3145736 | tf_op jit(solution)/shard_map/ppermute | solution.py:326
  35.3 32.4 %collective-permute-start.12 = (f32[256,512]{1,0:T(8,128)S(1)}, f32[256,512]{1,0:T(8,128)S(1)}, u32[]{:S(2)}, u32[]{:S(2)}) collective-permute-start(f32[256,512]{1,0:T(8,128)S(1)} %collective-permute-done.6.refs_7_), channel_id=1, source_target_pairs={{0,8},{8,0},{1,9},{9,1},{2,10},{10,2},{3,11},{11,3},{4,12},{12,4},... | collective-permute-start | bytes 1572872 | tf_op jit(solution)/shard_map/ppermute | solution.py:330
  41.5 42.9 %collective-permute-start.11 = (f32[512,512]{1,0:T(8,128)S(1)}, f32[512,512]{1,0:T(8,128)S(1)}, u32[]{:S(2)}, u32[]{:S(2)}) collective-permute-start(f32[512,512]{1,0:T(8,128)S(1)} %pad_maximum_fusion.1), channel_id=1, source_target_pairs={{0,8},{8,0},{1,9},{9,1},{2,10},{10,2},{3,11},{11,3},{4,12},{12,4},... | collective-permute-start | bytes 3145736 | tf_op jit(solution)/shard_map/ppermute | solution.py:330
  49.3 35.0 %collective-permute-start.5 = (f32[512,512]{1,0:T(8,128)}, f32[512,512]{1,0:T(8,128)}, u32[]{:S(2)}, u32[]{:S(2)}) collective-permute-start(f32[512,512]{1,0:T(8,128)} %collective-permute-done.refs_2_), channel_id=1, source_target_pairs={{0,2},{1,7},{2,4},{3,1},{4,6},{5,3},{6,0},{7,5},{8,10},{9,15},{10,... | collective-permute-start | bytes 3145736 | tf_op jit(solution)/shard_map/ppermute | solution.py:326
  66.2 22.5 %collective-permute-start.9 = (f32[512,512]{1,0:T(8,128)}, f32[512,512]{1,0:T(8,128)}, u32[]{:S(2)}, u32[]{:S(2)}) collective-permute-start(f32[512,512]{1,0:T(8,128)} %collective-permute-done.7.refs_10_), channel_id=1, source_target_pairs={{0,2},{1,7},{2,4},{3,1},{4,6},{5,3},{6,0},{7,5},{8,10},{9,15},{10,... | collective-permute-start | bytes 3145736 | tf_op jit(solution)/shard_map/ppermute | solution.py:326
  68.4 15.9 %collective-permute-start.10 = (f32[256,512]{1,0:T(8,128)S(1)}, f32[256,512]{1,0:T(8,128)}, u32[]{:S(2)}, u32[]{:S(2)}) collective-permute-start(f32[256,512]{1,0:T(8,128)S(1)} %get-tuple-element.34.refs_1_), channel_id=1, source_target_pairs={{0,8},{8,0},{1,9},{9,1},{2,10},{10,2},{3,11},{11,3},{4,12},{12,4},... | collective-permute-start | bytes 1572872 | tf_op jit(solution)/shard_map/ppermute | solution.py:330
  88.6 121.8 %all-to-all-start = ((f32[16,512,256]{2,1,0:T(8,128)}), f32[16,512,256]{2,1,0:T(8,128)}, u32[]{:S(2)}, u32[]{:S(2)}) async-start(f32[16,512,256]{2,1,0:T(8,128)} %bitcast.34), calls=%async_computation | async-start | bytes 16777216 | tf_op jit(solution)/shard_map/all_to_all | solution.py:380
  96.8 4.9 %collective-permute-start.13 = (f32[512,512]{1,0:T(8,128)S(1)}, f32[512,512]{1,0:T(8,128)S(1)}, u32[]{:S(2)}, u32[]{:S(2)}) collective-permute-start(f32[512,512]{1,0:T(8,128)S(1)} %pad_maximum_fusion.refs_0_), channel_id=1, source_target_pairs={{0,1},{1,0},{2,3},{3,2},{4,5},{5,4},{6,7},{7,6},{8,9},{9,8},{10,11... | collective-permute-start | bytes 3145736 | tf_op jit(solution)/shard_map/ppermute | solution.py:330
  97.0 4.3 %collective-permute-start.14 = (f32[256,512]{1,0:T(8,128)S(1)}, f32[256,512]{1,0:T(8,128)S(1)}, u32[]{:S(2)}, u32[]{:S(2)}) collective-permute-start(f32[256,512]{1,0:T(8,128)S(1)} %copy-done.3), channel_id=1, source_target_pairs={{0,1},{1,0},{2,3},{3,2},{4,5},{5,4},{6,7},{7,6},{8,9},{9,8},{10,11... | collective-permute-start | bytes 1572872 | tf_op jit(solution)/shard_map/ppermute | solution.py:330
  97.4 5.4 %collective-permute-start.16 = (f32[256,512]{1,0:T(8,128)S(1)}, f32[256,512]{1,0:T(8,128)S(1)}, u32[]{:S(2)}, u32[]{:S(2)}) collective-permute-start(f32[256,512]{1,0:T(8,128)S(1)} %copy-done.5), channel_id=1, source_target_pairs={{0,1},{1,0},{2,3},{3,2},{4,5},{5,4},{6,7},{7,6},{8,9},{9,8},{10,11... | collective-permute-start | bytes 1572872 | tf_op jit(solution)/shard_map/ppermute | solution.py:330
  97.6 6.6 %collective-permute-start.18 = (f32[256,512]{1,0:T(8,128)}, f32[256,512]{1,0:T(8,128)S(1)}, u32[]{:S(2)}, u32[]{:S(2)}) collective-permute-start(f32[256,512]{1,0:T(8,128)} %copy-done.6), channel_id=1, source_target_pairs={{0,1},{1,0},{2,3},{3,2},{4,5},{5,4},{6,7},{7,6},{8,9},{9,8},{10,11... | collective-permute-start | bytes 1572872 | tf_op jit(solution)/shard_map/ppermute | solution.py:330
  97.9 6.5 %collective-permute-start.20 = (f32[256,512]{1,0:T(8,128)}, f32[256,512]{1,0:T(8,128)S(1)}, u32[]{:S(2)}, u32[]{:S(2)}) collective-permute-start(f32[256,512]{1,0:T(8,128)} %copy-done.13), channel_id=1, source_target_pairs={{0,1},{1,0},{2,3},{3,2},{4,5},{5,4},{6,7},{7,6},{8,9},{9,8},{10,11... | collective-permute-start | bytes 1572872 | tf_op jit(solution)/shard_map/ppermute | solution.py:330
  101.7 7.5 %collective-permute-start.15 = (f32[512,512]{1,0:T(8,128)}, f32[512,512]{1,0:T(8,128)}, u32[]{:S(2)}, u32[]{:S(2)}) collective-permute-start(f32[512,512]{1,0:T(8,128)} %collective-permute-done.refs_2_), channel_id=1, source_target_pairs={{0,1},{1,0},{2,3},{3,2},{4,5},{5,4},{6,7},{7,6},{8,9},{9,8},{10,11... | collective-permute-start | bytes 3145736 | tf_op jit(solution)/shard_map/ppermute | solution.py:330
  103.7 5.6 %collective-permute-start.17 = (f32[512,512]{1,0:T(8,128)}, f32[512,512]{1,0:T(8,128)S(1)}, u32[]{:S(2)}, u32[]{:S(2)}) collective-permute-start(f32[512,512]{1,0:T(8,128)} %copy-done.9), channel_id=1, source_target_pairs={{0,1},{1,0},{2,3},{3,2},{4,5},{5,4},{6,7},{7,6},{8,9},{9,8},{10,11... | collective-permute-start | bytes 3145736 | tf_op jit(solution)/shard_map/ppermute | solution.py:330
  104.2 4.1 %collective-permute-start.28 = (f32[256,512]{1,0:T(8,128)}, f32[256,512]{1,0:T(8,128)S(1)}, u32[]{:S(2)}, u32[]{:S(2)}) collective-permute-start(f32[256,512]{1,0:T(8,128)} %copy-done.14), channel_id=1, source_target_pairs={{0,1},{1,0},{2,3},{3,2},{4,5},{5,4},{6,7},{7,6},{8,9},{9,8},{10,11... | collective-permute-start | bytes 1572872 | tf_op jit(solution)/shard_map/ppermute | solution.py:330
  104.4 4.2 %collective-permute-start.26 = (f32[256,512]{1,0:T(8,128)S(1)}, f32[256,512]{1,0:T(8,128)S(1)}, u32[]{:S(2)}, u32[]{:S(2)}) collective-permute-start(f32[256,512]{1,0:T(8,128)S(1)} %get-tuple-element.58.refs_13_), channel_id=1, source_target_pairs={{0,1},{1,0},{2,3},{3,2},{4,5},{5,4},{6,7},{7,6},{8,9},{9,8},{10,11... | collective-permute-start | bytes 1572872 | tf_op jit(solution)/shard_map/ppermute | solution.py:330
  108.7 4.1 %collective-permute-start.21 = (f32[512,512]{1,0:T(8,128)}, f32[512,512]{1,0:T(8,128)}, u32[]{:S(2)}, u32[]{:S(2)}) collective-permute-start(f32[512,512]{1,0:T(8,128)} %collective-permute-done.3.refs_8_), channel_id=1, source_target_pairs={{0,1},{1,0},{2,3},{3,2},{4,5},{5,4},{6,7},{7,6},{8,9},{9,8},{10,11... | collective-permute-start | bytes 3145736 | tf_op jit(solution)/shard_map/ppermute | solution.py:330
  108.9 5.5 %collective-permute-start.23 = (f32[512,512]{1,0:T(8,128)}, f32[512,512]{1,0:T(8,128)}, u32[]{:S(2)}, u32[]{:S(2)}) collective-permute-start(f32[512,512]{1,0:T(8,128)} %collective-permute-done.7.refs_10_), channel_id=1, source_target_pairs={{0,1},{1,0},{2,3},{3,2},{4,5},{5,4},{6,7},{7,6},{8,9},{9,8},{10,11... | collective-permute-start | bytes 3145736 | tf_op jit(solution)/shard_map/ppermute | solution.py:330
  109.2 6.6 %collective-permute-start.25 = (f32[512,512]{1,0:T(8,128)}, f32[512,512]{1,0:T(8,128)}, u32[]{:S(2)}, u32[]{:S(2)}) collective-permute-start(f32[512,512]{1,0:T(8,128)} %collective-permute-done.8.refs_12_), channel_id=1, source_target_pairs={{0,1},{1,0},{2,3},{3,2},{4,5},{5,4},{6,7},{7,6},{8,9},{9,8},{10,11... | collective-permute-start | bytes 3145736 | tf_op jit(solution)/shard_map/ppermute | solution.py:330
  109.4 7.9 %collective-permute-start.27 = (f32[512,512]{1,0:T(8,128)}, f32[512,512]{1,0:T(8,128)}, u32[]{:S(2)}, u32[]{:S(2)}) collective-permute-start(f32[512,512]{1,0:T(8,128)} %collective-permute-done.9.refs_14_), channel_id=1, source_target_pairs={{0,1},{1,0},{2,3},{3,2},{4,5},{5,4},{6,7},{7,6},{8,9},{9,8},{10,11... | collective-permute-start | bytes 3145736 | tf_op jit(solution)/shard_map/ppermute | solution.py:330
  136.2 20.3 %collective-permute-start.29 = (f32[3,256,256]{2,1,0:T(8,128)}, f32[3,256,256]{2,1,0:T(8,128)S(1)}, u32[]{:S(2)}, u32[]{:S(2)}) collective-permute-start(f32[3,256,256]{2,1,0:T(8,128)} %get-tuple-element.51), channel_id=1, source_target_pairs={{0,16},{16,0},{32,48},{48,32},{1,17},{17,1},{33,49},{49,33},{2,18}... | collective-permute-start | bytes 2359304 | tf_op jit(solution)/shard_map/ppermute | solution.py:387
  157.7 21.3 %collective-permute-start.30 = (f32[3,256,256]{2,1,0:T(8,128)S(1)}, f32[3,256,256]{2,1,0:T(8,128)S(1)}, u32[]{:S(2)}, u32[]{:S(2)}) collective-permute-start(f32[3,256,256]{2,1,0:T(8,128)S(1)} %add.226), channel_id=1, source_target_pairs={{0,32},{16,48},{32,0},{48,16},{1,33},{17,49},{33,1},{49,17},{2,34}... | collective-permute-start | bytes 2359304 | tf_op jit(solution)/shard_map/ppermute | solution.py:387
  179.1 53.5 %collective-permute-start.31 = (f32[3,256,256]{2,1,0:T(8,128)S(1)}, f32[3,256,256]{2,1,0:T(8,128)S(1)}, u32[]{:S(2)}, u32[]{:S(2)}) collective-permute-start(f32[3,256,256]{2,1,0:T(8,128)S(1)} %add.227), channel_id=1, source_target_pairs={{0,64},{64,0},{1,65},{65,1},{2,66},{66,2},{3,67},{67,3},{4,68},{68... | collective-permute-start | bytes 2359304 | tf_op jit(solution)/shard_map/ppermute | solution.py:330
  226.3 18.5 %all-to-all-start.1 = ((f32[8,96,256]{2,1,0:T(8,128)}), f32[8,96,256]{2,1,0:T(8,128)S(1)}, u32[]{:S(2)}, u32[]{:S(2)}) async-start(f32[8,96,256]{2,1,0:T(8,128)} %bitcast.36), calls=%async_computation.1 | async-start | bytes 1572864 | tf_op jit(solution)/shard_map/all_to_all | solution.py:305
  245.8 15.8 %all-to-all-start.2 = ((f32[8,96,256]{2,1,0:T(8,128)}), f32[8,96,256]{2,1,0:T(8,128)S(1)}, u32[]{:S(2)}, u32[]{:S(2)}) async-start(f32[8,96,256]{2,1,0:T(8,128)} %broadcast_in_dim.19), calls=%async_computation.2 | async-start | bytes 1572864 | tf_op jit(solution)/shard_map/all_to_all | solution.py:312
  (26 other events, 358.1 us)

commit v7 on v6

--- a/solution.py
+++ b/solution.py
@@ -31,6 +31,7 @@
 
 SLOTS = 4
 LIMIT = pltpu.CompilerParams(vmem_limit_bytes=60 * 2**20)
+SMALLER = pltpu.CompilerParams(vmem_limit_bytes=48 * 2**20)
 
 
 def fetch_pieces(pieces, k, v_buf, v_sems):
@@ -131,12 +132,17 @@
         w_ref[...] += split_triple((v_buf[slot, 0], v_buf[slot, 1]), halves(e_buf[slot]), ((1,), (0,)))
 
 
-def apply_kernel(places, e_ref, m_ref, w_ref, v_ref, o_ref, e_buf, v_buf, o_buf, y_ref, e_sems, v_sems, o_sems):
+def apply_kernel(
+    places, e_ref, m_ref, w_ref, v_ref, o_ref, w_buf, e_buf, v_buf, o_buf, y_ref, w_sem, e_sems, v_sems, o_sems
+):
     blocks = v_ref.shape[0]
     depth = e_buf.shape[1]
+    sums = pltpu.make_async_copy(w_ref, w_buf, w_sem)
+    sums.start()
     for k in range(SLOTS - 1):
         fetch_block(places, k, e_ref, e_buf, e_sems, v_ref, v_buf, v_sems)
-    y_ref[0], y_ref[1] = halves(triple(m_ref[...], w_ref[...], ((1,), (0,))))
+    sums.wait()
+    y_ref[0], y_ref[1] = halves(triple(m_ref[...], w_buf[...], ((1,), (0,))))
 
     def leave(k):
         slot = lax.rem(k, SLOTS)
@@ -223,19 +229,21 @@
     width = block.shape[1]
     return pl.pallas_call(
         apply_kernel,
-        in_specs=[SCALARS, FAR, NEAR, NEAR, FAR],
+        in_specs=[SCALARS, FAR, NEAR, pl.BlockSpec(memory_space=pl.ANY), FAR],
         out_specs=FAR,
         out_shape=jax.ShapeDtypeStruct(block.shape, jnp.float32),
         scratch_shapes=[
+            pltpu.VMEM((count, width), jnp.float32),
             pltpu.VMEM((SLOTS, depth, width), jnp.float32),
             pltpu.VMEM((SLOTS, 2, count, depth), jnp.bfloat16),
             pltpu.VMEM((SLOTS, depth, width), jnp.float32),
             pltpu.VMEM((2, count, width), jnp.bfloat16),
+            pltpu.SemaphoreType.DMA,
             pltpu.SemaphoreType.DMA((SLOTS,)),
             pltpu.SemaphoreType.DMA((SLOTS,)),
             pltpu.SemaphoreType.DMA((SLOTS,)),
         ],
-        compiler_params=LIMIT,
+        compiler_params=SMALLER,
         cost_estimate=cost(blocks, count, depth, width, 2),
     )(places, block, mixer, w, vectors)
 
@@ -263,7 +271,7 @@
         in_specs=[NEAR, NEAR],
         out_specs=NEAR,
         out_shape=jax.ShapeDtypeStruct((size, size), jnp.float32),
-        compiler_params=LIMIT,
+        compiler_params=SMALLER,
     )(tri_factors, gram)
 
 

time: 281 us -> 279 us (level)
  Pallas kernels: 63.1 us -> 59.1 us
  transfers between devices with their start and end apart: 35 -> 35, of which waited for: 19 -> 19; matrix products, arithmetic and copies ran while one was open for 1% -> 1% of each run, Pallas kernels for 16% -> 15%
where the time goes in v7:
time: 279 us; the launch traced here: 278 us
  waiting for transfers between devices  155 us (56%)
  Pallas kernels  59.1 us (21%)
  starting transfers between devices  54.5 us (20%)
  local copies, waits for them, and re-layouts  4.51 us (2%)
  other arithmetic  4.32 us (2%)
    ppermute x9, waiting for transfers between devices, send(): return lax.ppermute(piece, ('x', 'core'), turn(sign))  47.9 us
    ppermute x2, waiting for transfers between devices, on_device(): gram = gram + lax.ppermute(gram, 'z', [(i, i ^ step) for i in range(size)])  35 us
    all_to_all x1, waiting for transfers between devices, on_device(): block = lax.all_to_all(block, COL, split_axis=0, concat_axis=0, tiled=True)  29.6 us
    ppermute x21, waiting for transfers between devices, swap(): return lax.ppermute(piece, axis, [(0, 1), (1, 0)])  21.2 us
    pallas_call x1, Pallas kernels, gram_of(): pl.pallas_call(functools.partial(gram_kernel, blocks, size), in_specs=[FA...  18.8 us
    ppermute x21, starting transfers between devices, swap(): return lax.ppermute(piece, axis, [(0, 1), (1, 0)])  18.8 us
    pallas_call x1, Pallas kernels, apply(): pl.pallas_call(apply_kernel, in_specs=[SCALARS, FAR, NEAR, pl.BlockSpec(m...  16.5 us
    pallas_call x1, Pallas kernels, project(): pl.pallas_call(project_kernel, in_specs=[SCALARS, FAR, FAR], out_specs=NE...  15.8 us
  transfers between devices with their start and end apart: 35, of which 19 were waited for; matrix products, arithmetic and copies ran while one was open for 1% of the time, Pallas kernels for 15%

profile of v7, /device:TPU:2, one launch (start us, length us, event | category | flops | bytes accessed | tf_op | source)
XLA Modules:
  0.0 278.2 jit_solution(17992314859781626777)
XLA Ops:
  0.0 1.6 fusion
  2.3 3.3 %collective-permute-start.3 = (f32[512,512]{1,0:T(8,128)S(1)}, f32[512,512]{1,0:T(8,128)}, u32[]{:S(2)}, u32[]{:S(2)}) collective-permute-start(f32[512,512]{1,0:T(8,128)S(1)} %pad_maximum_fusion.refs_0_), channel_id=1, source_target_pairs={{0,8},{8,0},{1,9},{9,1},{2,10},{10,2},{3,11},{11,3},{4,12},{12,4},... | collective-permute-start | bytes 3145736 | tf_op jit(solution)/shard_map/ppermute | solution.py:338
  8.3 12.8 %collective-permute-done.1.refs_3_ = f32[256,512]{1,0:T(8,128)S(1)} collective-permute-done((f32[256,512]{1,0:T(8,128)S(1)}, f32[256,512]{1,0:T(8,128)S(1)}, u32[]{:S(2)}, u32[]{:S(2)}) %collective-permute-start.1) | collective-permute-done | bytes 524320 | tf_op jit(solution)/shard_map/ppermute | solution.py:334
  23.4 9.9 %collective-permute-done.2.refs_5_ = f32[256,512]{1,0:T(8,128)} collective-permute-done((f32[256,512]{1,0:T(8,128)S(1)}, f32[256,512]{1,0:T(8,128)}, u32[]{:S(2)}, u32[]{:S(2)}) %collective-permute-start.2) | collective-permute-done | bytes 524320 | tf_op jit(solution)/shard_map/ppermute | solution.py:334
  33.3 1.9 collective-permute-start.7
  35.4 6.1 %collective-permute-start.12 = (f32[256,512]{1,0:T(8,128)S(1)}, f32[256,512]{1,0:T(8,128)S(1)}, u32[]{:S(2)}, u32[]{:S(2)}) collective-permute-start(f32[256,512]{1,0:T(8,128)S(1)} %collective-permute-done.6.refs_7_), channel_id=1, source_target_pairs={{0,8},{8,0},{1,9},{9,1},{2,10},{10,2},{3,11},{11,3},{4,12},{12,4},... | collective-permute-start | bytes 1572872 | tf_op jit(solution)/shard_map/ppermute | solution.py:338
  42.7 6.6 %collective-permute-done.refs_2_ = f32[512,512]{1,0:T(8,128)} collective-permute-done((f32[512,512]{1,0:T(8,128)S(1)}, f32[512,512]{1,0:T(8,128)}, u32[]{:S(2)}, u32[]{:S(2)}) %collective-permute-start) | collective-permute-done | bytes 1048608 | tf_op jit(solution)/shard_map/ppermute | solution.py:334
  49.3 2.6 collective-permute-start.5
  51.9 14.2 %collective-permute-done.7.refs_10_ = f32[512,512]{1,0:T(8,128)} collective-permute-done((f32[512,512]{1,0:T(8,128)}, f32[512,512]{1,0:T(8,128)}, u32[]{:S(2)}, u32[]{:S(2)}) %collective-permute-start.7) | collective-permute-done | bytes 1048608 | tf_op jit(solution)/shard_map/ppermute | solution.py:334
  68.5 3.2 %collective-permute-start.10 = (f32[256,512]{1,0:T(8,128)S(1)}, f32[256,512]{1,0:T(8,128)}, u32[]{:S(2)}, u32[]{:S(2)}) collective-permute-start(f32[256,512]{1,0:T(8,128)S(1)} %get-tuple-element.34.refs_1_), channel_id=1, source_target_pairs={{0,8},{8,0},{1,9},{9,1},{2,10},{10,2},{3,11},{11,3},{4,12},{12,4},... | collective-permute-start | bytes 1572872 | tf_op jit(solution)/shard_map/ppermute | solution.py:338
  71.7 6.7 %shard_map.37 = f32[8192,256]{1,0:T(8,128)} custom-call(f32[512,4096]{1,0:T(8,128)} %e_ref.1), custom_call_target="tpu_custom_call" | custom-call | bytes 16777216 | tf_op jit(solution)/shard_map/pallas_call | solution.py:297
  78.3 6.0 %collective-permute-done.10.refs_9_ = f32[256,512]{1,0:T(8,128)} collective-permute-done((f32[256,512]{1,0:T(8,128)S(1)}, f32[256,512]{1,0:T(8,128)}, u32[]{:S(2)}, u32[]{:S(2)}) %collective-permute-start.10) | collective-permute-done | bytes 524320 | tf_op jit(solution)/shard_map/ppermute | solution.py:338
  84.3 4.3 %collective-permute-done.9.refs_14_ = f32[512,512]{1,0:T(8,128)} collective-permute-done((f32[512,512]{1,0:T(8,128)}, f32[512,512]{1,0:T(8,128)}, u32[]{:S(2)}, u32[]{:S(2)}) %collective-permute-start.9) | collective-permute-done | bytes 1048608 | tf_op jit(solution)/shard_map/ppermute | solution.py:334
  88.6 8.2 %all-to-all-start = ((f32[16,512,256]{2,1,0:T(8,128)}), f32[16,512,256]{2,1,0:T(8,128)}, u32[]{:S(2)}, u32[]{:S(2)}) async-start(f32[16,512,256]{2,1,0:T(8,128)} %bitcast.35), calls=%async_computation | async-start | bytes 16777216 | tf_op jit(solution)/shard_map/all_to_all | solution.py:388
  98.1 3.3 %collective-permute-done.14.refs_17_ = f32[256,512]{1,0:T(8,128)S(1)} collective-permute-done((f32[256,512]{1,0:T(8,128)S(1)}, f32[256,512]{1,0:T(8,128)S(1)}, u32[]{:S(2)}, u32[]{:S(2)}) %collective-permute-start.14) | collective-permute-done | bytes 524320 | tf_op jit(solution)/shard_map/ppermute | solution.py:338
  104.9 3.4 %collective-permute-done.28.refs_31_ = f32[256,512]{1,0:T(8,128)S(1)} collective-permute-done((f32[256,512]{1,0:T(8,128)}, f32[256,512]{1,0:T(8,128)S(1)}, u32[]{:S(2)}, u32[]{:S(2)}) %collective-permute-start.28) | collective-permute-done | bytes 524320 | tf_op jit(solution)/shard_map/ppermute | solution.py:338
  111.2 1.6 collective-permute-done.21.refs_24_
  112.8 1.5 collective-permute-done.23.refs_26_
  114.3 1.5 collective-permute-done.25.refs_28_
  117.4 18.8 %shard_map.38 = (f32[3,256,256]{2,1,0:T(8,128)}, bf16[16,2,768,512]{3,2,1,0:T(8,128)(2,1)}) custom-call(f32[512,512]{1,0:T(8,128)} %copy-done.2, f32[256,512]{1,0:T(8,128)} %copy-done.3, f32[512,512]{1,0:T(8,128)} %collective-permute-done.refs_2_, f32[256,512]{1,0:T(8,128)} %copy-done.5, f32[512,512]{1,0:T(8,128)} %collective-permute-done.4.refs_4_, ...), custom_call_target="tpu_custom_call" | custom-call | flops 9663676416 | bytes 25165824 | tf_op jit(solution)/shard_map/pallas_call | solution.py:189
  136.2 2.1 collective-permute-start.29
  138.2 18.3 %collective-permute-done.29 = f32[3,256,256]{2,1,0:T(8,128)S(1)} collective-permute-done((f32[3,256,256]{2,1,0:T(8,128)}, f32[3,256,256]{2,1,0:T(8,128)S(1)}, u32[]{:S(2)}, u32[]{:S(2)}) %collective-permute-start.29) | collective-permute-done | bytes 786464 | tf_op jit(solution)/shard_map/ppermute | solution.py:395
  157.7 3.8 %collective-permute-start.30 = (f32[3,256,256]{2,1,0:T(8,128)S(1)}, f32[3,256,256]{2,1,0:T(8,128)S(1)}, u32[]{:S(2)}, u32[]{:S(2)}) collective-permute-start(f32[3,256,256]{2,1,0:T(8,128)S(1)} %add.226), channel_id=1, source_target_pairs={{0,32},{16,48},{32,0},{48,16},{1,33},{17,49},{33,1},{49,17},{2,34}... | collective-permute-start | bytes 2359304 | tf_op jit(solution)/shard_map/ppermute | solution.py:395
  162.1 16.7 %collective-permute-done.30 = f32[3,256,256]{2,1,0:T(8,128)S(1)} collective-permute-done((f32[3,256,256]{2,1,0:T(8,128)S(1)}, f32[3,256,256]{2,1,0:T(8,128)S(1)}, u32[]{:S(2)}, u32[]{:S(2)}) %collective-permute-start.30) | collective-permute-done | bytes 786464 | tf_op jit(solution)/shard_map/ppermute | solution.py:395
  179.0 1.8 collective-permute-start.31
  180.8 29.6 %all-to-all-done = f32[16,512,256]{2,1,0:T(8,128)} async-done(((f32[16,512,256]{2,1,0:T(8,128)}), f32[16,512,256]{2,1,0:T(8,128)}, u32[]{:S(2)}, u32[]{:S(2)}) %all-to-all-start) | async-done | bytes 8388640 | tf_op jit(solution)/shard_map/all_to_all | solution.py:388
  210.4 15.8 %shard_map.39 = f32[768,256]{1,0:T(8,128)} custom-call(s32[16]{0:T(128)} %stack.67.places, f32[8192,256]{1,0:T(8,128)} %bitcast.20.e_ref, bf16[16,2,768,512]{3,2,1,0:T(8,128)(2,1)} %get-tuple-element.52.v_ref), custom_call_target="tpu_custom_call" | custom-call | flops 9663676416 | bytes 8388608 | tf_op jit(solution)/shard_map/pallas_call | solution.py:211
  226.3 6.4 %all-to-all-start.1 = ((f32[8,96,256]{2,1,0:T(8,128)}), f32[8,96,256]{2,1,0:T(8,128)S(1)}, u32[]{:S(2)}, u32[]{:S(2)}) async-start(f32[8,96,256]{2,1,0:T(8,128)} %bitcast.36), calls=%async_computation.1 | async-start | bytes 1572864 | tf_op jit(solution)/shard_map/all_to_all | solution.py:313
  232.7 12.1 %all-to-all-done.1 = f32[8,96,256]{2,1,0:T(8,128)S(1)} async-done(((f32[8,96,256]{2,1,0:T(8,128)}), f32[8,96,256]{2,1,0:T(8,128)S(1)}, u32[]{:S(2)}, u32[]{:S(2)}) %all-to-all-start.1) | async-done | bytes 786464 | tf_op jit(solution)/shard_map/all_to_all | solution.py:313
  245.8 3.6 %all-to-all-start.2 = ((f32[8,96,256]{2,1,0:T(8,128)}), f32[8,96,256]{2,1,0:T(8,128)S(1)}, u32[]{:S(2)}, u32[]{:S(2)}) async-start(f32[8,96,256]{2,1,0:T(8,128)} %broadcast_in_dim.19), calls=%async_computation.2 | async-start | bytes 1572864 | tf_op jit(solution)/shard_map/all_to_all | solution.py:320
  252.0 9.6 %all-to-all-done.2 = f32[8,96,256]{2,1,0:T(8,128)S(1)} async-done(((f32[8,96,256]{2,1,0:T(8,128)}), f32[8,96,256]{2,1,0:T(8,128)S(1)}, u32[]{:S(2)}, u32[]{:S(2)}) %all-to-all-start.2) | async-done | bytes 786464 | tf_op jit(solution)/shard_map/all_to_all | solution.py:320
  261.6 16.5 %shard_map.41 = f32[8192,256]{1,0:T(8,128)} custom-call(s32[16]{0:T(128)S(1)} %copy-done.1, f32[8192,256]{1,0:T(8,128)} %bitcast.20.e_ref, f32[768,768]{1,0:T(8,128)S(1)} %shard_map.40.m_ref, f32[768,256]{1,0:T(8,128)S(1)} %bitcast.34, bf16[16,2,768,512]{3,2,1,0:T(8,128)(2,1)} %get-tuple-element.52.v_ref), custom_call_target="tpu_custom_call" | custom-call | flops 9663676416 | bytes 16777216 | tf_op jit(solution)/shard_map/pallas_call | solution.py:230
  (98 shorter events, 24.1 us)
Async XLA Ops:
  1.8 31.5 %collective-permute-start.4 = (f32[512,512]{1,0:T(8,128)S(1)}, f32[512,512]{1,0:T(8,128)}, u32[]{:S(2)}, u32[]{:S(2)}) collective-permute-start(f32[512,512]{1,0:T(8,128)S(1)} %pad_maximum_fusion.refs_0_), channel_id=1, source_target_pairs={{0,6},{1,3},{2,0},{3,5},{4,2},{5,7},{6,4},{7,1},{8,14},{9,11},{10,... | collective-permute-start | bytes 3145736 | tf_op jit(solution)/shard_map/ppermute | solution.py:334
  2.3 31.0 %collective-permute-start.3 = (f32[512,512]{1,0:T(8,128)S(1)}, f32[512,512]{1,0:T(8,128)}, u32[]{:S(2)}, u32[]{:S(2)}) collective-permute-start(f32[512,512]{1,0:T(8,128)S(1)} %pad_maximum_fusion.refs_0_), channel_id=1, source_target_pairs={{0,8},{8,0},{1,9},{9,1},{2,10},{10,2},{3,11},{11,3},{4,12},{12,4},... | collective-permute-start | bytes 3145736 | tf_op jit(solution)/shard_map/ppermute | solution.py:338
  5.6 15.6 %collective-permute-start.1 = (f32[256,512]{1,0:T(8,128)S(1)}, f32[256,512]{1,0:T(8,128)S(1)}, u32[]{:S(2)}, u32[]{:S(2)}) collective-permute-start(f32[256,512]{1,0:T(8,128)S(1)} %get-tuple-element.34.refs_1_), channel_id=1, source_target_pairs={{0,2},{1,7},{2,4},{3,1},{4,6},{5,3},{6,0},{7,5},{8,10},{9,15},{10,... | collective-permute-start | bytes 1572872 | tf_op jit(solution)/shard_map/ppermute | solution.py:334
  7.0 26.2 %collective-permute-start.2 = (f32[256,512]{1,0:T(8,128)S(1)}, f32[256,512]{1,0:T(8,128)}, u32[]{:S(2)}, u32[]{:S(2)}) collective-permute-start(f32[256,512]{1,0:T(8,128)S(1)} %get-tuple-element.34.refs_1_), channel_id=1, source_target_pairs={{0,6},{1,3},{2,0},{3,5},{4,2},{5,7},{6,4},{7,1},{8,14},{9,11},{10,... | collective-permute-start | bytes 1572872 | tf_op jit(solution)/shard_map/ppermute | solution.py:334
  21.2 12.1 %collective-permute-start.6 = (f32[256,512]{1,0:T(8,128)S(1)}, f32[256,512]{1,0:T(8,128)S(1)}, u32[]{:S(2)}, u32[]{:S(2)}) collective-permute-start(f32[256,512]{1,0:T(8,128)S(1)} %collective-permute-done.1.refs_3_), channel_id=1, source_target_pairs={{0,2},{1,7},{2,4},{3,1},{4,6},{5,3},{6,0},{7,5},{8,10},{9,15},{10,... | collective-permute-start | bytes 1572872 | tf_op jit(solution)/shard_map/ppermute | solution.py:334
  21.9 27.4 %collective-permute-start = (f32[512,512]{1,0:T(8,128)S(1)}, f32[512,512]{1,0:T(8,128)}, u32[]{:S(2)}, u32[]{:S(2)}) collective-permute-start(f32[512,512]{1,0:T(8,128)S(1)} %pad_maximum_fusion.refs_0_), channel_id=1, source_target_pairs={{0,2},{1,7},{2,4},{3,1},{4,6},{5,3},{6,0},{7,5},{8,10},{9,15},{10,... | collective-permute-start | bytes 3145736 | tf_op jit(solution)/shard_map/ppermute | solution.py:334
  33.3 32.9 %collective-permute-start.7 = (f32[512,512]{1,0:T(8,128)}, f32[512,512]{1,0:T(8,128)}, u32[]{:S(2)}, u32[]{:S(2)}) collective-permute-start(f32[512,512]{1,0:T(8,128)} %collective-permute-done.3.refs_8_), channel_id=1, source_target_pairs={{0,2},{1,7},{2,4},{3,1},{4,6},{5,3},{6,0},{7,5},{8,10},{9,15},{10,... | collective-permute-start | bytes 3145736 | tf_op jit(solution)/shard_map/ppermute | solution.py:334
  35.1 49.2 %collective-permute-start.8 = (f32[512,512]{1,0:T(8,128)}, f32[512,512]{1,0:T(8,128)}, u32[]{:S(2)}, u32[]{:S(2)}) collective-permute-start(f32[512,512]{1,0:T(8,128)} %collective-permute-done.3.refs_8_), channel_id=1, source_target_pairs={{0,6},{1,3},{2,0},{3,5},{4,2},{5,7},{6,4},{7,1},{8,14},{9,11},{10,... | collective-permute-start | bytes 3145736 | tf_op jit(solution)/shard_map/ppermute | solution.py:334
  35.4 32.3 %collective-permute-start.12 = (f32[256,512]{1,0:T(8,128)S(1)}, f32[256,512]{1,0:T(8,128)S(1)}, u32[]{:S(2)}, u32[]{:S(2)}) collective-permute-start(f32[256,512]{1,0:T(8,128)S(1)} %collective-permute-done.6.refs_7_), channel_id=1, source_target_pairs={{0,8},{8,0},{1,9},{9,1},{2,10},{10,2},{3,11},{11,3},{4,12},{12,4},... | collective-permute-start | bytes 1572872 | tf_op jit(solution)/shard_map/ppermute | solution.py:338
  42.6 41.7 %collective-permute-start.11 = (f32[512,512]{1,0:T(8,128)S(1)}, f32[512,512]{1,0:T(8,128)S(1)}, u32[]{:S(2)}, u32[]{:S(2)}) collective-permute-start(f32[512,512]{1,0:T(8,128)S(1)} %pad_maximum_fusion.1), channel_id=1, source_target_pairs={{0,8},{8,0},{1,9},{9,1},{2,10},{10,2},{3,11},{11,3},{4,12},{12,4},... | collective-permute-start | bytes 3145736 | tf_op jit(solution)/shard_map/ppermute | solution.py:338
  49.3 35.0 %collective-permute-start.5 = (f32[512,512]{1,0:T(8,128)}, f32[512,512]{1,0:T(8,128)}, u32[]{:S(2)}, u32[]{:S(2)}) collective-permute-start(f32[512,512]{1,0:T(8,128)} %collective-permute-done.refs_2_), channel_id=1, source_target_pairs={{0,2},{1,7},{2,4},{3,1},{4,6},{5,3},{6,0},{7,5},{8,10},{9,15},{10,... | collective-permute-start | bytes 3145736 | tf_op jit(solution)/shard_map/ppermute | solution.py:334
  66.2 22.5 %collective-permute-start.9 = (f32[512,512]{1,0:T(8,128)}, f32[512,512]{1,0:T(8,128)}, u32[]{:S(2)}, u32[]{:S(2)}) collective-permute-start(f32[512,512]{1,0:T(8,128)} %collective-permute-done.7.refs_10_), channel_id=1, source_target_pairs={{0,2},{1,7},{2,4},{3,1},{4,6},{5,3},{6,0},{7,5},{8,10},{9,15},{10,... | collective-permute-start | bytes 3145736 | tf_op jit(solution)/shard_map/ppermute | solution.py:334
  68.5 15.9 %collective-permute-start.10 = (f32[256,512]{1,0:T(8,128)S(1)}, f32[256,512]{1,0:T(8,128)}, u32[]{:S(2)}, u32[]{:S(2)}) collective-permute-start(f32[256,512]{1,0:T(8,128)S(1)} %get-tuple-element.34.refs_1_), channel_id=1, source_target_pairs={{0,8},{8,0},{1,9},{9,1},{2,10},{10,2},{3,11},{11,3},{4,12},{12,4},... | collective-permute-start | bytes 1572872 | tf_op jit(solution)/shard_map/ppermute | solution.py:338
  88.6 121.8 %all-to-all-start = ((f32[16,512,256]{2,1,0:T(8,128)}), f32[16,512,256]{2,1,0:T(8,128)}, u32[]{:S(2)}, u32[]{:S(2)}) async-start(f32[16,512,256]{2,1,0:T(8,128)} %bitcast.35), calls=%async_computation | async-start | bytes 16777216 | tf_op jit(solution)/shard_map/all_to_all | solution.py:388
  96.8 4.9 %collective-permute-start.13 = (f32[512,512]{1,0:T(8,128)S(1)}, f32[512,512]{1,0:T(8,128)S(1)}, u32[]{:S(2)}, u32[]{:S(2)}) collective-permute-start(f32[512,512]{1,0:T(8,128)S(1)} %pad_maximum_fusion.refs_0_), channel_id=1, source_target_pairs={{0,1},{1,0},{2,3},{3,2},{4,5},{5,4},{6,7},{7,6},{8,9},{9,8},{10,11... | collective-permute-start | bytes 3145736 | tf_op jit(solution)/shard_map/ppermute | solution.py:338
  97.0 4.3 %collective-permute-start.14 = (f32[256,512]{1,0:T(8,128)S(1)}, f32[256,512]{1,0:T(8,128)S(1)}, u32[]{:S(2)}, u32[]{:S(2)}) collective-permute-start(f32[256,512]{1,0:T(8,128)S(1)} %copy-done.4), channel_id=1, source_target_pairs={{0,1},{1,0},{2,3},{3,2},{4,5},{5,4},{6,7},{7,6},{8,9},{9,8},{10,11... | collective-permute-start | bytes 1572872 | tf_op jit(solution)/shard_map/ppermute | solution.py:338
  97.4 5.4 %collective-permute-start.16 = (f32[256,512]{1,0:T(8,128)S(1)}, f32[256,512]{1,0:T(8,128)S(1)}, u32[]{:S(2)}, u32[]{:S(2)}) collective-permute-start(f32[256,512]{1,0:T(8,128)S(1)} %copy-done.6), channel_id=1, source_target_pairs={{0,1},{1,0},{2,3},{3,2},{4,5},{5,4},{6,7},{7,6},{8,9},{9,8},{10,11... | collective-permute-start | bytes 1572872 | tf_op jit(solution)/shard_map/ppermute | solution.py:338
  97.6 6.6 %collective-permute-start.18 = (f32[256,512]{1,0:T(8,128)}, f32[256,512]{1,0:T(8,128)S(1)}, u32[]{:S(2)}, u32[]{:S(2)}) collective-permute-start(f32[256,512]{1,0:T(8,128)} %collective-permute-done.2.refs_5_), channel_id=1, source_target_pairs={{0,1},{1,0},{2,3},{3,2},{4,5},{5,4},{6,7},{7,6},{8,9},{9,8},{10,11... | collective-permute-start | bytes 1572872 | tf_op jit(solution)/shard_map/ppermute | solution.py:338
  97.9 6.5 %collective-permute-start.20 = (f32[256,512]{1,0:T(8,128)}, f32[256,512]{1,0:T(8,128)S(1)}, u32[]{:S(2)}, u32[]{:S(2)}) collective-permute-start(f32[256,512]{1,0:T(8,128)} %copy-done.12), channel_id=1, source_target_pairs={{0,1},{1,0},{2,3},{3,2},{4,5},{5,4},{6,7},{7,6},{8,9},{9,8},{10,11... | collective-permute-start | bytes 1572872 | tf_op jit(solution)/shard_map/ppermute | solution.py:338
  101.7 7.5 %collective-permute-start.15 = (f32[512,512]{1,0:T(8,128)}, f32[512,512]{1,0:T(8,128)}, u32[]{:S(2)}, u32[]{:S(2)}) collective-permute-start(f32[512,512]{1,0:T(8,128)} %collective-permute-done.refs_2_), channel_id=1, source_target_pairs={{0,1},{1,0},{2,3},{3,2},{4,5},{5,4},{6,7},{7,6},{8,9},{9,8},{10,11... | collective-permute-start | bytes 3145736 | tf_op jit(solution)/shard_map/ppermute | solution.py:338
  103.7 5.7 %collective-permute-start.17 = (f32[512,512]{1,0:T(8,128)}, f32[512,512]{1,0:T(8,128)S(1)}, u32[]{:S(2)}, u32[]{:S(2)}) collective-permute-start(f32[512,512]{1,0:T(8,128)} %collective-permute-done.4.refs_4_), channel_id=1, source_target_pairs={{0,1},{1,0},{2,3},{3,2},{4,5},{5,4},{6,7},{7,6},{8,9},{9,8},{10,11... | collective-permute-start | bytes 3145736 | tf_op jit(solution)/shard_map/ppermute | solution.py:338
  104.2 4.1 %collective-permute-start.28 = (f32[256,512]{1,0:T(8,128)}, f32[256,512]{1,0:T(8,128)S(1)}, u32[]{:S(2)}, u32[]{:S(2)}) collective-permute-start(f32[256,512]{1,0:T(8,128)} %copy-done.13), channel_id=1, source_target_pairs={{0,1},{1,0},{2,3},{3,2},{4,5},{5,4},{6,7},{7,6},{8,9},{9,8},{10,11... | collective-permute-start | bytes 1572872 | tf_op jit(solution)/shard_map/ppermute | solution.py:338
  104.4 4.3 %collective-permute-start.26 = (f32[256,512]{1,0:T(8,128)S(1)}, f32[256,512]{1,0:T(8,128)S(1)}, u32[]{:S(2)}, u32[]{:S(2)}) collective-permute-start(f32[256,512]{1,0:T(8,128)S(1)} %get-tuple-element.58.refs_13_), channel_id=1, source_target_pairs={{0,1},{1,0},{2,3},{3,2},{4,5},{5,4},{6,7},{7,6},{8,9},{9,8},{10,11... | collective-permute-start | bytes 1572872 | tf_op jit(solution)/shard_map/ppermute | solution.py:338
  108.7 4.1 %collective-permute-start.21 = (f32[512,512]{1,0:T(8,128)}, f32[512,512]{1,0:T(8,128)}, u32[]{:S(2)}, u32[]{:S(2)}) collective-permute-start(f32[512,512]{1,0:T(8,128)} %collective-permute-done.3.refs_8_), channel_id=1, source_target_pairs={{0,1},{1,0},{2,3},{3,2},{4,5},{5,4},{6,7},{7,6},{8,9},{9,8},{10,11... | collective-permute-start | bytes 3145736 | tf_op jit(solution)/shard_map/ppermute | solution.py:338
  108.9 5.5 %collective-permute-start.23 = (f32[512,512]{1,0:T(8,128)}, f32[512,512]{1,0:T(8,128)}, u32[]{:S(2)}, u32[]{:S(2)}) collective-permute-start(f32[512,512]{1,0:T(8,128)} %collective-permute-done.7.refs_10_), channel_id=1, source_target_pairs={{0,1},{1,0},{2,3},{3,2},{4,5},{5,4},{6,7},{7,6},{8,9},{9,8},{10,11... | collective-permute-start | bytes 3145736 | tf_op jit(solution)/shard_map/ppermute | solution.py:338
  109.2 6.6 %collective-permute-start.25 = (f32[512,512]{1,0:T(8,128)}, f32[512,512]{1,0:T(8,128)}, u32[]{:S(2)}, u32[]{:S(2)}) collective-permute-start(f32[512,512]{1,0:T(8,128)} %collective-permute-done.8.refs_12_), channel_id=1, source_target_pairs={{0,1},{1,0},{2,3},{3,2},{4,5},{5,4},{6,7},{7,6},{8,9},{9,8},{10,11... | collective-permute-start | bytes 3145736 | tf_op jit(solution)/shard_map/ppermute | solution.py:338
  109.4 7.9 %collective-permute-start.27 = (f32[512,512]{1,0:T(8,128)}, f32[512,512]{1,0:T(8,128)}, u32[]{:S(2)}, u32[]{:S(2)}) collective-permute-start(f32[512,512]{1,0:T(8,128)} %collective-permute-done.9.refs_14_), channel_id=1, source_target_pairs={{0,1},{1,0},{2,3},{3,2},{4,5},{5,4},{6,7},{7,6},{8,9},{9,8},{10,11... | collective-permute-start | bytes 3145736 | tf_op jit(solution)/shard_map/ppermute | solution.py:338
  136.2 20.3 %collective-permute-start.29 = (f32[3,256,256]{2,1,0:T(8,128)}, f32[3,256,256]{2,1,0:T(8,128)S(1)}, u32[]{:S(2)}, u32[]{:S(2)}) collective-permute-start(f32[3,256,256]{2,1,0:T(8,128)} %get-tuple-element.51), channel_id=1, source_target_pairs={{0,16},{16,0},{32,48},{48,32},{1,17},{17,1},{33,49},{49,33},{2,18}... | collective-permute-start | bytes 2359304 | tf_op jit(solution)/shard_map/ppermute | solution.py:395
  157.7 21.1 %collective-permute-start.30 = (f32[3,256,256]{2,1,0:T(8,128)S(1)}, f32[3,256,256]{2,1,0:T(8,128)S(1)}, u32[]{:S(2)}, u32[]{:S(2)}) collective-permute-start(f32[3,256,256]{2,1,0:T(8,128)S(1)} %add.226), channel_id=1, source_target_pairs={{0,32},{16,48},{32,0},{48,16},{1,33},{17,49},{33,1},{49,17},{2,34}... | collective-permute-start | bytes 2359304 | tf_op jit(solution)/shard_map/ppermute | solution.py:395
  179.0 53.7 %collective-permute-start.31 = (f32[3,256,256]{2,1,0:T(8,128)S(1)}, f32[3,256,256]{2,1,0:T(8,128)S(1)}, u32[]{:S(2)}, u32[]{:S(2)}) collective-permute-start(f32[3,256,256]{2,1,0:T(8,128)S(1)} %add.227), channel_id=1, source_target_pairs={{0,64},{64,0},{1,65},{65,1},{2,66},{66,2},{3,67},{67,3},{4,68},{68... | collective-permute-start | bytes 2359304 | tf_op jit(solution)/shard_map/ppermute | solution.py:338
  226.3 18.5 %all-to-all-start.1 = ((f32[8,96,256]{2,1,0:T(8,128)}), f32[8,96,256]{2,1,0:T(8,128)S(1)}, u32[]{:S(2)}, u32[]{:S(2)}) async-start(f32[8,96,256]{2,1,0:T(8,128)} %bitcast.36), calls=%async_computation.1 | async-start | bytes 1572864 | tf_op jit(solution)/shard_map/all_to_all | solution.py:313
  245.8 15.8 %all-to-all-start.2 = ((f32[8,96,256]{2,1,0:T(8,128)}), f32[8,96,256]{2,1,0:T(8,128)S(1)}, u32[]{:S(2)}, u32[]{:S(2)}) async-start(f32[8,96,256]{2,1,0:T(8,128)} %broadcast_in_dim.19), calls=%async_computation.2 | async-start | bytes 1572864 | tf_op jit(solution)/shard_map/all_to_all | solution.py:320
  (25 other events, 383.3 us)

commit v8 on v7

--- a/solution.py
+++ b/solution.py
@@ -30,8 +30,7 @@
 
 
 SLOTS = 4
-LIMIT = pltpu.CompilerParams(vmem_limit_bytes=60 * 2**20)
-SMALLER = pltpu.CompilerParams(vmem_limit_bytes=48 * 2**20)
+LIMIT = pltpu.CompilerParams(vmem_limit_bytes=48 * 2**20)
 
 
 def fetch_pieces(pieces, k, v_buf, v_sems):
@@ -243,7 +242,7 @@
             pltpu.SemaphoreType.DMA((SLOTS,)),
             pltpu.SemaphoreType.DMA((SLOTS,)),
         ],
-        compiler_params=SMALLER,
+        compiler_params=LIMIT,
         cost_estimate=cost(blocks, count, depth, width, 2),
     )(places, block, mixer, w, vectors)
 
@@ -271,7 +270,7 @@
         in_specs=[NEAR, NEAR],
         out_specs=NEAR,
         out_shape=jax.ShapeDtypeStruct((size, size), jnp.float32),
-        compiler_params=SMALLER,
+        compiler_params=LIMIT,
     )(tri_factors, gram)
 
 

time: 279 us -> 279 us (level)
  waiting for transfers between devices: 155 us -> 158 us
  transfers between devices with their start and end apart: 35 -> 35, of which waited for: 19 -> 21; matrix products, arithmetic and copies ran while one was open for 1% -> 1% of each run, Pallas kernels for 15% -> 15%
where the time goes in v8:
time: 279 us
  waiting for transfers between devices  158 us (57%)
  Pallas kernels  57.8 us (21%)
  starting transfers between devices  54.3 us (19%)
  local copies, waits for them, and re-layouts  5.44 us (2%)
  other arithmetic  3.28 us (1%)
    ppermute x9, waiting for transfers between devices, send(): return lax.ppermute(piece, ('x', 'core'), turn(sign))  49 us
    ppermute x2, waiting for transfers between devices, on_device(): gram = gram + lax.ppermute(gram, 'z', [(i, i ^ step) for i in range(size)])  35.5 us
    all_to_all x1, waiting for transfers between devices, on_device(): block = lax.all_to_all(block, COL, split_axis=0, concat_axis=0, tiled=True)  30.6 us
    ppermute x21, waiting for transfers between devices, swap(): return lax.ppermute(piece, axis, [(0, 1), (1, 0)])  20.7 us
    ppermute x21, starting transfers between devices, swap(): return lax.ppermute(piece, axis, [(0, 1), (1, 0)])  18.7 us
    pallas_call x1, Pallas kernels, gram_of(): pl.pallas_call(functools.partial(gram_kernel, blocks, size), in_specs=[FA...  17.6 us
    pallas_call x1, Pallas kernels, apply(): pl.pallas_call(apply_kernel, in_specs=[SCALARS, FAR, NEAR, pl.BlockSpec(m...  16.5 us
    pallas_call x1, Pallas kernels, project(): pl.pallas_call(project_kernel, in_specs=[SCALARS, FAR, FAR], out_specs=NE...  15.7 us
  transfers between devices with their start and end apart: 35, of which 21 were waited for; matrix products, arithmetic and copies ran while one was open for 1% of the time, Pallas kernels for 15%

profile of v8, /device:TPU:2, one launch (start us, length us, event | category | flops | bytes accessed | tf_op | source)
XLA Modules:
  0.0 278.8 jit_solution(6373676618878903560)
XLA Ops:
  0.0 1.7 fusion
  2.3 3.3 %collective-permute-start.3 = (f32[512,512]{1,0:T(8,128)S(1)}, f32[512,512]{1,0:T(8,128)S(1)}, u32[]{:S(2)}, u32[]{:S(2)}) collective-permute-start(f32[512,512]{1,0:T(8,128)S(1)} %pad_maximum_fusion.refs_0_), channel_id=1, source_target_pairs={{0,8},{8,0},{1,9},{9,1},{2,10},{10,2},{3,11},{11,3},{4,12},{12,4},... | collective-permute-start | bytes 3145736 | tf_op jit(solution)/shard_map/ppermute | solution.py:337
  8.3 12.8 %collective-permute-done.1.refs_3_ = f32[256,512]{1,0:T(8,128)S(1)} collective-permute-done((f32[256,512]{1,0:T(8,128)S(1)}, f32[256,512]{1,0:T(8,128)S(1)}, u32[]{:S(2)}, u32[]{:S(2)}) %collective-permute-start.1) | collective-permute-done | bytes 524320 | tf_op jit(solution)/shard_map/ppermute | solution.py:333
  23.4 9.8 %collective-permute-done.2.refs_5_ = f32[256,512]{1,0:T(8,128)S(1)} collective-permute-done((f32[256,512]{1,0:T(8,128)S(1)}, f32[256,512]{1,0:T(8,128)S(1)}, u32[]{:S(2)}, u32[]{:S(2)}) %collective-permute-start.2) | collective-permute-done | bytes 524320 | tf_op jit(solution)/shard_map/ppermute | solution.py:333
  33.2 1.9 collective-permute-start.7
  35.3 6.1 %collective-permute-start.12 = (f32[256,512]{1,0:T(8,128)S(1)}, f32[256,512]{1,0:T(8,128)S(1)}, u32[]{:S(2)}, u32[]{:S(2)}) collective-permute-start(f32[256,512]{1,0:T(8,128)S(1)} %collective-permute-done.6.refs_7_), channel_id=1, source_target_pairs={{0,8},{8,0},{1,9},{9,1},{2,10},{10,2},{3,11},{11,3},{4,12},{12,4},... | collective-permute-start | bytes 1572872 | tf_op jit(solution)/shard_map/ppermute | solution.py:337
  41.6 8.1 %collective-permute-done.refs_2_ = f32[512,512]{1,0:T(8,128)S(1)} collective-permute-done((f32[512,512]{1,0:T(8,128)S(1)}, f32[512,512]{1,0:T(8,128)S(1)}, u32[]{:S(2)}, u32[]{:S(2)}) %collective-permute-start) | collective-permute-done | bytes 1048608 | tf_op jit(solution)/shard_map/ppermute | solution.py:333
  49.7 2.5 collective-permute-start.5
  52.1 13.9 %collective-permute-done.7.refs_10_ = f32[512,512]{1,0:T(8,128)S(1)} collective-permute-done((f32[512,512]{1,0:T(8,128)S(1)}, f32[512,512]{1,0:T(8,128)S(1)}, u32[]{:S(2)}, u32[]{:S(2)}) %collective-permute-start.7) | collective-permute-done | bytes 1048608 | tf_op jit(solution)/shard_map/ppermute | solution.py:333
  67.5 3.2 %collective-permute-start.10 = (f32[256,512]{1,0:T(8,128)S(1)}, f32[256,512]{1,0:T(8,128)S(1)}, u32[]{:S(2)}, u32[]{:S(2)}) collective-permute-start(f32[256,512]{1,0:T(8,128)S(1)} %get-tuple-element.34.refs_1_), channel_id=1, source_target_pairs={{0,8},{8,0},{1,9},{9,1},{2,10},{10,2},{3,11},{11,3},{4,12},{12,4},... | collective-permute-start | bytes 1572872 | tf_op jit(solution)/shard_map/ppermute | solution.py:337
  70.7 6.7 %shard_map.37 = f32[8192,256]{1,0:T(8,128)} custom-call(f32[512,4096]{1,0:T(8,128)} %e_ref.1), custom_call_target="tpu_custom_call" | custom-call | bytes 16777216 | tf_op jit(solution)/shard_map/pallas_call | solution.py:296
  77.4 6.7 %collective-permute-done.10.refs_9_ = f32[256,512]{1,0:T(8,128)S(1)} collective-permute-done((f32[256,512]{1,0:T(8,128)S(1)}, f32[256,512]{1,0:T(8,128)S(1)}, u32[]{:S(2)}, u32[]{:S(2)}) %collective-permute-start.10) | collective-permute-done | bytes 524320 | tf_op jit(solution)/shard_map/ppermute | solution.py:337
  84.1 4.4 %collective-permute-done.9.refs_14_ = f32[512,512]{1,0:T(8,128)S(1)} collective-permute-done((f32[512,512]{1,0:T(8,128)S(1)}, f32[512,512]{1,0:T(8,128)S(1)}, u32[]{:S(2)}, u32[]{:S(2)}) %collective-permute-start.9) | collective-permute-done | bytes 1048608 | tf_op jit(solution)/shard_map/ppermute | solution.py:333
  89.5 8.0 %all-to-all-start = ((f32[16,512,256]{2,1,0:T(8,128)}), f32[16,512,256]{2,1,0:T(8,128)}, u32[]{:S(2)}, u32[]{:S(2)}) async-start(f32[16,512,256]{2,1,0:T(8,128)} %bitcast.35), calls=%async_computation | async-start | bytes 16777216 | tf_op jit(solution)/shard_map/all_to_all | solution.py:387
  98.7 1.9 collective-permute-done.14.refs_17_
  105.5 1.9 collective-permute-done.28.refs_31_
  107.7 1.9 collective-permute-done.26.refs_29_
  111.3 1.5 collective-permute-done.21.refs_24_
  115.8 1.5 collective-permute-done.27.refs_30_
  118.4 17.6 %shard_map.38 = (f32[3,256,256]{2,1,0:T(8,128)}, bf16[16,2,768,512]{3,2,1,0:T(8,128)(2,1)}) custom-call(f32[512,512]{1,0:T(8,128)} %copy-done.1, f32[256,512]{1,0:T(8,128)S(1)} %get-tuple-element.34.refs_1_, f32[512,512]{1,0:T(8,128)} %copy-done.3, f32[256,512]{1,0:T(8,128)S(1)} %collective-permute-done.1.refs_3_, ...), custom_call_target="tpu_custom_call" | custom-call | flops 9663676416 | bytes 25165824 | tf_op jit(solution)/shard_map/pallas_call | solution.py:188
  135.9 2.1 collective-permute-start.29
  138.0 18.3 %collective-permute-done.29 = f32[3,256,256]{2,1,0:T(8,128)S(1)} collective-permute-done((f32[3,256,256]{2,1,0:T(8,128)}, f32[3,256,256]{2,1,0:T(8,128)S(1)}, u32[]{:S(2)}, u32[]{:S(2)}) %collective-permute-start.29) | collective-permute-done | bytes 786464 | tf_op jit(solution)/shard_map/ppermute | solution.py:394
  157.5 4.0 %collective-permute-start.30 = (f32[3,256,256]{2,1,0:T(8,128)S(1)}, f32[3,256,256]{2,1,0:T(8,128)S(1)}, u32[]{:S(2)}, u32[]{:S(2)}) collective-permute-start(f32[3,256,256]{2,1,0:T(8,128)S(1)} %add.226), channel_id=1, source_target_pairs={{0,32},{16,48},{32,0},{48,16},{1,33},{17,49},{33,1},{49,17},{2,34}... | collective-permute-start | bytes 2359304 | tf_op jit(solution)/shard_map/ppermute | solution.py:394
  161.6 17.3 %collective-permute-done.30 = f32[3,256,256]{2,1,0:T(8,128)S(1)} collective-permute-done((f32[3,256,256]{2,1,0:T(8,128)S(1)}, f32[3,256,256]{2,1,0:T(8,128)S(1)}, u32[]{:S(2)}, u32[]{:S(2)}) %collective-permute-start.30) | collective-permute-done | bytes 786464 | tf_op jit(solution)/shard_map/ppermute | solution.py:394
  178.9 1.6 collective-permute-start.31
  180.6 30.6 %all-to-all-done = f32[16,512,256]{2,1,0:T(8,128)} async-done(((f32[16,512,256]{2,1,0:T(8,128)}), f32[16,512,256]{2,1,0:T(8,128)}, u32[]{:S(2)}, u32[]{:S(2)}) %all-to-all-start) | async-done | bytes 8388640 | tf_op jit(solution)/shard_map/all_to_all | solution.py:387
  211.2 15.7 %shard_map.39 = f32[768,256]{1,0:T(8,128)} custom-call(s32[16]{0:T(128)S(1)} %stack.67.places, f32[8192,256]{1,0:T(8,128)} %bitcast.20.e_ref, bf16[16,2,768,512]{3,2,1,0:T(8,128)(2,1)} %get-tuple-element.52.v_ref), custom_call_target="tpu_custom_call" | custom-call | flops 9663676416 | bytes 8388608 | tf_op jit(solution)/shard_map/pallas_call | solution.py:210
  226.9 6.4 %all-to-all-start.1 = ((f32[8,96,256]{2,1,0:T(8,128)}), f32[8,96,256]{2,1,0:T(8,128)S(1)}, u32[]{:S(2)}, u32[]{:S(2)}) async-start(f32[8,96,256]{2,1,0:T(8,128)} %bitcast.21), calls=%async_computation.1 | async-start | bytes 1572864 | tf_op jit(solution)/shard_map/all_to_all | solution.py:312
  233.3 12.1 %all-to-all-done.1 = f32[8,96,256]{2,1,0:T(8,128)S(1)} async-done(((f32[8,96,256]{2,1,0:T(8,128)}), f32[8,96,256]{2,1,0:T(8,128)S(1)}, u32[]{:S(2)}, u32[]{:S(2)}) %all-to-all-start.1) | async-done | bytes 786464 | tf_op jit(solution)/shard_map/all_to_all | solution.py:312
  246.4 3.6 %all-to-all-start.2 = ((f32[8,96,256]{2,1,0:T(8,128)}), f32[8,96,256]{2,1,0:T(8,128)S(1)}, u32[]{:S(2)}, u32[]{:S(2)}) async-start(f32[8,96,256]{2,1,0:T(8,128)} %broadcast_in_dim.19), calls=%async_computation.2 | async-start | bytes 1572864 | tf_op jit(solution)/shard_map/all_to_all | solution.py:319
  252.6 9.6 %all-to-all-done.2 = f32[8,96,256]{2,1,0:T(8,128)S(1)} async-done(((f32[8,96,256]{2,1,0:T(8,128)}), f32[8,96,256]{2,1,0:T(8,128)S(1)}, u32[]{:S(2)}, u32[]{:S(2)}) %all-to-all-start.2) | async-done | bytes 786464 | tf_op jit(solution)/shard_map/all_to_all | solution.py:319
  262.2 16.5 %shard_map.41 = f32[8192,256]{1,0:T(8,128)} custom-call(s32[16]{0:T(128)S(1)} %stack.67.places, f32[8192,256]{1,0:T(8,128)} %bitcast.20.e_ref, f32[768,768]{1,0:T(8,128)S(1)} %shard_map.40.m_ref, f32[768,256]{1,0:T(8,128)S(1)} %bitcast.34, bf16[16,2,768,512]{3,2,1,0:T(8,128)(2,1)} %get-tuple-element.52.v_ref), custom_call_target="tpu_custom_call" | custom-call | flops 9663676416 | bytes 16777216 | tf_op jit(solution)/shard_map/pallas_call | solution.py:229
  (94 shorter events, 25.6 us)
Async XLA Ops:
  1.8 31.4 %collective-permute-start.4 = (f32[512,512]{1,0:T(8,128)S(1)}, f32[512,512]{1,0:T(8,128)}, u32[]{:S(2)}, u32[]{:S(2)}) collective-permute-start(f32[512,512]{1,0:T(8,128)S(1)} %pad_maximum_fusion.refs_0_), channel_id=1, source_target_pairs={{0,6},{1,3},{2,0},{3,5},{4,2},{5,7},{6,4},{7,1},{8,14},{9,11},{10,... | collective-permute-start | bytes 3145736 | tf_op jit(solution)/shard_map/ppermute | solution.py:333
  2.3 30.9 %collective-permute-start.3 = (f32[512,512]{1,0:T(8,128)S(1)}, f32[512,512]{1,0:T(8,128)S(1)}, u32[]{:S(2)}, u32[]{:S(2)}) collective-permute-start(f32[512,512]{1,0:T(8,128)S(1)} %pad_maximum_fusion.refs_0_), channel_id=1, source_target_pairs={{0,8},{8,0},{1,9},{9,1},{2,10},{10,2},{3,11},{11,3},{4,12},{12,4},... | collective-permute-start | bytes 3145736 | tf_op jit(solution)/shard_map/ppermute | solution.py:337
  5.5 15.6 %collective-permute-start.1 = (f32[256,512]{1,0:T(8,128)S(1)}, f32[256,512]{1,0:T(8,128)S(1)}, u32[]{:S(2)}, u32[]{:S(2)}) collective-permute-start(f32[256,512]{1,0:T(8,128)S(1)} %get-tuple-element.34.refs_1_), channel_id=1, source_target_pairs={{0,2},{1,7},{2,4},{3,1},{4,6},{5,3},{6,0},{7,5},{8,10},{9,15},{10,... | collective-permute-start | bytes 1572872 | tf_op jit(solution)/shard_map/ppermute | solution.py:333
  7.0 26.1 %collective-permute-start.2 = (f32[256,512]{1,0:T(8,128)S(1)}, f32[256,512]{1,0:T(8,128)S(1)}, u32[]{:S(2)}, u32[]{:S(2)}) collective-permute-start(f32[256,512]{1,0:T(8,128)S(1)} %get-tuple-element.34.refs_1_), channel_id=1, source_target_pairs={{0,6},{1,3},{2,0},{3,5},{4,2},{5,7},{6,4},{7,1},{8,14},{9,11},{10,... | collective-permute-start | bytes 1572872 | tf_op jit(solution)/shard_map/ppermute | solution.py:333
  21.1 12.0 %collective-permute-start.6 = (f32[256,512]{1,0:T(8,128)S(1)}, f32[256,512]{1,0:T(8,128)S(1)}, u32[]{:S(2)}, u32[]{:S(2)}) collective-permute-start(f32[256,512]{1,0:T(8,128)S(1)} %collective-permute-done.1.refs_3_), channel_id=1, source_target_pairs={{0,2},{1,7},{2,4},{3,1},{4,6},{5,3},{6,0},{7,5},{8,10},{9,15},{10,... | collective-permute-start | bytes 1572872 | tf_op jit(solution)/shard_map/ppermute | solution.py:333
  21.9 27.7 %collective-permute-start = (f32[512,512]{1,0:T(8,128)S(1)}, f32[512,512]{1,0:T(8,128)S(1)}, u32[]{:S(2)}, u32[]{:S(2)}) collective-permute-start(f32[512,512]{1,0:T(8,128)S(1)} %pad_maximum_fusion.refs_0_), channel_id=1, source_target_pairs={{0,2},{1,7},{2,4},{3,1},{4,6},{5,3},{6,0},{7,5},{8,10},{9,15},{10,... | collective-permute-start | bytes 3145736 | tf_op jit(solution)/shard_map/ppermute | solution.py:333
  33.2 32.9 %collective-permute-start.7 = (f32[512,512]{1,0:T(8,128)S(1)}, f32[512,512]{1,0:T(8,128)S(1)}, u32[]{:S(2)}, u32[]{:S(2)}) collective-permute-start(f32[512,512]{1,0:T(8,128)S(1)} %collective-permute-done.3.refs_8_), channel_id=1, source_target_pairs={{0,2},{1,7},{2,4},{3,1},{4,6},{5,3},{6,0},{7,5},{8,10},{9,15},{10,... | collective-permute-start | bytes 3145736 | tf_op jit(solution)/shard_map/ppermute | solution.py:333
  35.0 49.1 %collective-permute-start.8 = (f32[512,512]{1,0:T(8,128)S(1)}, f32[512,512]{1,0:T(8,128)S(1)}, u32[]{:S(2)}, u32[]{:S(2)}) collective-permute-start(f32[512,512]{1,0:T(8,128)S(1)} %collective-permute-done.3.refs_8_), channel_id=1, source_target_pairs={{0,6},{1,3},{2,0},{3,5},{4,2},{5,7},{6,4},{7,1},{8,14},{9,11},{10,... | collective-permute-start | bytes 3145736 | tf_op jit(solution)/shard_map/ppermute | solution.py:333
  35.3 32.3 %collective-permute-start.12 = (f32[256,512]{1,0:T(8,128)S(1)}, f32[256,512]{1,0:T(8,128)S(1)}, u32[]{:S(2)}, u32[]{:S(2)}) collective-permute-start(f32[256,512]{1,0:T(8,128)S(1)} %collective-permute-done.6.refs_7_), channel_id=1, source_target_pairs={{0,8},{8,0},{1,9},{9,1},{2,10},{10,2},{3,11},{11,3},{4,12},{12,4},... | collective-permute-start | bytes 1572872 | tf_op jit(solution)/shard_map/ppermute | solution.py:337
  41.5 42.6 %collective-permute-start.11 = (f32[512,512]{1,0:T(8,128)S(1)}, f32[512,512]{1,0:T(8,128)}, u32[]{:S(2)}, u32[]{:S(2)}) collective-permute-start(f32[512,512]{1,0:T(8,128)S(1)} %pad_maximum_fusion.1), channel_id=1, source_target_pairs={{0,8},{8,0},{1,9},{9,1},{2,10},{10,2},{3,11},{11,3},{4,12},{12,4},... | collective-permute-start | bytes 3145736 | tf_op jit(solution)/shard_map/ppermute | solution.py:337
  49.7 34.5 %collective-permute-start.5 = (f32[512,512]{1,0:T(8,128)S(1)}, f32[512,512]{1,0:T(8,128)S(1)}, u32[]{:S(2)}, u32[]{:S(2)}) collective-permute-start(f32[512,512]{1,0:T(8,128)S(1)} %collective-permute-done.refs_2_), channel_id=1, source_target_pairs={{0,2},{1,7},{2,4},{3,1},{4,6},{5,3},{6,0},{7,5},{8,10},{9,15},{10,... | collective-permute-start | bytes 3145736 | tf_op jit(solution)/shard_map/ppermute | solution.py:333
  66.0 22.5 %collective-permute-start.9 = (f32[512,512]{1,0:T(8,128)S(1)}, f32[512,512]{1,0:T(8,128)S(1)}, u32[]{:S(2)}, u32[]{:S(2)}) collective-permute-start(f32[512,512]{1,0:T(8,128)S(1)} %collective-permute-done.7.refs_10_), channel_id=1, source_target_pairs={{0,2},{1,7},{2,4},{3,1},{4,6},{5,3},{6,0},{7,5},{8,10},{9,15},{10,... | collective-permute-start | bytes 3145736 | tf_op jit(solution)/shard_map/ppermute | solution.py:333
  67.5 16.6 %collective-permute-start.10 = (f32[256,512]{1,0:T(8,128)S(1)}, f32[256,512]{1,0:T(8,128)S(1)}, u32[]{:S(2)}, u32[]{:S(2)}) collective-permute-start(f32[256,512]{1,0:T(8,128)S(1)} %get-tuple-element.34.refs_1_), channel_id=1, source_target_pairs={{0,8},{8,0},{1,9},{9,1},{2,10},{10,2},{3,11},{11,3},{4,12},{12,4},... | collective-permute-start | bytes 1572872 | tf_op jit(solution)/shard_map/ppermute | solution.py:337
  89.5 121.7 %all-to-all-start = ((f32[16,512,256]{2,1,0:T(8,128)}), f32[16,512,256]{2,1,0:T(8,128)}, u32[]{:S(2)}, u32[]{:S(2)}) async-start(f32[16,512,256]{2,1,0:T(8,128)} %bitcast.35), calls=%async_computation | async-start | bytes 16777216 | tf_op jit(solution)/shard_map/all_to_all | solution.py:387
  97.6 4.8 %collective-permute-start.13 = (f32[512,512]{1,0:T(8,128)}, f32[512,512]{1,0:T(8,128)S(1)}, u32[]{:S(2)}, u32[]{:S(2)}) collective-permute-start(f32[512,512]{1,0:T(8,128)} %copy-done.1), channel_id=1, source_target_pairs={{0,1},{1,0},{2,3},{3,2},{4,5},{5,4},{6,7},{7,6},{8,9},{9,8},{10,11... | collective-permute-start | bytes 3145736 | tf_op jit(solution)/shard_map/ppermute | solution.py:337
  98.1 4.6 %collective-permute-start.16 = (f32[256,512]{1,0:T(8,128)S(1)}, f32[256,512]{1,0:T(8,128)S(1)}, u32[]{:S(2)}, u32[]{:S(2)}) collective-permute-start(f32[256,512]{1,0:T(8,128)S(1)} %collective-permute-done.1.refs_3_), channel_id=1, source_target_pairs={{0,1},{1,0},{2,3},{3,2},{4,5},{5,4},{6,7},{7,6},{8,9},{9,8},{10,11... | collective-permute-start | bytes 1572872 | tf_op jit(solution)/shard_map/ppermute | solution.py:337
  98.2 5.9 %collective-permute-start.18 = (f32[256,512]{1,0:T(8,128)S(1)}, f32[256,512]{1,0:T(8,128)S(1)}, u32[]{:S(2)}, u32[]{:S(2)}) collective-permute-start(f32[256,512]{1,0:T(8,128)S(1)} %collective-permute-done.2.refs_5_), channel_id=1, source_target_pairs={{0,1},{1,0},{2,3},{3,2},{4,5},{5,4},{6,7},{7,6},{8,9},{9,8},{10,11... | collective-permute-start | bytes 1572872 | tf_op jit(solution)/shard_map/ppermute | solution.py:337
  98.6 6.0 %collective-permute-start.20 = (f32[256,512]{1,0:T(8,128)S(1)}, f32[256,512]{1,0:T(8,128)S(1)}, u32[]{:S(2)}, u32[]{:S(2)}) collective-permute-start(f32[256,512]{1,0:T(8,128)S(1)} %collective-permute-done.6.refs_7_), channel_id=1, source_target_pairs={{0,1},{1,0},{2,3},{3,2},{4,5},{5,4},{6,7},{7,6},{8,9},{9,8},{10,11... | collective-permute-start | bytes 1572872 | tf_op jit(solution)/shard_map/ppermute | solution.py:337
  100.6 4.5 %collective-permute-start.22 = (f32[256,512]{1,0:T(8,128)S(1)}, f32[256,512]{1,0:T(8,128)S(1)}, u32[]{:S(2)}, u32[]{:S(2)}) collective-permute-start(f32[256,512]{1,0:T(8,128)S(1)} %collective-permute-done.10.refs_9_), channel_id=1, source_target_pairs={{0,1},{1,0},{2,3},{3,2},{4,5},{5,4},{6,7},{7,6},{8,9},{9,8},{10,11... | collective-permute-start | bytes 1572872 | tf_op jit(solution)/shard_map/ppermute | solution.py:337
  102.3 7.8 %collective-permute-start.15 = (f32[512,512]{1,0:T(8,128)}, f32[512,512]{1,0:T(8,128)S(1)}, u32[]{:S(2)}, u32[]{:S(2)}) collective-permute-start(f32[512,512]{1,0:T(8,128)} %copy-done.3), channel_id=1, source_target_pairs={{0,1},{1,0},{2,3},{3,2},{4,5},{5,4},{6,7},{7,6},{8,9},{9,8},{10,11... | collective-permute-start | bytes 3145736 | tf_op jit(solution)/shard_map/ppermute | solution.py:337
  102.7 7.8 %collective-permute-start.17 = (f32[512,512]{1,0:T(8,128)}, f32[512,512]{1,0:T(8,128)S(1)}, u32[]{:S(2)}, u32[]{:S(2)}) collective-permute-start(f32[512,512]{1,0:T(8,128)} %collective-permute-done.4.refs_4_), channel_id=1, source_target_pairs={{0,1},{1,0},{2,3},{3,2},{4,5},{5,4},{6,7},{7,6},{8,9},{9,8},{10,11... | collective-permute-start | bytes 3145736 | tf_op jit(solution)/shard_map/ppermute | solution.py:337
  104.6 5.0 %collective-permute-start.26 = (f32[256,512]{1,0:T(8,128)S(1)}, f32[256,512]{1,0:T(8,128)S(1)}, u32[]{:S(2)}, u32[]{:S(2)}) collective-permute-start(f32[256,512]{1,0:T(8,128)S(1)} %get-tuple-element.58.refs_13_), channel_id=1, source_target_pairs={{0,1},{1,0},{2,3},{3,2},{4,5},{5,4},{6,7},{7,6},{8,9},{9,8},{10,11... | collective-permute-start | bytes 1572872 | tf_op jit(solution)/shard_map/ppermute | solution.py:337
  105.1 4.9 %collective-permute-start.24 = (f32[256,512]{1,0:T(8,128)S(1)}, f32[256,512]{1,0:T(8,128)}, u32[]{:S(2)}, u32[]{:S(2)}) collective-permute-start(f32[256,512]{1,0:T(8,128)S(1)} %get-tuple-element.59.refs_11_), channel_id=1, source_target_pairs={{0,1},{1,0},{2,3},{3,2},{4,5},{5,4},{6,7},{7,6},{8,9},{9,8},{10,11... | collective-permute-start | bytes 1572872 | tf_op jit(solution)/shard_map/ppermute | solution.py:337
  107.4 4.0 %collective-permute-start.19 = (f32[512,512]{1,0:T(8,128)}, f32[512,512]{1,0:T(8,128)S(1)}, u32[]{:S(2)}, u32[]{:S(2)}) collective-permute-start(f32[512,512]{1,0:T(8,128)} %copy-done.6), channel_id=1, source_target_pairs={{0,1},{1,0},{2,3},{3,2},{4,5},{5,4},{6,7},{7,6},{8,9},{9,8},{10,11... | collective-permute-start | bytes 3145736 | tf_op jit(solution)/shard_map/ppermute | solution.py:337
  110.0 4.3 %collective-permute-start.23 = (f32[512,512]{1,0:T(8,128)}, f32[512,512]{1,0:T(8,128)S(1)}, u32[]{:S(2)}, u32[]{:S(2)}) collective-permute-start(f32[512,512]{1,0:T(8,128)} %copy-done.4), channel_id=1, source_target_pairs={{0,1},{1,0},{2,3},{3,2},{4,5},{5,4},{6,7},{7,6},{8,9},{9,8},{10,11... | collective-permute-start | bytes 3145736 | tf_op jit(solution)/shard_map/ppermute | solution.py:337
  110.1 5.7 %collective-permute-start.25 = (f32[512,512]{1,0:T(8,128)}, f32[512,512]{1,0:T(8,128)S(1)}, u32[]{:S(2)}, u32[]{:S(2)}) collective-permute-start(f32[512,512]{1,0:T(8,128)} %copy-done.5), channel_id=1, source_target_pairs={{0,1},{1,0},{2,3},{3,2},{4,5},{5,4},{6,7},{7,6},{8,9},{9,8},{10,11... | collective-permute-start | bytes 3145736 | tf_op jit(solution)/shard_map/ppermute | solution.py:337
  110.5 6.8 %collective-permute-start.27 = (f32[512,512]{1,0:T(8,128)}, f32[512,512]{1,0:T(8,128)S(1)}, u32[]{:S(2)}, u32[]{:S(2)}) collective-permute-start(f32[512,512]{1,0:T(8,128)} %copy-done.7), channel_id=1, source_target_pairs={{0,1},{1,0},{2,3},{3,2},{4,5},{5,4},{6,7},{7,6},{8,9},{9,8},{10,11... | collective-permute-start | bytes 3145736 | tf_op jit(solution)/shard_map/ppermute | solution.py:337
  135.9 20.3 %collective-permute-start.29 = (f32[3,256,256]{2,1,0:T(8,128)}, f32[3,256,256]{2,1,0:T(8,128)S(1)}, u32[]{:S(2)}, u32[]{:S(2)}) collective-permute-start(f32[3,256,256]{2,1,0:T(8,128)} %get-tuple-element.51), channel_id=1, source_target_pairs={{0,16},{16,0},{32,48},{48,32},{1,17},{17,1},{33,49},{49,33},{2,18}... | collective-permute-start | bytes 2359304 | tf_op jit(solution)/shard_map/ppermute | solution.py:394
  157.5 21.3 %collective-permute-start.30 = (f32[3,256,256]{2,1,0:T(8,128)S(1)}, f32[3,256,256]{2,1,0:T(8,128)S(1)}, u32[]{:S(2)}, u32[]{:S(2)}) collective-permute-start(f32[3,256,256]{2,1,0:T(8,128)S(1)} %add.226), channel_id=1, source_target_pairs={{0,32},{16,48},{32,0},{48,16},{1,33},{17,49},{33,1},{49,17},{2,34}... | collective-permute-start | bytes 2359304 | tf_op jit(solution)/shard_map/ppermute | solution.py:394
  178.9 54.3 %collective-permute-start.31 = (f32[3,256,256]{2,1,0:T(8,128)S(1)}, f32[3,256,256]{2,1,0:T(8,128)S(1)}, u32[]{:S(2)}, u32[]{:S(2)}) collective-permute-start(f32[3,256,256]{2,1,0:T(8,128)S(1)} %add.227), channel_id=1, source_target_pairs={{0,64},{64,0},{1,65},{65,1},{2,66},{66,2},{3,67},{67,3},{4,68},{68... | collective-permute-start | bytes 2359304 | tf_op jit(solution)/shard_map/ppermute | solution.py:337
  226.9 18.5 %all-to-all-start.1 = ((f32[8,96,256]{2,1,0:T(8,128)}), f32[8,96,256]{2,1,0:T(8,128)S(1)}, u32[]{:S(2)}, u32[]{:S(2)}) async-start(f32[8,96,256]{2,1,0:T(8,128)} %bitcast.21), calls=%async_computation.1 | async-start | bytes 1572864 | tf_op jit(solution)/shard_map/all_to_all | solution.py:312
  246.4 15.8 %all-to-all-start.2 = ((f32[8,96,256]{2,1,0:T(8,128)}), f32[8,96,256]{2,1,0:T(8,128)S(1)}, u32[]{:S(2)}, u32[]{:S(2)}) async-start(f32[8,96,256]{2,1,0:T(8,128)} %broadcast_in_dim.19), calls=%async_computation.2 | async-start | bytes 1572864 | tf_op jit(solution)/shard_map/all_to_all | solution.py:319
  (23 other events, 264.2 us)
